TPU v7x, 32 devices: a whole 2x2x4 slice. The times are simulated.
32 devices in a mesh: tm: 8 (over z, x), head: 4 (over y, core).
Axes of the slice: x: 2, y: 2, z: 4, core: 2. Of those that a mesh axis runs over, the one named last changes fastest.
Arguments:
- query: bfloat16 [4096, 2560], P(('tm', 'head')), may hold values from -5 to 5, as said below
- keys: bfloat16 [4096, 2560], P(('tm', 'head')), may hold values from -5 to 5, as said below
- values: bfloat16 [4096, 2560], P(('tm', 'head')), may hold values from -6 to 6
- grad_out: bfloat16 [4096, 2560], P(('tm', 'head')), may hold values from -6 to 6
- tile_pattern: int32 [3, 4, 3], replicated, may hold values from 0 to 3, as said below
- window: int32 [8], replicated, may hold values from 1 to 3
Outputs:
- attended: bfloat16 [4096, 2560], P(('tm', 'head'))
- grad_query: bfloat16 [4096, 2560], P(('tm', 'head'))
- grad_keys: bfloat16 [4096, 2560], P(('tm', 'head'))
- grad_values: bfloat16 [4096, 2560], P(('tm', 'head'))
Inputs may be any that keep to these rules, and one draw needn't show every extreme that they name: `query`: queries of the attention. `keys`: keys of the attention. `tile_pattern`: entry [l, q, 0] is q; the 3 entries of each row are distinct.
All inputs are finite; a program needn't handle non-finite values.
Results may differ from a plain program's by a relative error of at most 0.0091.
Values may be sent and summed in bfloat16 or wider, within the bound.
No kernel may reach another device: no remote copies, remote signals or barrier semaphores. Data moves between devices by JAX's collectives and lax.ppermute only.
A program may use at most 128 MiB of HBM per device.

v0:
```python
from functools import partial
import math

import jax
import jax.numpy as jnp
from jax import lax
from jax.sharding import PartitionSpec as P

HD = 128
QT = 4
SEL = 3
W = 3


NEG = -1e30


def shifted(block, axis, distance):
    devices = range(lax.axis_size(axis))
    route = [(i - distance, i) for i in devices if i - distance in devices]
    return lax.ppermute(block, axis, route)


def to_heads(array, heads_local, tile_len):
    return jnp.transpose(array.reshape(QT, tile_len, heads_local, HD), (2, 0, 1, 3))


def tile_pass(q_all, g_all, keys_all, vals_all, live_cols, carry, inputs):
    acc_k, acc_v = carry
    index, chosen = inputs
    heads_local = q_all.shape[0]
    tile_len = q_all.shape[2]
    count = W * SEL * tile_len
    q_head = lax.dynamic_index_in_dim(q_all, index, 1, False)
    g_head = lax.dynamic_index_in_dim(g_all, index, 1, False)
    k_sel = jnp.concatenate([jnp.take(keys_all[lag], chosen[lag], axis=1) for lag in range(W)], 1)
    v_sel = jnp.concatenate([jnp.take(vals_all[lag], chosen[lag], axis=1) for lag in range(W)], 1)
    k_sel = k_sel.reshape(heads_local, count, HD)
    v_sel = v_sel.reshape(heads_local, count, HD)
    scale = 1.0 / math.sqrt(HD)
    scores = jnp.einsum("had,hbd->hab", q_head, k_sel, preferred_element_type=jnp.float32) * scale
    scores = jnp.where(live_cols, scores, NEG)
    top = jnp.max(scores, -1, keepdims=True)
    expo = jnp.exp(scores - top)
    prob = expo / jnp.sum(expo, -1, keepdims=True)
    prob_b = prob.astype(jnp.bfloat16)
    output = jnp.einsum("hab,hbd->had", prob_b, v_sel, preferred_element_type=jnp.float32)
    delta = jnp.sum(g_head.astype(jnp.float32) * output, -1, keepdims=True)
    dprob = jnp.einsum("had,hbd->hab", g_head, v_sel, preferred_element_type=jnp.float32)
    dscore = (prob * (dprob - delta) * scale).astype(jnp.bfloat16)
    dquery = jnp.einsum("hab,hbd->had", dscore, k_sel, preferred_element_type=jnp.float32)
    dkeys = jnp.einsum("hab,had->hbd", dscore, q_head, preferred_element_type=jnp.float32)
    dvals = jnp.einsum("hab,had->hbd", prob_b, g_head, preferred_element_type=jnp.float32)
    dkeys = dkeys.reshape(heads_local, W, SEL, tile_len, HD)
    dvals = dvals.reshape(heads_local, W, SEL, tile_len, HD)
    onehot = (chosen[:, :, None] == jnp.arange(QT, dtype=jnp.int32)[None, None, :]).astype(
        jnp.float32
    )
    highest = lax.Precision.HIGHEST
    acc_k = acc_k + jnp.einsum("hwstd,wsk->whktd", dkeys, onehot, precision=highest)
    acc_v = acc_v + jnp.einsum("hwstd,wsk->whktd", dvals, onehot, precision=highest)
    return ((acc_k, acc_v), (output.astype(jnp.bfloat16), dquery.astype(jnp.bfloat16)))


def shards(query, keys, values, grad_out, tile_pattern, window):
    q_loc, k_loc, v_loc, g_loc = (
        lax.all_to_all(query, "head", split_axis=1, concat_axis=0, tiled=True),
        lax.all_to_all(keys, "head", split_axis=1, concat_axis=0, tiled=True),
        lax.all_to_all(values, "head", split_axis=1, concat_axis=0, tiled=True),
        lax.all_to_all(grad_out, "head", split_axis=1, concat_axis=0, tiled=True),
    )
    frame_len = q_loc.shape[0]
    width = q_loc.shape[1]
    heads_local = width // HD
    tile_len = frame_len // QT
    frame = lax.axis_index("tm")
    q_all = to_heads(q_loc, heads_local, tile_len)
    g_all = to_heads(g_loc, heads_local, tile_len)
    paired = jnp.stack(
        (to_heads(k_loc, heads_local, tile_len), to_heads(v_loc, heads_local, tile_len))
    )
    earlier = [paired]
    for lag in range(1, W):
        earlier.append(shifted(paired, "tm", lag))
    keys_all = [piece[0] for piece in earlier]
    vals_all = [piece[1] for piece in earlier]
    lags = jnp.arange(W, dtype=jnp.int32)
    limit = lax.dynamic_index_in_dim(window, frame, 0, False)
    live = (lags <= frame) & (lags < limit)
    live_cols = jnp.repeat(live, SEL * tile_len)
    sel_tiles = jnp.transpose(tile_pattern, (1, 0, 2))
    zeros = jnp.zeros((W, heads_local, QT, tile_len, HD), jnp.float32)
    stepper = partial(tile_pass, q_all, g_all, keys_all, vals_all, live_cols)
    tile_ids = jnp.arange(QT, dtype=jnp.int32)
    (acc_k, acc_v), (out_tiles, dq_tiles) = lax.scan(stepper, (zeros, zeros), (tile_ids, sel_tiles))
    grad_pairs = jnp.stack((acc_k, acc_v), 1)
    pending = grad_pairs[W - 1].astype(jnp.bfloat16)
    total = grad_pairs[0]
    for lag in range(W - 1, 0, -1):
        moved = shifted(pending, "tm", -1)
        if lag > 1:
            pending = (grad_pairs[lag - 1] + moved.astype(jnp.float32)).astype(jnp.bfloat16)
        else:
            total = total + moved.astype(jnp.float32)
    out_loc = jnp.transpose(out_tiles, (0, 2, 1, 3)).reshape(frame_len, width)
    dq_loc = jnp.transpose(dq_tiles, (0, 2, 1, 3)).reshape(frame_len, width)
    dk_loc = jnp.transpose(total[0], (1, 2, 0, 3)).reshape(frame_len, width).astype(jnp.bfloat16)
    dv_loc = jnp.transpose(total[1], (1, 2, 0, 3)).reshape(frame_len, width).astype(jnp.bfloat16)
    attended, grad_query, grad_keys, grad_values = (
        lax.all_to_all(out_loc, "head", split_axis=0, concat_axis=1, tiled=True),
        lax.all_to_all(dq_loc, "head", split_axis=0, concat_axis=1, tiled=True),
        lax.all_to_all(dk_loc, "head", split_axis=0, concat_axis=1, tiled=True),
        lax.all_to_all(dv_loc, "head", split_axis=0, concat_axis=1, tiled=True),
    )
    return (attended, grad_query, grad_keys, grad_values)


def solution(mesh):
    placed = (
        P(("tm", "head"), None),
        P(("tm", "head"), None),
        P(("tm", "head"), None),
        P(("tm", "head"), None),
        P(),
        P(),
    )
    return jax.shard_map(
        shards,
        mesh=mesh,
        in_specs=placed,
        out_specs=(
            P(("tm", "head"), None),
            P(("tm", "head"), None),
            P(("tm", "head"), None),
            P(("tm", "head"), None),
        ),
        check_vma=False,
    )
```

profile of v0, /device:TPU:0, one launch (start us, length us, event | category | flops | bytes accessed | tf_op | source)
XLA Modules:
  0.0 418.4 jit_solution(18156017292960311971)
XLA Ops:
  2.9 4.2 %all-to-all-start.1 = ((bf16[128,4,640]{0,2,1:T(8,128)(2,1)}), bf16[128,4,640]{0,2,1:T(8,128)(2,1)S(1)}, u32[]{:S(2)}, u32[]{:S(2)}) async-start(bf16[128,4,640]{0,2,1:T(8,128)(2,1)} %bitcast.5), calls=%async_computation.1 | async-start | bytes 1310720 | tf_op jit(solution)/shard_map/all_to_all | solution.py:68
  7.4 9.9 %all-to-all-done.1 = bf16[128,4,640]{0,2,1:T(8,128)(2,1)S(1)} async-done(((bf16[128,4,640]{0,2,1:T(8,128)(2,1)}), bf16[128,4,640]{0,2,1:T(8,128)(2,1)S(1)}, u32[]{:S(2)}, u32[]{:S(2)}) %all-to-all-start.1) | async-done | bytes 655392 | tf_op jit(solution)/shard_map/all_to_all | solution.py:68
  17.4 12.6 %all_to_all.134 = bf16[128,4,640]{0,2,1:T(8,128)(2,1)S(1)} all-to-all(bf16[128,4,640]{0,2,1:T(8,128)(2,1)S(1)} %bitcast.231), channel_id=1, replica_groups=mesh['tm'=8,'head'=4] {'head'}, dimensions={1} | all-to-all | bytes 1310720 | tf_op jit(solution)/shard_map/all_to_all | solution.py:69
  31.3 5.3 %collective-permute-start.1 = (bf16[2,5,4,128,128]{3,4,1,2,0:T(8,128)(2,1)}, bf16[2,5,4,128,128]{3,4,1,2,0:T(8,128)(2,1)}, u32[]{:S(2)}, u32[]{:S(2)}) collective-permute-start(bf16[2,5,4,128,128]{3,4,1,2,0:T(8,128)(2,1)} %pad_maximum_fusion.3), channel_id=1, source_target_pairs={{0,8},{4,12},{8,16},{12,20},{16,24},{20,28},{1,9},{5,13},{9,17},{1... | collective-permute-start | bytes 3932168 | tf_op jit(solution)/shard_map/ppermute | solution.py:21
  36.6 4.5 %collective-permute-start = (bf16[2,5,4,128,128]{3,4,1,2,0:T(8,128)(2,1)}, bf16[2,5,4,128,128]{3,4,1,2,0:T(8,128)(2,1)}, u32[]{:S(2)}, u32[]{:S(2)}) collective-permute-start(bf16[2,5,4,128,128]{3,4,1,2,0:T(8,128)(2,1)} %pad_maximum_fusion.3), channel_id=1, source_target_pairs={{0,4},{4,8},{8,12},{12,16},{16,20},{20,24},{24,28},{1,5},{5,9},{9,... | collective-permute-start | bytes 3932168 | tf_op jit(solution)/shard_map/ppermute | solution.py:21
  42.1 4.2 all-to-all-start
  49.4 7.2 %all-to-all-done = bf16[128,4,640]{0,2,1:T(8,128)(2,1)} async-done(((bf16[128,4,640]{0,2,1:T(8,128)(2,1)}), bf16[128,4,640]{0,2,1:T(8,128)(2,1)}, u32[]{:S(2)}, u32[]{:S(2)}) %all-to-all-start) | async-done | bytes 655392 | tf_op jit(solution)/shard_map/all_to_all | solution.py:67
  74.5 210.7 %while.17 = (s32[]{:T(128)}, f32[3,5,4,128,128]{4,2,3,1,0:T(4,128)}, f32[3,5,4,128,128]{4,2,3,1,0:T(4,128)}, bf16[4,5,128,128]{2,3,1,0:T(8,128)(2,1)}, bf16[4,5,...) while((s32[]{:T(128)}, ...), condition=%wide.region_4.6_spmd.clone, body=%wide.region_0.5_spmd.clone.sunk | while | flops 1220120320 | bytes 180746352 | solution.py:95
  103.9 8.8 %bitcast_add_fusion.5 = f32[3,5,4,128,128]{4,2,3,1,0:T(4,128)S(1)} fusion(f32[3,5,4,128,128]{4,2,3,1,0:T(4,128)S(1)} %copy-done, f32[5,3,3,128,128]{4,3,2,1,0:T(8,128)S(1)} %bitcast.210, pred[]{:T(512)S(6)} %compare.3, s32[3,3]{1,0:T(4,128)S(1)} %fusion.111), kind=kOutput, calls=%fused_computation.9.clone.1 | convolution fusion | flops 37355556 | bytes 10813477 | tf_op jit(solution)/shard_map/while/body/eval_jaxpr/hwstd,wsk->whktd/dot_general | solution.py:61
  116.4 8.9 %bitcast_add_fusion.4 = f32[3,5,4,128,128]{4,2,3,1,0:T(4,128)S(1)} fusion(f32[3,5,4,128,128]{4,2,3,1,0:T(4,128)S(1)} %copy-done.2, f32[5,3,3,128,128]{4,3,2,1,0:T(8,128)S(1)} %bitcast.209, pred[]{:T(512)S(6)} %compare.3, s32[3,3]{1,0:T(4,128)S(1)} %fusion.111), kind=kOutput, calls=%fused_computation.10.clone.1 | convolution fusion | flops 37355556 | bytes 10813477 | tf_op jit(solution)/shard_map/while/body/eval_jaxpr/hwstd,wsk->whktd/dot_general | solution.py:60
  156.6 8.8 %bitcast_add_fusion.5 = f32[3,5,4,128,128]{4,2,3,1,0:T(4,128)S(1)} fusion(f32[3,5,4,128,128]{4,2,3,1,0:T(4,128)S(1)} %copy-done, f32[5,3,3,128,128]{4,3,2,1,0:T(8,128)S(1)} %bitcast.210, pred[]{:T(512)S(6)} %compare.3, s32[3,3]{1,0:T(4,128)S(1)} %fusion.111), kind=kOutput, calls=%fused_computation.9.clone.1 | convolution fusion | flops 37355556 | bytes 10813477 | tf_op jit(solution)/shard_map/while/body/eval_jaxpr/hwstd,wsk->whktd/dot_general | solution.py:61
  169.1 8.8 %bitcast_add_fusion.4 = f32[3,5,4,128,128]{4,2,3,1,0:T(4,128)S(1)} fusion(f32[3,5,4,128,128]{4,2,3,1,0:T(4,128)S(1)} %copy-done.2, f32[5,3,3,128,128]{4,3,2,1,0:T(8,128)S(1)} %bitcast.209, pred[]{:T(512)S(6)} %compare.3, s32[3,3]{1,0:T(4,128)S(1)} %fusion.111), kind=kOutput, calls=%fused_computation.10.clone.1 | convolution fusion | flops 37355556 | bytes 10813477 | tf_op jit(solution)/shard_map/while/body/eval_jaxpr/hwstd,wsk->whktd/dot_general | solution.py:60
  192.7 3.9 fusion.107
  209.3 8.8 %bitcast_add_fusion.5 = f32[3,5,4,128,128]{4,2,3,1,0:T(4,128)S(1)} fusion(f32[3,5,4,128,128]{4,2,3,1,0:T(4,128)S(1)} %copy-done, f32[5,3,3,128,128]{4,3,2,1,0:T(8,128)S(1)} %bitcast.210, pred[]{:T(512)S(6)} %compare.3, s32[3,3]{1,0:T(4,128)S(1)} %fusion.111), kind=kOutput, calls=%fused_computation.9.clone.1 | convolution fusion | flops 37355556 | bytes 10813477 | tf_op jit(solution)/shard_map/while/body/eval_jaxpr/hwstd,wsk->whktd/dot_general | solution.py:61
  221.8 8.8 %bitcast_add_fusion.4 = f32[3,5,4,128,128]{4,2,3,1,0:T(4,128)S(1)} fusion(f32[3,5,4,128,128]{4,2,3,1,0:T(4,128)S(1)} %copy-done.2, f32[5,3,3,128,128]{4,3,2,1,0:T(8,128)S(1)} %bitcast.209, pred[]{:T(512)S(6)} %compare.3, s32[3,3]{1,0:T(4,128)S(1)} %fusion.111), kind=kOutput, calls=%fused_computation.10.clone.1 | convolution fusion | flops 37355556 | bytes 10813477 | tf_op jit(solution)/shard_map/while/body/eval_jaxpr/hwstd,wsk->whktd/dot_general | solution.py:60
  262.0 8.8 %bitcast_add_fusion.5 = f32[3,5,4,128,128]{4,2,3,1,0:T(4,128)S(1)} fusion(f32[3,5,4,128,128]{4,2,3,1,0:T(4,128)S(1)} %copy-done, f32[5,3,3,128,128]{4,3,2,1,0:T(8,128)S(1)} %bitcast.210, pred[]{:T(512)S(6)} %compare.3, s32[3,3]{1,0:T(4,128)S(1)} %fusion.111), kind=kOutput, calls=%fused_computation.9.clone.1 | convolution fusion | flops 37355556 | bytes 10813477 | tf_op jit(solution)/shard_map/while/body/eval_jaxpr/hwstd,wsk->whktd/dot_general | solution.py:61
  274.4 8.8 %bitcast_add_fusion.4 = f32[3,5,4,128,128]{4,2,3,1,0:T(4,128)S(1)} fusion(f32[3,5,4,128,128]{4,2,3,1,0:T(4,128)S(1)} %copy-done.2, f32[5,3,3,128,128]{4,3,2,1,0:T(8,128)S(1)} %bitcast.209, pred[]{:T(512)S(6)} %compare.3, s32[3,3]{1,0:T(4,128)S(1)} %fusion.111), kind=kOutput, calls=%fused_computation.10.clone.1 | convolution fusion | flops 37355556 | bytes 10813477 | tf_op jit(solution)/shard_map/while/body/eval_jaxpr/hwstd,wsk->whktd/dot_general | solution.py:60
  285.2 6.3 %copy.106 = f32[3,5,4,128,128]{3,4,1,2,0:T(8,128)} copy(f32[3,5,4,128,128]{4,2,3,1,0:T(4,128)} %get-tuple-element.92) | data formatting | bytes 7864320 | tf_op jit(solution)/shard_map/while | solution.py:95
  291.5 6.3 %copy.107 = f32[3,5,4,128,128]{3,4,1,2,0:T(8,128)} copy(f32[3,5,4,128,128]{4,2,3,1,0:T(4,128)} %get-tuple-element.93) | data formatting | bytes 7864320 | tf_op jit(solution)/shard_map/while | solution.py:95
  301.4 52.2 %collective-permute-done.2 = bf16[2,5,4,128,128]{3,4,1,2,0:T(8,128)(2,1)S(1)} collective-permute-done((bf16[2,5,4,128,128]{3,4,1,2,0:T(8,128)(2,1)S(1)}, bf16[2,5,4,128,128]{3,4,1,2,0:T(8,128)(2,1)S(1)}, u32[]{:S(2)}, u32[]{:S(2)}) %collective-permute-start.2) | collective-permute-done | bytes 1310752 | tf_op jit(solution)/shard_map/ppermute | solution.py:21
  361.0 9.1 %all-to-all-done.5 = bf16[4,128,640]{1,2,0:T(8,128)(2,1)S(1)} async-done(((bf16[4,128,640]{1,2,0:T(8,128)(2,1)}), bf16[4,128,640]{1,2,0:T(8,128)(2,1)S(1)}, u32[]{:S(2)}, u32[]{:S(2)}) %all-to-all-start.5) | async-done | bytes 655392 | tf_op jit(solution)/shard_map/all_to_all | solution.py:111
  373.6 13.8 %collective-permute-done.3 = bf16[2,5,4,128,128]{3,4,1,2,0:T(8,128)(2,1)S(1)} collective-permute-done((bf16[2,5,4,128,128]{3,4,1,2,0:T(8,128)(2,1)}, bf16[2,5,4,128,128]{3,4,1,2,0:T(8,128)(2,1)S(1)}, u32[]{:S(2)}, u32[]{:S(2)}) %collective-permute-start.3) | collective-permute-done | bytes 1310752 | tf_op jit(solution)/shard_map/ppermute | solution.py:21
  390.5 13.1 %all_to_all.135 = bf16[4,128,640]{1,2,0:T(8,128)(2,1)S(1)} all-to-all(bf16[4,128,640]{1,2,0:T(8,128)(2,1)S(1)} %bitcast.226), channel_id=1, replica_groups=mesh['tm'=8,'head'=4] {'head'}, dimensions={0} | all-to-all | bytes 1310720 | tf_op jit(solution)/shard_map/all_to_all | solution.py:112
  410.7 6.6 %all-to-all-done.7 = bf16[4,128,640]{1,2,0:T(8,128)(2,1)S(1)} async-done(((bf16[4,128,640]{1,2,0:T(8,128)(2,1)}), bf16[4,128,640]{1,2,0:T(8,128)(2,1)S(1)}, u32[]{:S(2)}, u32[]{:S(2)}) %all-to-all-start.7) | async-done | bytes 655392 | tf_op jit(solution)/shard_map/all_to_all | solution.py:113
  (304 shorter events, 179.0 us)
Async XLA Ops:
  2.9 14.5 %all-to-all-start.1 = ((bf16[128,4,640]{0,2,1:T(8,128)(2,1)}), bf16[128,4,640]{0,2,1:T(8,128)(2,1)S(1)}, u32[]{:S(2)}, u32[]{:S(2)}) async-start(bf16[128,4,640]{0,2,1:T(8,128)(2,1)} %bitcast.5), calls=%async_computation.1 | async-start | bytes 1310720 | tf_op jit(solution)/shard_map/all_to_all | solution.py:68
  7.4 33.6 %copy-start.17 = (bf16[128,2560]{1,0:T(8,128)(2,1)S(1)}, bf16[128,2560]{1,0:T(8,128)(2,1)}, u32[]{:S(2)}) copy-start(bf16[128,2560]{1,0:T(8,128)(2,1)} %param.10) | copy-start | bytes 1966084
  30.0 16.4 %copy-start.20 = (s32[3,4,3]{2,1,0:T(4,128)S(1)}, s32[3,4,3]{2,1,0:T(4,128)}, u32[]{:S(2)}) copy-start(s32[3,4,3]{2,1,0:T(4,128)} %param.14) | copy-start | bytes 436
  30.0 16.4 %copy-start.18 = (bf16[128,2560]{1,0:T(8,128)(2,1)S(1)}, bf16[128,2560]{1,0:T(8,128)(2,1)}, u32[]{:S(2)}) copy-start(bf16[128,2560]{1,0:T(8,128)(2,1)} %param.13) | copy-start | bytes 1966084
  31.3 16.2 %copy-start.21 = (s32[8]{0:T(128)S(1)}, s32[8]{0:T(128)}, u32[]{:S(2)}) copy-start(s32[8]{0:T(128)} %param.15) | copy-start | bytes 100
  31.3 32.2 %collective-permute-start.1 = (bf16[2,5,4,128,128]{3,4,1,2,0:T(8,128)(2,1)}, bf16[2,5,4,128,128]{3,4,1,2,0:T(8,128)(2,1)}, u32[]{:S(2)}, u32[]{:S(2)}) collective-permute-start(bf16[2,5,4,128,128]{3,4,1,2,0:T(8,128)(2,1)} %pad_maximum_fusion.3), channel_id=1, source_target_pairs={{0,8},{4,12},{8,16},{12,20},{16,24},{20,28},{1,9},{5,13},{9,17},{1... | collective-permute-start | bytes 3932168 | tf_op jit(solution)/shard_map/ppermute | solution.py:21
  36.6 32.4 %collective-permute-start = (bf16[2,5,4,128,128]{3,4,1,2,0:T(8,128)(2,1)}, bf16[2,5,4,128,128]{3,4,1,2,0:T(8,128)(2,1)}, u32[]{:S(2)}, u32[]{:S(2)}) collective-permute-start(bf16[2,5,4,128,128]{3,4,1,2,0:T(8,128)(2,1)} %pad_maximum_fusion.3), channel_id=1, source_target_pairs={{0,4},{4,8},{8,12},{12,16},{16,20},{20,24},{24,28},{1,5},{5,9},{9,... | collective-permute-start | bytes 3932168 | tf_op jit(solution)/shard_map/ppermute | solution.py:21
  42.1 14.5 %all-to-all-start = ((bf16[128,4,640]{0,2,1:T(8,128)(2,1)}), bf16[128,4,640]{0,2,1:T(8,128)(2,1)}, u32[]{:S(2)}, u32[]{:S(2)}) async-start(bf16[128,4,640]{0,2,1:T(8,128)(2,1)} %bitcast.1), calls=%async_computation | async-start | bytes 1310720 | tf_op jit(solution)/shard_map/all_to_all | solution.py:67
  56.6 17.8 %all-to-all-start.3 = ((bf16[128,4,640]{0,2,1:T(8,128)(2,1)}), bf16[128,4,640]{0,2,1:T(8,128)(2,1)S(1)}, u32[]{:S(2)}, u32[]{:S(2)}) async-start(bf16[128,4,640]{0,2,1:T(8,128)(2,1)} %bitcast.227), calls=%async_computation.3 | async-start | bytes 1310720 | tf_op jit(solution)/shard_map/all_to_all | solution.py:70
  112.8 12.5 %copy-start.1 = (f32[3,5,4,128,128]{4,2,3,1,0:T(4,128)}, f32[3,5,4,128,128]{4,2,3,1,0:T(4,128)S(1)}, u32[]{:S(2)}) copy-start(f32[3,5,4,128,128]{4,2,3,1,0:T(4,128)S(1)} %bitcast_add_fusion.5) | copy-start | bytes 11796484 | tf_op jit(solution)/shard_map/while
  116.4 10.7 %copy-start.11 = (bf16[5,4,128,128]{3,2,1,0:T(8,128)(2,1)S(1)}, bf16[5,4,128,128]{3,2,1,0:T(8,128)(2,1)}, u32[]{:S(2)}) copy-start(bf16[5,4,128,128]{3,2,1,0:T(8,128)(2,1)} %copy-done.10) | copy-start | bytes 1966084 | tf_op jit(solution)/shard_map/while
  116.4 10.7 %copy-start.13 = (bf16[5,4,128,128]{3,2,1,0:T(8,128)(2,1)S(1)}, bf16[5,4,128,128]{3,2,1,0:T(8,128)(2,1)}, u32[]{:S(2)}) copy-start(bf16[5,4,128,128]{3,2,1,0:T(8,128)(2,1)} %copy-done.12) | copy-start | bytes 1966084 | tf_op jit(solution)/shard_map/while
  116.4 10.7 %copy-start.15 = (bf16[5,4,128,128]{2,3,0,1:T(8,128)(2,1)S(1)}, bf16[5,4,128,128]{2,3,0,1:T(8,128)(2,1)}, u32[]{:S(2)}) copy-start(bf16[5,4,128,128]{2,3,0,1:T(8,128)(2,1)} %copy-done.14) | copy-start | bytes 1966084 | tf_op jit(solution)/shard_map/while
  165.5 12.5 %copy-start.1 = (f32[3,5,4,128,128]{4,2,3,1,0:T(4,128)}, f32[3,5,4,128,128]{4,2,3,1,0:T(4,128)S(1)}, u32[]{:S(2)}) copy-start(f32[3,5,4,128,128]{4,2,3,1,0:T(4,128)S(1)} %bitcast_add_fusion.5) | copy-start | bytes 11796484 | tf_op jit(solution)/shard_map/while
  218.1 12.5 %copy-start.1 = (f32[3,5,4,128,128]{4,2,3,1,0:T(4,128)}, f32[3,5,4,128,128]{4,2,3,1,0:T(4,128)S(1)}, u32[]{:S(2)}) copy-start(f32[3,5,4,128,128]{4,2,3,1,0:T(4,128)S(1)} %bitcast_add_fusion.5) | copy-start | bytes 11796484 | tf_op jit(solution)/shard_map/while
  270.8 12.5 %copy-start.1 = (f32[3,5,4,128,128]{4,2,3,1,0:T(4,128)}, f32[3,5,4,128,128]{4,2,3,1,0:T(4,128)S(1)}, u32[]{:S(2)}) copy-start(f32[3,5,4,128,128]{4,2,3,1,0:T(4,128)S(1)} %bitcast_add_fusion.5) | copy-start | bytes 11796484 | tf_op jit(solution)/shard_map/while
  297.7 55.9 %copy-start.8 = (f32[3,5,4,128,128]{3,4,1,2,0:T(8,128)S(1)}, f32[3,5,4,128,128]{3,4,1,2,0:T(8,128)}, u32[]{:S(2)}) copy-start(f32[3,5,4,128,128]{3,4,1,2,0:T(8,128)} %copy.106) | copy-start | bytes 11796484
  297.7 55.9 %copy-start.9 = (f32[3,5,4,128,128]{3,4,1,2,0:T(8,128)S(1)}, f32[3,5,4,128,128]{3,4,1,2,0:T(8,128)}, u32[]{:S(2)}) copy-start(f32[3,5,4,128,128]{3,4,1,2,0:T(8,128)} %copy.107) | copy-start | bytes 11796484
  299.8 60.1 %copy-start.19 = (bf16[4,5,128,128]{2,3,1,0:T(8,128)(2,1)S(1)}, bf16[4,5,128,128]{2,3,1,0:T(8,128)(2,1)}, u32[]{:S(2)}) copy-start(bf16[4,5,128,128]{2,3,1,0:T(8,128)(2,1)} %get-tuple-element.90) | copy-start | bytes 1966084
  299.8 53.8 %collective-permute-start.2 = (bf16[2,5,4,128,128]{3,4,1,2,0:T(8,128)(2,1)S(1)}, bf16[2,5,4,128,128]{3,4,1,2,0:T(8,128)(2,1)S(1)}, u32[]{:S(2)}, u32[]{:S(2)}) collective-permute-start(bf16[2,5,4,128,128]{3,4,1,2,0:T(8,128)(2,1)S(1)} %fusion.54), channel_id=1, source_target_pairs={{4,0},{8,4},{12,8},{16,12},{20,16},{24,20},{28,24},{5,1},{9,5},{13... | collective-permute-start | bytes 3932168 | tf_op jit(solution)/shard_map/ppermute | solution.py:21
  355.1 32.3 %collective-permute-start.3 = (bf16[2,5,4,128,128]{3,4,1,2,0:T(8,128)(2,1)}, bf16[2,5,4,128,128]{3,4,1,2,0:T(8,128)(2,1)S(1)}, u32[]{:S(2)}, u32[]{:S(2)}) collective-permute-start(bf16[2,5,4,128,128]{3,4,1,2,0:T(8,128)(2,1)} %fusion.48), channel_id=1, source_target_pairs={{4,0},{8,4},{12,8},{16,12},{20,16},{24,20},{28,24},{5,1},{9,5},{13... | collective-permute-start | bytes 3932168 | tf_op jit(solution)/shard_map/ppermute | solution.py:21
  356.4 13.7 %all-to-all-start.5 = ((bf16[4,128,640]{1,2,0:T(8,128)(2,1)}), bf16[4,128,640]{1,2,0:T(8,128)(2,1)S(1)}, u32[]{:S(2)}, u32[]{:S(2)}) async-start(bf16[4,128,640]{1,2,0:T(8,128)(2,1)} %bitcast.33), calls=%async_computation.5 | async-start | bytes 1310720 | tf_op jit(solution)/shard_map/all_to_all | solution.py:111
  370.1 20.4 %all-to-all-start.4 = ((bf16[4,128,640]{2,1,0:T(8,128)(2,1)}), bf16[4,128,640]{2,1,0:T(8,128)(2,1)S(1)}, u32[]{:S(2)}, u32[]{:S(2)}) async-start(bf16[4,128,640]{2,1,0:T(8,128)(2,1)} %copy.103), calls=%async_computation.4 | async-start | bytes 1310720 | tf_op jit(solution)/shard_map/all_to_all | solution.py:110
  403.6 13.7 %all-to-all-start.7 = ((bf16[4,128,640]{1,2,0:T(8,128)(2,1)}), bf16[4,128,640]{1,2,0:T(8,128)(2,1)S(1)}, u32[]{:S(2)}, u32[]{:S(2)}) async-start(bf16[4,128,640]{1,2,0:T(8,128)(2,1)} %bitcast.48), calls=%async_computation.7 | async-start | bytes 1310720 | tf_op jit(solution)/shard_map/all_to_all | solution.py:113
  (50 other events, 266.6 us)
where the time goes:
time: 421 us; the launch traced here: 418 us
  matrix products  116 us (28%)
  local copies, waits for them, and re-layouts  107 us (25%)
  waiting for transfers between devices  102 us (24%)
  starting transfers between devices  35 us (8%)
  blocking collectives  25.7 us (6%)
  other arithmetic  23.6 us (6%)
  loops' own time  8.54 us (2%)
    ppermute x4, waiting for transfers between devices, shifted(): return lax.ppermute(block, axis, route)  69.5 us
    dot_general x4, matrix products, tile_pass(): jnp.einsum('hwstd,wsk->whktd', dkeys, onehot, precision=highest)  35.4 us
    dot_general x4, matrix products, tile_pass(): jnp.einsum('hwstd,wsk->whktd', dvals, onehot, precision=highest)  35.3 us
    while x112, local copies, waits for them, and re-layouts  22.4 us
    gather x12, local copies, waits for them, and re-layouts, tile_pass(): jnp.take(keys_all[lag], chosen[lag], axis=1)  16.4 us
    gather x12, local copies, waits for them, and re-layouts, tile_pass(): jnp.take(vals_all[lag], chosen[lag], axis=1)  16.4 us
    unnamed x31, local copies, waits for them, and re-layouts  16.2 us
    sub x4, matrix products, tile_pass(): expo = jnp.exp(scores - top)  15.6 us
  transfers between devices with their start and end apart: 10, of which 7 were waited for; matrix products, arithmetic and copies ran while one was open for 6% of the time, Pallas kernels for 0%

commit v1 on v0

v1 whole, which is shorter than its diff:
```python
import math

import jax
import jax.numpy as jnp
from jax import lax
from jax.experimental import pallas as pl
from jax.experimental.pallas import tpu as pltpu
from jax.sharding import PartitionSpec as P

HD = 128
QT = 4
SEL = 3
W = 3
GROUP = 2
CORES = 2
SLOTS = 4
CHUNKS = (2, 3)
NEG = -1e30
AXES = ("tm", "head")


def params(limit=32):
    return pltpu.CompilerParams(vmem_limit_bytes=limit * 2**20)


def moved(block, to):
    frames, heads = lax.axis_size("tm"), lax.axis_size("head")
    route = []
    for t in range(frames):
        for h in range(heads):
            t2, h2 = to(t, h)
            if 0 <= t2 < frames:
                route.append((t * heads + h, t2 * heads + h2))
    return lax.ppermute(block, AXES, route)


def to_slot(block, slot):
    return moved(block, lambda t, h: (t ^ (slot // 2), h ^ (slot % 2 * CORES)))


def to_core(block):
    return moved(block, lambda t, h: (t, h ^ 1))


def to_group(block, step):
    return moved(block, lambda t, h: (t + step * GROUP, h))


def place():
    t, h = lax.axis_index("tm"), lax.axis_index("head")
    return t // GROUP, t % GROUP, h // CORES, h % CORES


def where_am_i():
    t, h = lax.axis_index("tm"), lax.axis_index("head")
    return jnp.stack([t, h]).astype(jnp.int32)


def pack_kernel(chunks, per_chip, me, a_ref, b_ref, *outs):
    x, y = me[0] % GROUP, me[1] // CORES
    tiles = a_ref.shape[1] // (HD * per_chip * GROUP)
    n = 0
    start = 0
    for nh in chunks:
        for slot in range(SLOTS):
            chip = (x ^ (slot // 2)) * tiles + (y ^ (slot % 2))
            for h in range(nh):
                col = pl.multiple_of((chip * per_chip + start + h) * HD, HD)
                outs[n][0, h] = a_ref[:, pl.ds(col, HD)]
                outs[n][1, h] = b_ref[:, pl.ds(col, HD)]
            n += 1
        start += nh


def pack(me, a, b, chunks, per_chip):
    rows = a.shape[0]
    shapes = [
        jax.ShapeDtypeStruct((2, nh, rows, HD), a.dtype) for nh in chunks for _ in range(SLOTS)
    ]
    vmem = pl.BlockSpec(memory_space=pltpu.VMEM)
    outs = pl.pallas_call(
        lambda *refs: pack_kernel(chunks, per_chip, *refs),
        out_shape=shapes,
        in_specs=[pl.BlockSpec(memory_space=pltpu.SMEM), vmem, vmem],
        out_specs=[vmem] * len(shapes),
        compiler_params=params(),
    )(me, a, b)
    return [outs[i * SLOTS : (i + 1) * SLOTS] for i in range(len(chunks))]


def unpack_kernel(chunks, per_chip, me, *refs):
    a_ref, b_ref = refs[-2:]
    x, y = me[0] % GROUP, me[1] // CORES
    tiles = a_ref.shape[1] // (HD * per_chip * GROUP)
    n = 0
    start = 0
    for nh in chunks:
        for slot in range(SLOTS):
            chip = (x ^ (slot // 2)) * tiles + (y ^ (slot % 2))
            for h in range(nh):
                col = pl.multiple_of((chip * per_chip + start + h) * HD, HD)
                a_ref[:, pl.ds(col, HD)] = refs[n][0, h]
                b_ref[:, pl.ds(col, HD)] = refs[n][1, h]
            n += 1
        start += nh


def unpack(me, pieces, chunks, per_chip, width):
    flat = [p for group in pieces for p in group]
    rows = flat[0].shape[2]
    vmem = pl.BlockSpec(memory_space=pltpu.VMEM)
    return pl.pallas_call(
        lambda *refs: unpack_kernel(chunks, per_chip, *refs),
        out_shape=[jax.ShapeDtypeStruct((rows, width), flat[0].dtype)] * 2,
        in_specs=[pl.BlockSpec(memory_space=pltpu.SMEM)] + [vmem] * len(flat),
        out_specs=[vmem] * 2,
        compiler_params=params(),
    )(me, *flat)


def dot(a, b, dims):
    return lax.dot_general(a, b, (dims, ((), ())), preferred_element_type=jnp.float32)


def attend_kernel(me, tp, win, *refs):
    kv_refs = refs[:4]
    qg_refs = refs[4:8]
    aq_refs = refs[8:12]
    own_f, halo_f, own_b, halo_b = refs[12:16]
    kv, ksel, vsel, acc = refs[16:]
    group, x = me[0] // GROUP, me[0] % GROUP
    y, core = me[1] // CORES, me[1] % CORES
    scale = 1.0 / math.sqrt(HD)
    c2 = scale * math.log2(math.e)
    for part in range(4):
        for s in range(SLOTS):
            kv[part * SLOTS + s] = kv_refs[part][s]
    acc[...] = jnp.zeros_like(acc)
    for j in range(SLOTS):
        q = qg_refs[j][0]
        g = qg_refs[j][1]
        xq = x ^ (j // 2)
        tile = (y ^ (j % 2)) * CORES + core
        frame = group * GROUP + xq
        limit = win[frame]
        slots = []
        biases = []
        for lag in range(W):
            rest = xq - lag
            plane = jnp.where(rest < 0, 1, 0)
            dx = (rest & 1) ^ x
            live = (lag <= frame) & (lag < limit)
            biases.append(jnp.where(live, 0.0, NEG))
            for i in range(SEL):
                t = tp[lag, tile, i]
                dc = (t % CORES) ^ core
                dy = (t // CORES) ^ y
                slot = plane * 8 + dc * 4 + dx * 2 + dy
                at = (lag * SEL + i) * HD
                ksel[j, at : at + HD] = kv[slot, 0]
                vsel[j, at : at + HD] = kv[slot, 1]
                slots.append(slot)
        span = SEL * HD
        k_all, v_all = ksel[j], vsel[j]
        s = dot(q, k_all, ((1,), (1,))) * c2
        s = jnp.concatenate(
            [s[:, lag * span : (lag + 1) * span] + biases[lag] for lag in range(W)], 1
        )
        top = jnp.max(s, -1, keepdims=True)
        e = jnp.exp2(s - top)
        prob = e * (1.0 / jnp.sum(e, -1, keepdims=True))
        prob_b = prob.astype(jnp.bfloat16)
        out = dot(prob_b, v_all, ((1,), (0,)))
        delta = jnp.sum(g.astype(jnp.float32) * out, -1, keepdims=True)
        dprob = dot(g, v_all, ((1,), (1,)))
        ds = (prob * (dprob - delta)).astype(jnp.bfloat16)
        aq_refs[j][0] = out.astype(jnp.bfloat16)
        aq_refs[j][1] = (dot(ds, k_all, ((1,), (0,))) * scale).astype(jnp.bfloat16)
        dk = dot(q, ds, ((0,), (0,)))
        dv = dot(g, prob_b, ((0,), (0,)))
        for i, slot in enumerate(slots):
            acc[slot, 0] += dk[:, i * HD : (i + 1) * HD]
            acc[slot, 1] += dv[:, i * HD : (i + 1) * HD]
    for part, ref in enumerate((own_f, own_b, halo_f, halo_b)):
        for s in range(SLOTS):
            ref[s, 0] = (acc[part * SLOTS + s, 0].T * scale).astype(ref.dtype)
            ref[s, 1] = acc[part * SLOTS + s, 1].T.astype(ref.dtype)


def attend(me, tp, win, own, other, halo, halo_other, qg):
    nh, rows = own.shape[2], own.shape[3]
    smem = pl.BlockSpec(memory_space=pltpu.SMEM)
    kv_spec = pl.BlockSpec((SLOTS, 2, None, rows, HD), lambda h: (0, 0, h, 0, 0))
    qg_spec = pl.BlockSpec((2, None, rows, HD), lambda h: (0, h, 0, 0))
    kv_shape = (SLOTS, 2, nh, rows, HD)
    bf, f32 = jnp.bfloat16, jnp.float32
    count = W * SEL * rows
    outs = pl.pallas_call(
        attend_kernel,
        grid=(nh,),
        out_shape=[jax.ShapeDtypeStruct((2, nh, rows, HD), bf)] * 4
        + [jax.ShapeDtypeStruct(kv_shape, t) for t in (f32, f32, bf, bf)],
        in_specs=[smem] * 3 + [kv_spec] * 4 + [qg_spec] * 4,
        out_specs=[qg_spec] * 4 + [kv_spec] * 4,
        scratch_shapes=[
            pltpu.VMEM((4 * SLOTS, 2, rows, HD), bf),
            pltpu.VMEM((SLOTS, count, HD), bf),
            pltpu.VMEM((SLOTS, count, HD), bf),
            pltpu.VMEM((4 * SLOTS, 2, HD, rows), f32),
        ],
        compiler_params=params(),
        cost_estimate=pl.CostEstimate(
            flops=nh * SLOTS * 12 * rows * count * HD,
            bytes_accessed=nh * rows * HD * 2 * 72,
            transcendentals=nh * SLOTS * rows * count,
        ),
    )(me, tp, win, own, other, halo, halo_other, *qg)
    return outs[:4], outs[4:]


def shards(query, keys, values, grad_out, tile_pattern, window):
    width = query.shape[1]
    per_chip = width // HD // (GROUP * (lax.axis_size("head") // CORES))
    chunks = CHUNKS if sum(CHUNKS) == per_chip else (per_chip,)
    me = where_am_i()
    f32, bf = jnp.float32, jnp.bfloat16
    kv_sent = pack(me, keys, values, chunks, per_chip)
    qg_sent = pack(me, query, grad_out, chunks, per_chip)
    out_pieces, grad_pieces = [], []
    for i in range(len(chunks)):
        kv = [kv_sent[i][0]] + [to_slot(kv_sent[i][s], s) for s in range(1, SLOTS)]
        qg = [qg_sent[i][0]] + [to_slot(qg_sent[i][s], s) for s in range(1, SLOTS)]
        own = jnp.stack(kv)
        halo = to_group(own, 1)
        other = to_core(own)
        halo_other = to_core(halo)
        aq, (own_f, halo_f, own_b, halo_b) = attend(
            me, tile_pattern, window, own, other, halo, halo_other, qg
        )
        back = (halo_f + to_core(halo_b).astype(f32)).astype(bf)
        later = to_group(back, -1)
        mine = to_core(own_b)
        out_pieces.append([aq[0]] + [to_slot(aq[s], s) for s in range(1, SLOTS)])
        total = [
            (own_f[s] + mine[s].astype(f32) + later[s].astype(f32)).astype(bf)
            for s in range(SLOTS)
        ]
        grad_pieces.append([total[0]] + [to_slot(total[s], s) for s in range(1, SLOTS)])
    attended, grad_query = unpack(me, out_pieces, chunks, per_chip, width)
    grad_keys, grad_values = unpack(me, grad_pieces, chunks, per_chip, width)
    return (attended, grad_query, grad_keys, grad_values)


def solution(mesh):
    placed = P(AXES, None)
    return jax.shard_map(
        shards,
        mesh=mesh,
        in_specs=(placed,) * 4 + (P(), P()),
        out_specs=(placed,) * 4,
        check_vma=False,
    )
```

time: 421 us -> 168 us (0.40)
  matrix products: 116 us -> 0 us
  local copies, waits for them, and re-layouts: 107 us -> 2.2 us
  Pallas kernels: 0 us -> 32.5 us
  blocking collectives: 25.7 us -> 0 us
  other arithmetic: 23.6 us -> 1.13 us
  waiting for transfers between devices: 102 us -> 85.6 us
  starting transfers between devices: 35 us -> 45.7 us
  loops' own time: 8.54 us -> 0 us
    dot_general x28 -> x0, matrix products: 100 us -> none  [the longest x4 35.4 us: tile_pass(): jnp.einsum('hwstd,wsk->whktd', dkeys, onehot, precision=highest)]
    while x114 -> x0, local copies, waits for them, and re-layouts: 35 us -> none
    ppermute x4 -> x36, starting transfers between devices: 12.6 us -> 45.7 us  [moved(): return lax.ppermute(block, AXES, route)]
    all_to_all x6 -> x0, waiting for transfers between devices: 32.9 us -> none  [the longest x1 9.91 us: shards(): lax.all_to_all(keys, 'head', split_axis=1, concat_axis=0, tiled=True)]
    gather x24 -> x0, local copies, waits for them, and re-layouts: 32.8 us -> none  [the longest x12 16.4 us: tile_pass(): jnp.take(keys_all[lag], chosen[lag], axis=1)]
    pallas_call x0 -> x6, Pallas kernels: none -> 32.5 us  [the longest x2 27.2 us: attend(): pl.pallas_call(attend_kernel, grid=(nh,), out_shape=[jax.ShapeDtypeStruct...]
    all_to_all x2 -> x0, blocking collectives: 25.7 us -> none  [the longest x1 13.1 us: shards(): lax.all_to_all(dk_loc, 'head', split_axis=0, concat_axis=1, tiled=True)]
    all_to_all x6 -> x0, starting transfers between devices: 22.4 us -> none  [the longest x1 4.24 us: shards(): lax.all_to_all(keys, 'head', split_axis=1, concat_axis=0, tiled=True)]
  transfers between devices with their start and end apart: 10 -> 36, of which waited for: 7 -> 17; matrix products, arithmetic and copies ran while one was open for 6% -> 1% of each run, Pallas kernels for 0% -> 18%
where the time goes in v1:
time: 168 us
  waiting for transfers between devices  85.6 us (51%)
  starting transfers between devices  45.7 us (27%)
  Pallas kernels  32.5 us (19%)
  local copies, waits for them, and re-layouts  2.2 us (1%)
    ppermute x36, waiting for transfers between devices, moved(): return lax.ppermute(block, AXES, route)  85.6 us
    ppermute x36, starting transfers between devices, moved(): return lax.ppermute(block, AXES, route)  45.7 us
    pallas_call x2, Pallas kernels, attend(): pl.pallas_call(attend_kernel, grid=(nh,), out_shape=[jax.ShapeDtypeStruct...  27.2 us
    pallas_call x2, Pallas kernels, unpack(): pl.pallas_call(lambda *refs: unpack_kernel(chunks, per_chip, *refs), out_...  3.7 us
  transfers between devices with their start and end apart: 36, of which 17 were waited for; matrix products, arithmetic and copies ran while one was open for 1% of the time, Pallas kernels for 18%

profile of v1, /device:TPU:0, one launch (start us, length us, event | category | flops | bytes accessed | tf_op | source)
XLA Modules:
  0.0 168.0 jit_solution(5709932536654574630)
XLA Ops:
  3.7 3.0 %collective-permute-start.12 = (bf16[2,3,128,128]{3,2,1,0:T(8,128)(2,1)S(1)}, bf16[2,3,128,128]{3,2,1,0:T(8,128)(2,1)S(1)}, u32[]{:S(2)}, u32[]{:S(2)}) collective-permute-start(bf16[2,3,128,128]{3,2,1,0:T(8,128)(2,1)S(1)} %get-tuple-element.53), channel_id=1, source_target_pairs={{0,2},{1,3},{2,0},{3,1},{4,6},{5,7},{6,4},{7,5},{8,10},{9,11},{10,... | collective-permute-start | bytes 589832 | tf_op jit(solution)/shard_map/ppermute | solution.py:34
  8.3 3.4 %collective-permute-done.12 = bf16[2,3,128,128]{3,2,1,0:T(8,128)(2,1)S(1)} collective-permute-done((bf16[2,3,128,128]{3,2,1,0:T(8,128)(2,1)S(1)}, bf16[2,3,128,128]{3,2,1,0:T(8,128)(2,1)S(1)}, u32[]{:S(2)}, u32[]{:S(2)}) %collective-permute-start.12) | collective-permute-done | bytes 196640 | tf_op jit(solution)/shard_map/ppermute | solution.py:34
  11.6 2.9 %collective-permute-done.13 = bf16[2,3,128,128]{3,2,1,0:T(8,128)(2,1)S(1)} collective-permute-done((bf16[2,3,128,128]{3,2,1,0:T(8,128)(2,1)S(1)}, bf16[2,3,128,128]{3,2,1,0:T(8,128)(2,1)S(1)}, u32[]{:S(2)}, u32[]{:S(2)}) %collective-permute-start.13) | collective-permute-done | bytes 196640 | tf_op jit(solution)/shard_map/ppermute | solution.py:34
  14.6 2.5 %collective-permute-done.14 = bf16[2,3,128,128]{3,2,1,0:T(8,128)(2,1)S(1)} collective-permute-done((bf16[2,3,128,128]{3,2,1,0:T(8,128)(2,1)S(1)}, bf16[2,3,128,128]{3,2,1,0:T(8,128)(2,1)S(1)}, u32[]{:S(2)}, u32[]{:S(2)}) %collective-permute-start.14) | collective-permute-done | bytes 196640 | tf_op jit(solution)/shard_map/ppermute | solution.py:34
  17.2 3.7 %collective-permute-start.16 = (bf16[4,2,3,128,128]{4,3,2,1,0:T(8,128)(2,1)S(1)}, bf16[4,2,3,128,128]{4,3,2,1,0:T(8,128)(2,1)S(1)}, u32[]{:S(2)}, u32[]{:S(2)}) collective-permute-start(bf16[4,2,3,128,128]{4,3,2,1,0:T(8,128)(2,1)S(1)} %pad_maximum_fusion.refs_0_), channel_id=1, source_target_pairs={{0,8},{1,9},{2,10},{3,11},{4,12},{5,13},{6,14},{7,15},{8,16},{9,17... | collective-permute-start | bytes 2359304 | tf_op jit(solution)/shard_map/ppermute | solution.py:34
  21.0 15.5 %collective-permute-done.16.refs_2_ = bf16[4,2,3,128,128]{4,3,2,1,0:T(8,128)(2,1)S(1)} collective-permute-done((bf16[4,2,3,128,128]{4,3,2,1,0:T(8,128)(2,1)S(1)}, bf16[4,2,3,128,128]{4,3,2,1,0:T(8,128)(2,1)S(1)}, u32[]{:S(2)}, u32[]{:S(2)}) %collective-permute-start.16) | collective-permute-done | bytes 786464 | tf_op jit(solution)/shard_map/ppermute | solution.py:34
  40.0 2.4 %collective-permute-done = bf16[2,2,128,128]{3,2,1,0:T(8,128)(2,1)S(1)} collective-permute-done((bf16[2,2,128,128]{3,2,1,0:T(8,128)(2,1)S(1)}, bf16[2,2,128,128]{3,2,1,0:T(8,128)(2,1)S(1)}, u32[]{:S(2)}, u32[]{:S(2)}) %collective-permute-start) | collective-permute-done | bytes 131104 | tf_op jit(solution)/shard_map/ppermute | solution.py:34
  46.4 4.4 %collective-permute-start.4 = (bf16[4,2,2,128,128]{4,3,2,1,0:T(8,128)(2,1)S(1)}, bf16[4,2,2,128,128]{4,3,2,1,0:T(8,128)(2,1)S(1)}, u32[]{:S(2)}, u32[]{:S(2)}) collective-permute-start(bf16[4,2,2,128,128]{4,3,2,1,0:T(8,128)(2,1)S(1)} %pad_maximum_fusion.1.refs_0_), channel_id=1, source_target_pairs={{0,8},{1,9},{2,10},{3,11},{4,12},{5,13},{6,14},{7,15},{8,16},{9,17... | collective-permute-start | bytes 1572872 | tf_op jit(solution)/shard_map/ppermute | solution.py:34
  54.8 3.0 %collective-permute-done.18.refs_5_ = bf16[2,3,128,128]{3,2,1,0:T(8,128)(2,1)S(1)} collective-permute-done((bf16[2,3,128,128]{3,2,1,0:T(8,128)(2,1)S(1)}, bf16[2,3,128,128]{3,2,1,0:T(8,128)(2,1)S(1)}, u32[]{:S(2)}, u32[]{:S(2)}) %collective-permute-start.18) | collective-permute-done | bytes 196640 | tf_op jit(solution)/shard_map/ppermute | solution.py:34
  57.8 2.3 %collective-permute-start.20 = (bf16[2,3,128,128]{3,2,1,0:T(8,128)(2,1)S(1)}, bf16[2,3,128,128]{3,2,1,0:T(8,128)(2,1)S(1)}, u32[]{:S(2)}, u32[]{:S(2)}) collective-permute-start(bf16[2,3,128,128]{3,2,1,0:T(8,128)(2,1)S(1)} %get-tuple-element.59), channel_id=1, source_target_pairs={{0,6},{1,7},{2,4},{3,5},{4,2},{5,3},{6,0},{7,1},{8,14},{9,15},{10,... | collective-permute-start | bytes 589832 | tf_op jit(solution)/shard_map/ppermute | solution.py:34
  61.7 2.7 %collective-permute-done.20.refs_7_ = bf16[2,3,128,128]{3,2,1,0:T(8,128)(2,1)S(1)} collective-permute-done((bf16[2,3,128,128]{3,2,1,0:T(8,128)(2,1)S(1)}, bf16[2,3,128,128]{3,2,1,0:T(8,128)(2,1)S(1)}, u32[]{:S(2)}, u32[]{:S(2)}) %collective-permute-start.20) | collective-permute-done | bytes 196640 | tf_op jit(solution)/shard_map/ppermute | solution.py:34
  64.4 16.2 %shard_map.96 = (bf16[2,3,128,128]{3,2,1,0:T(8,128)(2,1)S(1)}, bf16[2,3,128,128]{3,2,1,0:T(8,128)(2,1)S(1)}, bf16[2,3,128,128]{3,2,1,0:T(8,128)(2,1)S(1)}, bf16[...) custom-call(s32[2]{0:T(128)S(1)} %pad_add_fusion.refs_0_.me, ...), custom_call_target="tpu_custom_call" | custom-call | flops 2717908992 | bytes 7077888 | tf_op jit(solution)/shard_map/pallas_call | solution.py:198
  83.7 2.9 %collective-permute-done.6.refs_5_ = bf16[2,2,128,128]{3,2,1,0:T(8,128)(2,1)S(1)} collective-permute-done((bf16[2,2,128,128]{3,2,1,0:T(8,128)(2,1)S(1)}, bf16[2,2,128,128]{3,2,1,0:T(8,128)(2,1)S(1)}, u32[]{:S(2)}, u32[]{:S(2)}) %collective-permute-start.6) | collective-permute-done | bytes 131104 | tf_op jit(solution)/shard_map/ppermute | solution.py:34
  86.6 2.3 %collective-permute-start.8 = (bf16[2,2,128,128]{3,2,1,0:T(8,128)(2,1)S(1)}, bf16[2,2,128,128]{3,2,1,0:T(8,128)(2,1)S(1)}, u32[]{:S(2)}, u32[]{:S(2)}) collective-permute-start(bf16[2,2,128,128]{3,2,1,0:T(8,128)(2,1)S(1)} %get-tuple-element.47), channel_id=1, source_target_pairs={{0,6},{1,7},{2,4},{3,5},{4,2},{5,3},{6,0},{7,1},{8,14},{9,15},{10,... | collective-permute-start | bytes 393224 | tf_op jit(solution)/shard_map/ppermute | solution.py:34
  89.0 3.6 %collective-permute-done.8.refs_7_ = bf16[2,2,128,128]{3,2,1,0:T(8,128)(2,1)S(1)} collective-permute-done((bf16[2,2,128,128]{3,2,1,0:T(8,128)(2,1)S(1)}, bf16[2,2,128,128]{3,2,1,0:T(8,128)(2,1)S(1)}, u32[]{:S(2)}, u32[]{:S(2)}) %collective-permute-start.8) | collective-permute-done | bytes 131104 | tf_op jit(solution)/shard_map/ppermute | solution.py:34
  92.6 11.0 %shard_map.95 = (bf16[2,2,128,128]{3,2,1,0:T(8,128)(2,1)S(1)}, bf16[2,2,128,128]{3,2,1,0:T(8,128)(2,1)S(1)}, bf16[2,2,128,128]{3,2,1,0:T(8,128)(2,1)S(1)}, bf16[...) custom-call(s32[2]{0:T(128)S(1)} %pad_add_fusion.refs_0_.me, ...), custom_call_target="tpu_custom_call" | custom-call | flops 1811939328 | bytes 4718592 | tf_op jit(solution)/shard_map/pallas_call | solution.py:198
  110.4 27.3 %collective-permute-done.26 = bf16[4,2,2,128,128]{4,3,2,1,0:T(8,128)(2,1)S(1)} collective-permute-done((bf16[4,2,2,128,128]{4,3,2,1,0:T(8,128)(2,1)S(1)}, bf16[4,2,2,128,128]{4,3,2,1,0:T(8,128)(2,1)S(1)}, u32[]{:S(2)}, u32[]{:S(2)}) %collective-permute-start.26) | collective-permute-done | bytes 524320 | tf_op jit(solution)/shard_map/ppermute | solution.py:34
  137.7 2.3 %collective-permute-start.11 = (bf16[2,2,128,128]{3,2,1,0:T(8,128)(2,1)S(1)}, bf16[2,2,128,128]{3,2,1,0:T(8,128)(2,1)S(1)}, u32[]{:S(2)}, u32[]{:S(2)}) collective-permute-start(bf16[2,2,128,128]{3,2,1,0:T(8,128)(2,1)S(1)} %get-tuple-element.51), channel_id=1, source_target_pairs={{0,6},{1,7},{2,4},{3,5},{4,2},{5,3},{6,0},{7,1},{8,14},{9,15},{10,... | collective-permute-start | bytes 393224 | tf_op jit(solution)/shard_map/ppermute | solution.py:34
  141.5 2.3 %collective-permute-start.23 = (bf16[2,3,128,128]{3,2,1,0:T(8,128)(2,1)S(1)}, bf16[2,3,128,128]{3,2,1,0:T(8,128)(2,1)S(1)}, u32[]{:S(2)}, u32[]{:S(2)}) collective-permute-start(bf16[2,3,128,128]{3,2,1,0:T(8,128)(2,1)S(1)} %get-tuple-element.63), channel_id=1, source_target_pairs={{0,6},{1,7},{2,4},{3,5},{4,2},{5,3},{6,0},{7,1},{8,14},{9,15},{10,... | collective-permute-start | bytes 589832 | tf_op jit(solution)/shard_map/ppermute | solution.py:34
  144.8 2.6 %collective-permute-start.35 = (bf16[2,3,128,128]{3,2,1,0:T(8,128)(2,1)S(1)}, bf16[2,3,128,128]{3,2,1,0:T(8,128)(2,1)S(1)}, u32[]{:S(2)}, u32[]{:S(2)}) collective-permute-start(bf16[2,3,128,128]{3,2,1,0:T(8,128)(2,1)S(1)} %get-tuple-element.76), channel_id=1, source_target_pairs={{0,6},{1,7},{2,4},{3,5},{4,2},{5,3},{6,0},{7,1},{8,14},{9,15},{10,... | collective-permute-start | bytes 589832 | tf_op jit(solution)/shard_map/ppermute | solution.py:34
  147.4 2.3 %collective-permute-done.21.refs_6_ = bf16[2,3,128,128]{3,2,1,0:T(8,128)(2,1)S(1)} collective-permute-done((bf16[2,3,128,128]{3,2,1,0:T(8,128)(2,1)S(1)}, bf16[2,3,128,128]{3,2,1,0:T(8,128)(2,1)S(1)}, u32[]{:S(2)}, u32[]{:S(2)}) %collective-permute-start.21) | collective-permute-done | bytes 196640 | tf_op jit(solution)/shard_map/ppermute | solution.py:34
  151.4 2.5 %collective-permute-done.23.refs_8_ = bf16[2,3,128,128]{3,2,1,0:T(8,128)(2,1)S(1)} collective-permute-done((bf16[2,3,128,128]{3,2,1,0:T(8,128)(2,1)S(1)}, bf16[2,3,128,128]{3,2,1,0:T(8,128)(2,1)S(1)}, u32[]{:S(2)}, u32[]{:S(2)}) %collective-permute-start.23) | collective-permute-done | bytes 196640 | tf_op jit(solution)/shard_map/ppermute | solution.py:34
  154.7 2.1 %collective-permute-done.29.refs_4_ = bf16[2,2,128,128]{3,2,1,0:T(8,128)(2,1)S(1)} collective-permute-done((bf16[2,2,128,128]{3,2,1,0:T(8,128)(2,1)S(1)}, bf16[2,2,128,128]{3,2,1,0:T(8,128)(2,1)S(1)}, u32[]{:S(2)}, u32[]{:S(2)}) %collective-permute-start.29) | collective-permute-done | bytes 131104 | tf_op jit(solution)/shard_map/ppermute | solution.py:34
  159.4 6.8 %collective-permute-done.28.refs_3_ = bf16[2,2,128,128]{3,2,1,0:T(8,128)(2,1)S(1)} collective-permute-done((bf16[2,2,128,128]{3,2,1,0:T(8,128)(2,1)S(1)}, bf16[2,2,128,128]{3,2,1,0:T(8,128)(2,1)S(1)}, u32[]{:S(2)}, u32[]{:S(2)}) %collective-permute-start.28) | collective-permute-done | bytes 131104 | tf_op jit(solution)/shard_map/ppermute | solution.py:34
  (73 shorter events, 36.9 us)
Async XLA Ops:
  3.7 7.9 %collective-permute-start.12 = (bf16[2,3,128,128]{3,2,1,0:T(8,128)(2,1)S(1)}, bf16[2,3,128,128]{3,2,1,0:T(8,128)(2,1)S(1)}, u32[]{:S(2)}, u32[]{:S(2)}) collective-permute-start(bf16[2,3,128,128]{3,2,1,0:T(8,128)(2,1)S(1)} %get-tuple-element.53), channel_id=1, source_target_pairs={{0,2},{1,3},{2,0},{3,1},{4,6},{5,7},{6,4},{7,5},{8,10},{9,11},{10,... | collective-permute-start | bytes 589832 | tf_op jit(solution)/shard_map/ppermute | solution.py:34
  6.7 7.8 %collective-permute-start.13 = (bf16[2,3,128,128]{3,2,1,0:T(8,128)(2,1)S(1)}, bf16[2,3,128,128]{3,2,1,0:T(8,128)(2,1)S(1)}, u32[]{:S(2)}, u32[]{:S(2)}) collective-permute-start(bf16[2,3,128,128]{3,2,1,0:T(8,128)(2,1)S(1)} %get-tuple-element.54), channel_id=1, source_target_pairs={{0,4},{1,5},{2,6},{3,7},{4,0},{5,1},{6,2},{7,3},{8,12},{9,13},{10,... | collective-permute-start | bytes 589832 | tf_op jit(solution)/shard_map/ppermute | solution.py:34
  8.2 8.9 %collective-permute-start.14 = (bf16[2,3,128,128]{3,2,1,0:T(8,128)(2,1)S(1)}, bf16[2,3,128,128]{3,2,1,0:T(8,128)(2,1)S(1)}, u32[]{:S(2)}, u32[]{:S(2)}) collective-permute-start(bf16[2,3,128,128]{3,2,1,0:T(8,128)(2,1)S(1)} %get-tuple-element.55), channel_id=1, source_target_pairs={{0,6},{1,7},{2,4},{3,5},{4,2},{5,3},{6,0},{7,1},{8,14},{9,15},{10,... | collective-permute-start | bytes 589832 | tf_op jit(solution)/shard_map/ppermute | solution.py:34
  17.2 19.2 %collective-permute-start.16 = (bf16[4,2,3,128,128]{4,3,2,1,0:T(8,128)(2,1)S(1)}, bf16[4,2,3,128,128]{4,3,2,1,0:T(8,128)(2,1)S(1)}, u32[]{:S(2)}, u32[]{:S(2)}) collective-permute-start(bf16[4,2,3,128,128]{4,3,2,1,0:T(8,128)(2,1)S(1)} %pad_maximum_fusion.refs_0_), channel_id=1, source_target_pairs={{0,8},{1,9},{2,10},{3,11},{4,12},{5,13},{6,14},{7,15},{8,16},{9,17... | collective-permute-start | bytes 2359304 | tf_op jit(solution)/shard_map/ppermute | solution.py:34
  20.9 43.5 %collective-permute-start.15 = (bf16[4,2,3,128,128]{4,3,2,1,0:T(8,128)(2,1)S(1)}, bf16[4,2,3,128,128]{4,3,2,1,0:T(8,128)(2,1)S(1)}, u32[]{:S(2)}, u32[]{:S(2)}) collective-permute-start(bf16[4,2,3,128,128]{4,3,2,1,0:T(8,128)(2,1)S(1)} %pad_maximum_fusion.refs_0_), channel_id=1, source_target_pairs={{0,1},{1,0},{2,3},{3,2},{4,5},{5,4},{6,7},{7,6},{8,9},{9,8},{10,11... | collective-permute-start | bytes 2359304 | tf_op jit(solution)/shard_map/ppermute | solution.py:34
  36.5 27.9 %collective-permute-start.17 = (bf16[4,2,3,128,128]{4,3,2,1,0:T(8,128)(2,1)S(1)}, bf16[4,2,3,128,128]{4,3,2,1,0:T(8,128)(2,1)S(1)}, u32[]{:S(2)}, u32[]{:S(2)}) collective-permute-start(bf16[4,2,3,128,128]{4,3,2,1,0:T(8,128)(2,1)S(1)} %collective-permute-done.16.refs_2_), channel_id=1, source_target_pairs={{0,1},{1,0},{2,3},{3,2},{4,5},{5,4},{6,7},{7,6},{8,9},{9,8},{10,11... | collective-permute-start | bytes 2359304 | tf_op jit(solution)/shard_map/ppermute | solution.py:34
  46.4 15.3 %collective-permute-start.4 = (bf16[4,2,2,128,128]{4,3,2,1,0:T(8,128)(2,1)S(1)}, bf16[4,2,2,128,128]{4,3,2,1,0:T(8,128)(2,1)S(1)}, u32[]{:S(2)}, u32[]{:S(2)}) collective-permute-start(bf16[4,2,2,128,128]{4,3,2,1,0:T(8,128)(2,1)S(1)} %pad_maximum_fusion.1.refs_0_), channel_id=1, source_target_pairs={{0,8},{1,9},{2,10},{3,11},{4,12},{5,13},{6,14},{7,15},{8,16},{9,17... | collective-permute-start | bytes 1572872 | tf_op jit(solution)/shard_map/ppermute | solution.py:34
  60.1 32.5 %collective-permute-start.3 = (bf16[4,2,2,128,128]{4,3,2,1,0:T(8,128)(2,1)S(1)}, bf16[4,2,2,128,128]{4,3,2,1,0:T(8,128)(2,1)S(1)}, u32[]{:S(2)}, u32[]{:S(2)}) collective-permute-start(bf16[4,2,2,128,128]{4,3,2,1,0:T(8,128)(2,1)S(1)} %pad_maximum_fusion.1.refs_0_), channel_id=1, source_target_pairs={{0,1},{1,0},{2,3},{3,2},{4,5},{5,4},{6,7},{7,6},{8,9},{9,8},{10,11... | collective-permute-start | bytes 1572872 | tf_op jit(solution)/shard_map/ppermute | solution.py:34
  61.7 30.9 %collective-permute-start.5 = (bf16[4,2,2,128,128]{4,3,2,1,0:T(8,128)(2,1)S(1)}, bf16[4,2,2,128,128]{4,3,2,1,0:T(8,128)(2,1)S(1)}, u32[]{:S(2)}, u32[]{:S(2)}) collective-permute-start(bf16[4,2,2,128,128]{4,3,2,1,0:T(8,128)(2,1)S(1)} %collective-permute-done.4.refs_2_), channel_id=1, source_target_pairs={{0,1},{1,0},{2,3},{3,2},{4,5},{5,4},{6,7},{7,6},{8,9},{9,8},{10,11... | collective-permute-start | bytes 1572872 | tf_op jit(solution)/shard_map/ppermute | solution.py:34
  80.6 23.6 %collective-permute-start.31 = (bf16[4,2,3,128,128]{4,3,2,1,0:T(8,128)(2,1)S(1)}, bf16[4,2,3,128,128]{4,3,2,1,0:T(8,128)(2,1)S(1)}, u32[]{:S(2)}, u32[]{:S(2)}) collective-permute-start(bf16[4,2,3,128,128]{4,3,2,1,0:T(8,128)(2,1)S(1)} %get-tuple-element.73), channel_id=1, source_target_pairs={{0,1},{1,0},{2,3},{3,2},{4,5},{5,4},{6,7},{7,6},{8,9},{9,8},{10,11... | collective-permute-start | bytes 2359304 | tf_op jit(solution)/shard_map/ppermute | solution.py:34
  104.2 37.3 %collective-permute-start.30 = (bf16[4,2,3,128,128]{4,3,2,1,0:T(8,128)(2,1)S(1)}, bf16[4,2,3,128,128]{4,3,2,1,0:T(8,128)(2,1)S(1)}, u32[]{:S(2)}, u32[]{:S(2)}) collective-permute-start(bf16[4,2,3,128,128]{4,3,2,1,0:T(8,128)(2,1)S(1)} %get-tuple-element.71), channel_id=1, source_target_pairs={{0,1},{1,0},{2,3},{3,2},{4,5},{5,4},{6,7},{7,6},{8,9},{9,8},{10,11... | collective-permute-start | bytes 2359304 | tf_op jit(solution)/shard_map/ppermute | solution.py:34
  104.5 39.3 %collective-permute-start.32 = (bf16[4,2,3,128,128]{4,3,2,1,0:T(8,128)(2,1)S(1)}, bf16[4,2,3,128,128]{4,3,2,1,0:T(8,128)(2,1)S(1)}, u32[]{:S(2)}, u32[]{:S(2)}) collective-permute-start(bf16[4,2,3,128,128]{4,3,2,1,0:T(8,128)(2,1)S(1)} %add_convert_fusion), channel_id=1, source_target_pairs={{8,0},{9,1},{10,2},{11,3},{12,4},{13,5},{14,6},{15,7},{16,8},{17,9... | collective-permute-start | bytes 2359304 | tf_op jit(solution)/shard_map/ppermute | solution.py:34
  106.1 31.6 %collective-permute-start.26 = (bf16[4,2,2,128,128]{4,3,2,1,0:T(8,128)(2,1)S(1)}, bf16[4,2,2,128,128]{4,3,2,1,0:T(8,128)(2,1)S(1)}, u32[]{:S(2)}, u32[]{:S(2)}) collective-permute-start(bf16[4,2,2,128,128]{4,3,2,1,0:T(8,128)(2,1)S(1)} %add_convert_fusion.1), channel_id=1, source_target_pairs={{8,0},{9,1},{10,2},{11,3},{12,4},{13,5},{14,6},{15,7},{16,8},{17,9... | collective-permute-start | bytes 1572872 | tf_op jit(solution)/shard_map/ppermute | solution.py:34
  107.4 32.8 %collective-permute-start.9 = (bf16[2,2,128,128]{3,2,1,0:T(8,128)(2,1)S(1)}, bf16[2,2,128,128]{3,2,1,0:T(8,128)(2,1)S(1)}, u32[]{:S(2)}, u32[]{:S(2)}) collective-permute-start(bf16[2,2,128,128]{3,2,1,0:T(8,128)(2,1)S(1)} %get-tuple-element.49), channel_id=1, source_target_pairs={{0,2},{1,3},{2,0},{3,1},{4,6},{5,7},{6,4},{7,5},{8,10},{9,11},{10,... | collective-permute-start | bytes 393224 | tf_op jit(solution)/shard_map/ppermute | solution.py:34
  108.9 31.9 %collective-permute-start.10 = (bf16[2,2,128,128]{3,2,1,0:T(8,128)(2,1)S(1)}, bf16[2,2,128,128]{3,2,1,0:T(8,128)(2,1)S(1)}, u32[]{:S(2)}, u32[]{:S(2)}) collective-permute-start(bf16[2,2,128,128]{3,2,1,0:T(8,128)(2,1)S(1)} %get-tuple-element.50), channel_id=1, source_target_pairs={{0,4},{1,5},{2,6},{3,7},{4,0},{5,1},{6,2},{7,3},{8,12},{9,13},{10,... | collective-permute-start | bytes 393224 | tf_op jit(solution)/shard_map/ppermute | solution.py:34
  140.3 9.4 %collective-permute-start.21 = (bf16[2,3,128,128]{3,2,1,0:T(8,128)(2,1)S(1)}, bf16[2,3,128,128]{3,2,1,0:T(8,128)(2,1)S(1)}, u32[]{:S(2)}, u32[]{:S(2)}) collective-permute-start(bf16[2,3,128,128]{3,2,1,0:T(8,128)(2,1)S(1)} %get-tuple-element.61), channel_id=1, source_target_pairs={{0,2},{1,3},{2,0},{3,1},{4,6},{5,7},{6,4},{7,5},{8,10},{9,11},{10,... | collective-permute-start | bytes 589832 | tf_op jit(solution)/shard_map/ppermute | solution.py:34
  140.8 9.5 %collective-permute-start.22 = (bf16[2,3,128,128]{3,2,1,0:T(8,128)(2,1)S(1)}, bf16[2,3,128,128]{3,2,1,0:T(8,128)(2,1)S(1)}, u32[]{:S(2)}, u32[]{:S(2)}) collective-permute-start(bf16[2,3,128,128]{3,2,1,0:T(8,128)(2,1)S(1)} %get-tuple-element.62), channel_id=1, source_target_pairs={{0,4},{1,5},{2,6},{3,7},{4,0},{5,1},{6,2},{7,3},{8,12},{9,13},{10,... | collective-permute-start | bytes 589832 | tf_op jit(solution)/shard_map/ppermute | solution.py:34
  141.5 12.5 %collective-permute-start.23 = (bf16[2,3,128,128]{3,2,1,0:T(8,128)(2,1)S(1)}, bf16[2,3,128,128]{3,2,1,0:T(8,128)(2,1)S(1)}, u32[]{:S(2)}, u32[]{:S(2)}) collective-permute-start(bf16[2,3,128,128]{3,2,1,0:T(8,128)(2,1)S(1)} %get-tuple-element.63), channel_id=1, source_target_pairs={{0,6},{1,7},{2,4},{3,5},{4,2},{5,3},{6,0},{7,1},{8,14},{9,15},{10,... | collective-permute-start | bytes 589832 | tf_op jit(solution)/shard_map/ppermute | solution.py:34
  143.8 12.9 %collective-permute-start.29 = (bf16[2,2,128,128]{3,2,1,0:T(8,128)(2,1)S(1)}, bf16[2,2,128,128]{3,2,1,0:T(8,128)(2,1)S(1)}, u32[]{:S(2)}, u32[]{:S(2)}) collective-permute-start(bf16[2,2,128,128]{3,2,1,0:T(8,128)(2,1)S(1)} %get-tuple-element.80), channel_id=1, source_target_pairs={{0,6},{1,7},{2,4},{3,5},{4,2},{5,3},{6,0},{7,1},{8,14},{9,15},{10,... | collective-permute-start | bytes 393224 | tf_op jit(solution)/shard_map/ppermute | solution.py:34
  144.8 21.4 %collective-permute-start.35 = (bf16[2,3,128,128]{3,2,1,0:T(8,128)(2,1)S(1)}, bf16[2,3,128,128]{3,2,1,0:T(8,128)(2,1)S(1)}, u32[]{:S(2)}, u32[]{:S(2)}) collective-permute-start(bf16[2,3,128,128]{3,2,1,0:T(8,128)(2,1)S(1)} %get-tuple-element.76), channel_id=1, source_target_pairs={{0,6},{1,7},{2,4},{3,5},{4,2},{5,3},{6,0},{7,1},{8,14},{9,15},{10,... | collective-permute-start | bytes 589832 | tf_op jit(solution)/shard_map/ppermute | solution.py:34
  149.6 16.5 %collective-permute-start.34 = (bf16[2,3,128,128]{3,2,1,0:T(8,128)(2,1)S(1)}, bf16[2,3,128,128]{3,2,1,0:T(8,128)(2,1)S(1)}, u32[]{:S(2)}, u32[]{:S(2)}) collective-permute-start(bf16[2,3,128,128]{3,2,1,0:T(8,128)(2,1)S(1)} %get-tuple-element.77), channel_id=1, source_target_pairs={{0,4},{1,5},{2,6},{3,7},{4,0},{5,1},{6,2},{7,3},{8,12},{9,13},{10,... | collective-permute-start | bytes 589832 | tf_op jit(solution)/shard_map/ppermute | solution.py:34
  150.4 15.8 %collective-permute-start.33 = (bf16[2,3,128,128]{3,2,1,0:T(8,128)(2,1)S(1)}, bf16[2,3,128,128]{3,2,1,0:T(8,128)(2,1)S(1)}, u32[]{:S(2)}, u32[]{:S(2)}) collective-permute-start(bf16[2,3,128,128]{3,2,1,0:T(8,128)(2,1)S(1)} %get-tuple-element.78), channel_id=1, source_target_pairs={{0,2},{1,3},{2,0},{3,1},{4,6},{5,7},{6,4},{7,5},{8,10},{9,11},{10,... | collective-permute-start | bytes 589832 | tf_op jit(solution)/shard_map/ppermute | solution.py:34
  153.9 12.2 %collective-permute-start.28 = (bf16[2,2,128,128]{3,2,1,0:T(8,128)(2,1)S(1)}, bf16[2,2,128,128]{3,2,1,0:T(8,128)(2,1)S(1)}, u32[]{:S(2)}, u32[]{:S(2)}) collective-permute-start(bf16[2,2,128,128]{3,2,1,0:T(8,128)(2,1)S(1)} %get-tuple-element.81), channel_id=1, source_target_pairs={{0,4},{1,5},{2,6},{3,7},{4,0},{5,1},{6,2},{7,3},{8,12},{9,13},{10,... | collective-permute-start | bytes 393224 | tf_op jit(solution)/shard_map/ppermute | solution.py:34
  156.8 9.4 %collective-permute-start.27 = (bf16[2,2,128,128]{3,2,1,0:T(8,128)(2,1)S(1)}, bf16[2,2,128,128]{3,2,1,0:T(8,128)(2,1)S(1)}, u32[]{:S(2)}, u32[]{:S(2)}) collective-permute-start(bf16[2,2,128,128]{3,2,1,0:T(8,128)(2,1)S(1)} %get-tuple-element.82), channel_id=1, source_target_pairs={{0,2},{1,3},{2,0},{3,1},{4,6},{5,7},{6,4},{7,5},{8,10},{9,11},{10,... | collective-permute-start | bytes 393224 | tf_op jit(solution)/shard_map/ppermute | solution.py:34
  (18 other events, 262.9 us)

commit v2 on v1

v2 whole, which is shorter than its diff:
```python
import math

import jax
import jax.numpy as jnp
from jax import lax
from jax.experimental import pallas as pl
from jax.experimental.pallas import tpu as pltpu
from jax.sharding import PartitionSpec as P

HD = 128
QT = 4
SEL = 3
W = 3
GROUP = 2
CORES = 2
SLOTS = 4
FIRST = 2
NEG = -1e30
AXES = ("tm", "head")


def params(limit=32):
    return pltpu.CompilerParams(vmem_limit_bytes=limit * 2**20)


def moved(block, to):
    frames, heads = lax.axis_size("tm"), lax.axis_size("head")
    route = []
    for t in range(frames):
        for h in range(heads):
            t2, h2 = to(t, h)
            if 0 <= t2 < frames:
                route.append((t * heads + h, t2 * heads + h2))
    return lax.ppermute(block, AXES, route)


def to_slot(block, slot):
    return moved(block, lambda t, h: (t ^ (slot // 2), h ^ (slot % 2 * CORES)))


def to_core(block):
    return moved(block, lambda t, h: (t, h ^ 1))


def to_group(block, step):
    return moved(block, lambda t, h: (t + step * GROUP, h))


def place():
    t, h = lax.axis_index("tm"), lax.axis_index("head")
    return t // GROUP, t % GROUP, h // CORES, h % CORES


def where_am_i():
    t, h = lax.axis_index("tm"), lax.axis_index("head")
    return jnp.stack([t, h]).astype(jnp.int32)


def columns(me, ref, per_chip, slot):
    x, y = me[0] % GROUP, me[1] // CORES
    tiles = ref.shape[1] // (HD * per_chip * GROUP)
    chip = (x ^ (slot // 2)) * tiles + (y ^ (slot % 2))
    return lambda head: pl.ds(pl.multiple_of((chip * per_chip + head) * HD, HD), HD)


def pack_kernel(plan, per_chip, used, me, *refs):
    outs = refs[used:]
    for slot in range(SLOTS):
        at = columns(me, refs[0], per_chip, slot)
        for n, (first, head) in enumerate(plan):
            outs[slot][n, 0] = refs[first][:, at(head)]
            outs[slot][n, 1] = refs[first + 1][:, at(head)]


def pack(me, arrays, plan, per_chip, after=()):
    rows = arrays[0].shape[0]
    shape = jax.ShapeDtypeStruct((len(plan), 2, rows, HD), arrays[0].dtype)
    vmem = pl.BlockSpec(memory_space=pltpu.VMEM)
    used = len(arrays) + len(after)
    return pl.pallas_call(
        lambda *refs: pack_kernel(plan, per_chip, used, *refs),
        out_shape=[shape] * SLOTS,
        in_specs=[pl.BlockSpec(memory_space=pltpu.SMEM)]
        + [vmem] * len(arrays)
        + [pl.BlockSpec(memory_space=pl.ANY)] * len(after),
        out_specs=[vmem] * SLOTS,
        compiler_params=params(),
    )(me, *arrays, *after)


def unpack_kernel(places, per_chip, me, *refs):
    a_ref, b_ref = refs[-2:]
    for slot in range(SLOTS):
        at = columns(me, a_ref, per_chip, slot)
        for head, (group, n) in enumerate(places):
            ref = refs[group * SLOTS + slot]
            a_ref[:, at(head)] = ref[n, 0]
            b_ref[:, at(head)] = ref[n, 1]


def unpack(me, groups, places, per_chip, width):
    flat = [p for group in groups for p in group]
    rows = flat[0].shape[2]
    vmem = pl.BlockSpec(memory_space=pltpu.VMEM)
    return pl.pallas_call(
        lambda *refs: unpack_kernel(places, per_chip, *refs),
        out_shape=[jax.ShapeDtypeStruct((rows, width), flat[0].dtype)] * 2,
        in_specs=[pl.BlockSpec(memory_space=pltpu.SMEM)] + [vmem] * len(flat),
        out_specs=[vmem] * 2,
        compiler_params=params(),
    )(me, *flat)


def dot(a, b, dims):
    return lax.dot_general(a, b, (dims, ((), ())), preferred_element_type=jnp.float32)


def attend_kernel(me, tp, win, *refs):
    kv_refs = refs[:4]
    qg_refs = refs[4:8]
    aq_refs = refs[8:12]
    own_f, halo_f, sent_b = refs[12:15]
    kv, ksel, vsel, acc = refs[15:]
    group, x = me[0] // GROUP, me[0] % GROUP
    y, core = me[1] // CORES, me[1] % CORES
    scale = 1.0 / math.sqrt(HD)
    c2 = scale * math.log2(math.e)
    for part in range(4):
        for s in range(SLOTS):
            kv[part * SLOTS + s] = kv_refs[part][s]
    acc[...] = jnp.zeros_like(acc)
    for j in range(SLOTS):
        q = qg_refs[j][0]
        g = qg_refs[j][1]
        xq = x ^ (j // 2)
        tile = (y ^ (j % 2)) * CORES + core
        frame = group * GROUP + xq
        limit = win[frame]
        slots = []
        biases = []
        for lag in range(W):
            rest = xq - lag
            plane = jnp.where(rest < 0, 1, 0)
            dx = (rest & 1) ^ x
            live = (lag <= frame) & (lag < limit)
            biases.append(jnp.where(live, 0.0, NEG))
            for i in range(SEL):
                t = tp[lag, tile, i]
                dc = (t % CORES) ^ core
                dy = (t // CORES) ^ y
                slot = plane * 8 + dc * 4 + dx * 2 + dy
                at = (lag * SEL + i) * HD
                ksel[j, at : at + HD] = kv[slot, 0]
                vsel[j, at : at + HD] = kv[slot, 1]
                slots.append(slot)
        span = SEL * HD
        k_all, v_all = ksel[j], vsel[j]
        s = dot(q, k_all, ((1,), (1,))) * c2
        s = jnp.concatenate(
            [s[:, lag * span : (lag + 1) * span] + biases[lag] for lag in range(W)], 1
        )
        top = jnp.max(s, -1, keepdims=True)
        e = jnp.exp2(s - top)
        prob = e * (1.0 / jnp.sum(e, -1, keepdims=True))
        prob_b = prob.astype(jnp.bfloat16)
        out = dot(prob_b, v_all, ((1,), (0,)))
        delta = jnp.sum(g.astype(jnp.float32) * out, -1, keepdims=True)
        dprob = dot(g, v_all, ((1,), (1,)))
        ds = (prob * (dprob - delta)).astype(jnp.bfloat16)
        aq_refs[j][0] = out.astype(jnp.bfloat16)
        aq_refs[j][1] = (dot(ds, k_all, ((1,), (0,))) * scale).astype(jnp.bfloat16)
        dk = dot(q, ds, ((0,), (0,)))
        dv = dot(g, prob_b, ((0,), (0,)))
        for i, slot in enumerate(slots):
            acc[slot, 0] += dk[:, i * HD : (i + 1) * HD]
            acc[slot, 1] += dv[:, i * HD : (i + 1) * HD]
    for part, (ref, to) in enumerate(((own_f, 0), (sent_b, 0), (halo_f, 0), (sent_b, SLOTS))):
        for s in range(SLOTS):
            ref[to + s, 0] = (acc[part * SLOTS + s, 0].T * scale).astype(ref.dtype)
            ref[to + s, 1] = acc[part * SLOTS + s, 1].T.astype(ref.dtype)


def attend(me, tp, win, own, other, halo, halo_other, qg, qg_at):
    nh, rows = own.shape[1], own.shape[3]
    smem = pl.BlockSpec(memory_space=pltpu.SMEM)
    kv_spec = pl.BlockSpec((SLOTS, None, 2, rows, HD), lambda h: (0, h, 0, 0, 0))
    both_spec = pl.BlockSpec((2 * SLOTS, None, 2, rows, HD), lambda h: (0, h, 0, 0, 0))
    qg_spec = pl.BlockSpec((None, 2, rows, HD), lambda h: (h + qg_at, 0, 0, 0))
    aq_spec = pl.BlockSpec((None, 2, rows, HD), lambda h: (h, 0, 0, 0))
    bf, f32 = jnp.bfloat16, jnp.float32
    count = W * SEL * rows
    outs = pl.pallas_call(
        attend_kernel,
        grid=(nh,),
        out_shape=[jax.ShapeDtypeStruct((nh, 2, rows, HD), bf)] * 4
        + [
            jax.ShapeDtypeStruct((SLOTS, nh, 2, rows, HD), f32),
            jax.ShapeDtypeStruct((SLOTS, nh, 2, rows, HD), f32),
            jax.ShapeDtypeStruct((2 * SLOTS, nh, 2, rows, HD), bf),
        ],
        in_specs=[smem] * 3 + [kv_spec] * 4 + [qg_spec] * 4,
        out_specs=[aq_spec] * 4 + [kv_spec] * 2 + [both_spec],
        scratch_shapes=[
            pltpu.VMEM((4 * SLOTS, 2, rows, HD), bf),
            pltpu.VMEM((SLOTS, count, HD), bf),
            pltpu.VMEM((SLOTS, count, HD), bf),
            pltpu.VMEM((4 * SLOTS, 2, HD, rows), f32),
        ],
        compiler_params=params(),
        cost_estimate=pl.CostEstimate(flops=1, bytes_accessed=1, transcendentals=0),
    )(me, tp, win, own, other, halo, halo_other, *qg)
    return outs[:4], outs[4:]


def exchange(pieces):
    return [pieces[0]] + [to_slot(pieces[s], s) for s in range(1, SLOTS)]


def shards(query, keys, values, grad_out, tile_pattern, window):
    width = query.shape[1]
    per_chip = width // HD // (GROUP * (lax.axis_size("head") // CORES))
    na = min(FIRST, per_chip - 1)
    nb = per_chip - na
    me = where_am_i()
    f32, bf = jnp.float32, jnp.bfloat16
    heads = range(per_chip)

    def summed(own_f, mine, later):
        return [
            (own_f[s] + mine[s].astype(f32) + later[s].astype(f32)).astype(bf)
            for s in range(SLOTS)
        ]

    def backward(halo_f, sent_b):
        mine = to_core(sent_b)
        back = (halo_f + mine[SLOTS:].astype(f32)).astype(bf)
        return mine, back, to_group(back, -1)

    kv_a = exchange(pack(me, [keys, values], [(0, h) for h in heads[:na]], per_chip))
    own_a = jnp.stack(kv_a)
    halo_a = to_group(own_a, 1)
    other_a = to_core(own_a)
    mixed = exchange(
        pack(
            me,
            [query, grad_out, keys, values],
            [(0, h) for h in heads[:na]] + [(2, h) for h in heads[na:]],
            per_chip,
            after=kv_a[1:],
        )
    )
    mixed, halo_a = lax.optimization_barrier((mixed, halo_a))
    own_b = jnp.stack([p[na:] for p in mixed])
    halo_b = to_group(own_b, 1)
    other_b = to_core(own_b)
    qg_b = exchange(
        pack(me, [query, grad_out], [(0, h) for h in heads[na:]], per_chip, after=mixed[1:])
    )
    halo_other_a = to_core(halo_a)
    aq_a, (own_fa, halo_fa, sent_a) = attend(
        me, tile_pattern, window, own_a, other_a, halo_a, halo_other_a, mixed, 0
    )
    sent_a, qg_b, halo_b = lax.optimization_barrier((sent_a, qg_b, halo_b))
    mine_a, back_a, later_a = backward(halo_fa, sent_a)
    got_aq_a = exchange(aq_a)
    halo_other_b = to_core(halo_b)
    qg_b, back_a = lax.optimization_barrier((qg_b, back_a))
    aq_b, (own_fb, halo_fb, sent_b) = attend(
        me, tile_pattern, window, own_b, other_b, halo_b, halo_other_b, qg_b, 0
    )
    sent_b, later_a, got_aq_a = lax.optimization_barrier((sent_b, later_a, got_aq_a))
    mine_b, _, later_b = backward(halo_fb, sent_b)
    total_a = summed(own_fa, mine_a, later_a)
    got_mixed = exchange([jnp.concatenate([aq_b[s], total_a[s]]) for s in range(SLOTS)])
    attended, grad_query = unpack(
        me,
        [got_aq_a, got_mixed],
        [(0, n) for n in range(na)] + [(1, n) for n in range(nb)],
        per_chip,
        width,
    )
    got_b = exchange(summed(own_fb, mine_b, later_b))
    grad_keys, grad_values = unpack(
        me,
        [got_mixed, got_b],
        [(0, nb + n) for n in range(na)] + [(1, n) for n in range(nb)],
        per_chip,
        width,
    )
    return (attended, grad_query, grad_keys, grad_values)


def solution(mesh):
    placed = P(AXES, None)
    return jax.shard_map(
        shards,
        mesh=mesh,
        in_specs=(placed,) * 4 + (P(), P()),
        out_specs=(placed,) * 4,
        check_vma=False,
    )
```

time: 168 us -> 119 us (0.71)
  waiting for transfers between devices: 85.6 us -> 47.8 us
  starting transfers between devices: 45.7 us -> 33.7 us
    ppermute x36 -> x28, waiting for transfers between devices: 85.6 us -> 47.8 us  [moved(): return lax.ppermute(block, AXES, route)]
    ppermute x36 -> x28, starting transfers between devices: 45.7 us -> 33.7 us  [moved(): return lax.ppermute(block, AXES, route)]
    pallas_call x4 -> x5, Pallas kernels: 5.28 us -> 5.82 us  [the longest x2 3.67 us: unpack(): pl.pallas_call(lambda *refs: unpack_kernel(places, per_chip, *refs), out_...]
  transfers between devices with their start and end apart: 36 -> 28, of which waited for: 17 -> 12; matrix products, arithmetic and copies ran while one was open for 1% -> 1% of each run, Pallas kernels for 18% -> 25%
where the time goes in v2:
time: 119 us
  waiting for transfers between devices  47.8 us (40%)
  starting transfers between devices  33.7 us (28%)
  Pallas kernels  32.6 us (27%)
  local copies, waits for them, and re-layouts  2.33 us (2%)
  other arithmetic  1.3 us (1%)
    ppermute x28, waiting for transfers between devices, moved(): return lax.ppermute(block, AXES, route)  47.8 us
    ppermute x28, starting transfers between devices, moved(): return lax.ppermute(block, AXES, route)  33.7 us
    pallas_call x2, Pallas kernels, attend(): pl.pallas_call(attend_kernel, grid=(nh,), out_shape=[jax.ShapeDtypeStruct...  26.7 us
    pallas_call x2, Pallas kernels, unpack(): pl.pallas_call(lambda *refs: unpack_kernel(places, per_chip, *refs), out_...  3.67 us
  transfers between devices with their start and end apart: 28, of which 12 were waited for; matrix products, arithmetic and copies ran while one was open for 1% of the time, Pallas kernels for 25%

profile of v2, /device:TPU:0, one launch (start us, length us, event | category | flops | bytes accessed | tf_op | source)
XLA Modules:
  0.0 118.7 jit_solution(4409687353408338406)
XLA Ops:
  3.6 3.0 %collective-permute-start = (bf16[2,2,128,128]{3,2,1,0:T(8,128)(2,1)S(1)}, bf16[2,2,128,128]{3,2,1,0:T(8,128)(2,1)S(1)}, u32[]{:S(2)}, u32[]{:S(2)}) collective-permute-start(bf16[2,2,128,128]{3,2,1,0:T(8,128)(2,1)S(1)} %get-tuple-element.55), channel_id=1, source_target_pairs={{0,2},{1,3},{2,0},{3,1},{4,6},{5,7},{6,4},{7,5},{8,10},{9,11},{10,... | collective-permute-start | bytes 393224 | tf_op jit(solution)/shard_map/ppermute | solution.py:34
  6.7 1.5 %collective-permute-start.1 = (bf16[2,2,128,128]{3,2,1,0:T(8,128)(2,1)S(1)}, bf16[2,2,128,128]{3,2,1,0:T(8,128)(2,1)S(1)}, u32[]{:S(2)}, u32[]{:S(2)}) collective-permute-start(bf16[2,2,128,128]{3,2,1,0:T(8,128)(2,1)S(1)} %get-tuple-element.56), channel_id=1, source_target_pairs={{0,4},{1,5},{2,6},{3,7},{4,0},{5,1},{6,2},{7,3},{8,12},{9,13},{10,... | collective-permute-start | bytes 393224 | tf_op jit(solution)/shard_map/ppermute | solution.py:34
  8.2 2.0 %collective-permute-done.refs_5_ = bf16[2,2,128,128]{3,2,1,0:T(8,128)(2,1)S(1)} collective-permute-done((bf16[2,2,128,128]{3,2,1,0:T(8,128)(2,1)S(1)}, bf16[2,2,128,128]{3,2,1,0:T(8,128)(2,1)S(1)}, u32[]{:S(2)}, u32[]{:S(2)}) %collective-permute-start) | collective-permute-done | bytes 131104 | tf_op jit(solution)/shard_map/ppermute | solution.py:34
  10.2 2.9 %collective-permute-done.1.refs_6_ = bf16[2,2,128,128]{3,2,1,0:T(8,128)(2,1)S(1)} collective-permute-done((bf16[2,2,128,128]{3,2,1,0:T(8,128)(2,1)S(1)}, bf16[2,2,128,128]{3,2,1,0:T(8,128)(2,1)S(1)}, u32[]{:S(2)}, u32[]{:S(2)}) %collective-permute-start.1) | collective-permute-done | bytes 131104 | tf_op jit(solution)/shard_map/ppermute | solution.py:34
  14.3 3.7 %collective-permute-start.6 = (bf16[4,2,2,128,128]{4,3,2,1,0:T(8,128)(2,1)S(1)}, bf16[4,2,2,128,128]{4,3,2,1,0:T(8,128)(2,1)S(1)}, u32[]{:S(2)}, u32[]{:S(2)}) collective-permute-start(bf16[4,2,2,128,128]{4,3,2,1,0:T(8,128)(2,1)S(1)} %pad_maximum_fusion.1.refs_0_), channel_id=1, source_target_pairs={{0,8},{1,9},{2,10},{3,11},{4,12},{5,13},{6,14},{7,15},{8,16},{9,17... | collective-permute-start | bytes 1572872 | tf_op jit(solution)/shard_map/ppermute | solution.py:34
  18.8 1.6 %collective-permute-start.3 = (bf16[5,2,128,128]{3,2,1,0:T(8,128)(2,1)S(1)}, bf16[5,2,128,128]{3,2,1,0:T(8,128)(2,1)S(1)}, u32[]{:S(2)}, u32[]{:S(2)}) collective-permute-start(bf16[5,2,128,128]{3,2,1,0:T(8,128)(2,1)S(1)} %get-tuple-element.59), channel_id=1, source_target_pairs={{0,2},{1,3},{2,0},{3,1},{4,6},{5,7},{6,4},{7,5},{8,10},{9,11},{10,... | collective-permute-start | bytes 983048 | tf_op jit(solution)/shard_map/ppermute | solution.py:34
  20.4 1.5 %collective-permute-start.4 = (bf16[5,2,128,128]{3,2,1,0:T(8,128)(2,1)S(1)}, bf16[5,2,128,128]{3,2,1,0:T(8,128)(2,1)S(1)}, u32[]{:S(2)}, u32[]{:S(2)}) collective-permute-start(bf16[5,2,128,128]{3,2,1,0:T(8,128)(2,1)S(1)} %get-tuple-element.60), channel_id=1, source_target_pairs={{0,4},{1,5},{2,6},{3,7},{4,0},{5,1},{6,2},{7,3},{8,12},{9,13},{10,... | collective-permute-start | bytes 983048 | tf_op jit(solution)/shard_map/ppermute | solution.py:34
  22.4 6.3 %collective-permute-done.3.refs_5_.refs_3_ = bf16[5,2,128,128]{3,2,1,0:T(8,128)(2,1)S(1)} collective-permute-done((bf16[5,2,128,128]{3,2,1,0:T(8,128)(2,1)S(1)}, bf16[5,2,128,128]{3,2,1,0:T(8,128)(2,1)S(1)}, u32[]{:S(2)}, u32[]{:S(2)}) %collective-permute-start.3) | collective-permute-done | bytes 327712 | tf_op jit(solution)/shard_map/ppermute | solution.py:34
  28.6 2.4 %collective-permute-done.4.refs_6_.refs_4_ = bf16[5,2,128,128]{3,2,1,0:T(8,128)(2,1)S(1)} collective-permute-done((bf16[5,2,128,128]{3,2,1,0:T(8,128)(2,1)S(1)}, bf16[5,2,128,128]{3,2,1,0:T(8,128)(2,1)S(1)}, u32[]{:S(2)}, u32[]{:S(2)}) %collective-permute-start.4) | collective-permute-done | bytes 327712 | tf_op jit(solution)/shard_map/ppermute | solution.py:34
  31.0 4.4 %collective-permute-done.5.refs_7_.refs_5_ = bf16[5,2,128,128]{3,2,1,0:T(8,128)(2,1)S(1)} collective-permute-done((bf16[5,2,128,128]{3,2,1,0:T(8,128)(2,1)S(1)}, bf16[5,2,128,128]{3,2,1,0:T(8,128)(2,1)S(1)}, u32[]{:S(2)}, u32[]{:S(2)}) %collective-permute-start.5) | collective-permute-done | bytes 327712 | tf_op jit(solution)/shard_map/ppermute | solution.py:34
  35.6 3.5 %collective-permute-start.13 = (bf16[4,3,2,128,128]{4,3,2,1,0:T(8,128)(2,1)S(1)}, bf16[4,3,2,128,128]{4,3,2,1,0:T(8,128)(2,1)S(1)}, u32[]{:S(2)}, u32[]{:S(2)}) collective-permute-start(bf16[4,3,2,128,128]{4,3,2,1,0:T(8,128)(2,1)S(1)} %pad_maximum_fusion.refs_0_), channel_id=1, source_target_pairs={{0,8},{1,9},{2,10},{3,11},{4,12},{5,13},{6,14},{7,15},{8,16},{9,17... | collective-permute-start | bytes 2359304 | tf_op jit(solution)/shard_map/ppermute | solution.py:34
  41.4 1.5 %collective-permute-start.11 = (bf16[3,2,128,128]{3,2,1,0:T(8,128)(2,1)S(1)}, bf16[3,2,128,128]{3,2,1,0:T(8,128)(2,1)S(1)}, u32[]{:S(2)}, u32[]{:S(2)}) collective-permute-start(bf16[3,2,128,128]{3,2,1,0:T(8,128)(2,1)S(1)} %get-tuple-element.71), channel_id=1, source_target_pairs={{0,4},{1,5},{2,6},{3,7},{4,0},{5,1},{6,2},{7,3},{8,12},{9,13},{10,... | collective-permute-start | bytes 589832 | tf_op jit(solution)/shard_map/ppermute | solution.py:34
  44.0 10.8 %shard_map.95 = (bf16[2,2,128,128]{3,2,1,0:T(8,128)(2,1)S(1)}, bf16[2,2,128,128]{3,2,1,0:T(8,128)(2,1)S(1)}, bf16[2,2,128,128]{3,2,1,0:T(8,128)(2,1)S(1)}, bf16[...) custom-call(s32[2]{0:T(128)S(1)} %pad_add_fusion.refs_0_.me, ...), custom_call_target="tpu_custom_call" | custom-call | flops 1 | bytes 1 | tf_op jit(solution)/shard_map/pallas_call | solution.py:192
  55.5 2.1 %collective-permute-done.15 = bf16[8,2,2,128,128]{4,3,2,1,0:T(8,128)(2,1)S(1)} collective-permute-done((bf16[8,2,2,128,128]{4,3,2,1,0:T(8,128)(2,1)S(1)}, bf16[8,2,2,128,128]{4,3,2,1,0:T(8,128)(2,1)S(1)}, u32[]{:S(2)}, u32[]{:S(2)}) %collective-permute-start.15) | collective-permute-done | bytes 1048608 | tf_op jit(solution)/shard_map/ppermute | solution.py:34
  60.2 1.5 %collective-permute-start.18 = (bf16[2,2,128,128]{3,2,1,0:T(8,128)(2,1)S(1)}, bf16[2,2,128,128]{3,2,1,0:T(8,128)(2,1)S(1)}, u32[]{:S(2)}, u32[]{:S(2)}) collective-permute-start(bf16[2,2,128,128]{3,2,1,0:T(8,128)(2,1)S(1)} %get-tuple-element.87), channel_id=1, source_target_pairs={{0,4},{1,5},{2,6},{3,7},{4,0},{5,1},{6,2},{7,3},{8,12},{9,13},{10,... | collective-permute-start | bytes 393224 | tf_op jit(solution)/shard_map/ppermute | solution.py:34
  62.8 15.9 %shard_map.97 = (bf16[3,2,128,128]{3,2,1,0:T(8,128)(2,1)S(1)}, bf16[3,2,128,128]{3,2,1,0:T(8,128)(2,1)S(1)}, bf16[3,2,128,128]{3,2,1,0:T(8,128)(2,1)S(1)}, bf16[...) custom-call(s32[2]{0:T(128)S(1)} %pad_add_fusion.refs_0_.me, ...), custom_call_target="tpu_custom_call" | custom-call | flops 1 | bytes 1 | tf_op jit(solution)/shard_map/pallas_call | solution.py:192
  78.8 3.4 %collective-permute-done.23 = bf16[8,3,2,128,128]{4,3,2,1,0:T(8,128)(2,1)S(1)} collective-permute-done((bf16[8,3,2,128,128]{4,3,2,1,0:T(8,128)(2,1)S(1)}, bf16[8,3,2,128,128]{4,3,2,1,0:T(8,128)(2,1)S(1)}, u32[]{:S(2)}, u32[]{:S(2)}) %collective-permute-start.23) | collective-permute-done | bytes 1572896 | tf_op jit(solution)/shard_map/ppermute | solution.py:34
  85.0 1.6 %collective-permute-start.21 = (bf16[5,2,128,128]{3,2,1,0:T(8,128)(2,1)S(1)}, bf16[5,2,128,128]{3,2,1,0:T(8,128)(2,1)S(1)}, u32[]{:S(2)}, u32[]{:S(2)}) collective-permute-start(bf16[5,2,128,128]{3,2,1,0:T(8,128)(2,1)S(1)} %pad_maximum_fusion.4), channel_id=1, source_target_pairs={{0,4},{1,5},{2,6},{3,7},{4,0},{5,1},{6,2},{7,3},{8,12},{9,13},{10,... | collective-permute-start | bytes 983048 | tf_op jit(solution)/shard_map/ppermute | solution.py:34
  87.8 17.1 %collective-permute-done.24 = bf16[4,3,2,128,128]{4,3,2,1,0:T(8,128)(2,1)S(1)} collective-permute-done((bf16[4,3,2,128,128]{4,3,2,1,0:T(8,128)(2,1)S(1)}, bf16[4,3,2,128,128]{4,3,2,1,0:T(8,128)(2,1)S(1)}, u32[]{:S(2)}, u32[]{:S(2)}) %collective-permute-start.24) | collective-permute-done | bytes 786464 | tf_op jit(solution)/shard_map/ppermute | solution.py:34
  105.2 1.9 %collective-permute-start.27 = (bf16[3,2,128,128]{3,2,1,0:T(8,128)(2,1)S(1)}, bf16[3,2,128,128]{3,2,1,0:T(8,128)(2,1)S(1)}, u32[]{:S(2)}, u32[]{:S(2)}) collective-permute-start(bf16[3,2,128,128]{3,2,1,0:T(8,128)(2,1)S(1)} %get-tuple-element.106), channel_id=1, source_target_pairs={{0,6},{1,7},{2,4},{3,5},{4,2},{5,3},{6,0},{7,1},{8,14},{9,15},{10,... | collective-permute-start | bytes 589832 | tf_op jit(solution)/shard_map/ppermute | solution.py:34
  108.8 1.8 %shard_map.98 = (bf16[128,2560]{1,0:T(8,128)(2,1)}, bf16[128,2560]{1,0:T(8,128)(2,1)}) custom-call(s32[2]{0:T(128)S(1)} %pad_add_fusion.refs_0_.me, bf16[2,2,128,128]{3,2,1,0:T(8,128)(2,1)S(1)} %get-tuple-element.89.refs_1_, bf16[2,2,128,128]{3,2,1,0:T(8,128)(2,1)S(1)} %collective-permute-done.17.refs_2_, ...), custom_call_target="tpu_custom_call" | custom-call | tf_op jit(solution)/shard_map/pallas_call | solution.py:105
  110.7 3.4 %collective-permute-done.27.refs_8_ = bf16[3,2,128,128]{3,2,1,0:T(8,128)(2,1)S(1)} collective-permute-done((bf16[3,2,128,128]{3,2,1,0:T(8,128)(2,1)S(1)}, bf16[3,2,128,128]{3,2,1,0:T(8,128)(2,1)S(1)}, u32[]{:S(2)}, u32[]{:S(2)}) %collective-permute-start.27) | collective-permute-done | bytes 196640 | tf_op jit(solution)/shard_map/ppermute | solution.py:34
  114.0 2.2 %collective-permute-done.26.refs_7_ = bf16[3,2,128,128]{3,2,1,0:T(8,128)(2,1)S(1)} collective-permute-done((bf16[3,2,128,128]{3,2,1,0:T(8,128)(2,1)S(1)}, bf16[3,2,128,128]{3,2,1,0:T(8,128)(2,1)S(1)}, u32[]{:S(2)}, u32[]{:S(2)}) %collective-permute-start.26) | collective-permute-done | bytes 196640 | tf_op jit(solution)/shard_map/ppermute | solution.py:34
  116.8 1.8 %shard_map.99 = (bf16[128,2560]{1,0:T(8,128)(2,1)}, bf16[128,2560]{1,0:T(8,128)(2,1)}) custom-call(s32[2]{0:T(128)S(1)} %pad_add_fusion.refs_0_.me, bf16[5,2,128,128]{3,2,1,0:T(8,128)(2,1)S(1)} %pad_maximum_fusion.2.refs_5_.refs_1_, bf16[5,2,128,128]{3,2,1,0:T(8,128)(2,1)S(1)} %collective-permute-done.20.refs_6_.refs_2_, ...), custom_call_target="tpu_custom_call" | custom-call | tf_op jit(solution)/shard_map/pallas_call | solution.py:105
  (64 shorter events, 20.1 us)
Async XLA Ops:
  3.6 6.5 %collective-permute-start = (bf16[2,2,128,128]{3,2,1,0:T(8,128)(2,1)S(1)}, bf16[2,2,128,128]{3,2,1,0:T(8,128)(2,1)S(1)}, u32[]{:S(2)}, u32[]{:S(2)}) collective-permute-start(bf16[2,2,128,128]{3,2,1,0:T(8,128)(2,1)S(1)} %get-tuple-element.55), channel_id=1, source_target_pairs={{0,2},{1,3},{2,0},{3,1},{4,6},{5,7},{6,4},{7,5},{8,10},{9,11},{10,... | collective-permute-start | bytes 393224 | tf_op jit(solution)/shard_map/ppermute | solution.py:34
  6.7 6.4 %collective-permute-start.1 = (bf16[2,2,128,128]{3,2,1,0:T(8,128)(2,1)S(1)}, bf16[2,2,128,128]{3,2,1,0:T(8,128)(2,1)S(1)}, u32[]{:S(2)}, u32[]{:S(2)}) collective-permute-start(bf16[2,2,128,128]{3,2,1,0:T(8,128)(2,1)S(1)} %get-tuple-element.56), channel_id=1, source_target_pairs={{0,4},{1,5},{2,6},{3,7},{4,0},{5,1},{6,2},{7,3},{8,12},{9,13},{10,... | collective-permute-start | bytes 393224 | tf_op jit(solution)/shard_map/ppermute | solution.py:34
  8.2 6.1 %collective-permute-start.2 = (bf16[2,2,128,128]{3,2,1,0:T(8,128)(2,1)S(1)}, bf16[2,2,128,128]{3,2,1,0:T(8,128)(2,1)S(1)}, u32[]{:S(2)}, u32[]{:S(2)}) collective-permute-start(bf16[2,2,128,128]{3,2,1,0:T(8,128)(2,1)S(1)} %get-tuple-element.57), channel_id=1, source_target_pairs={{0,6},{1,7},{2,4},{3,5},{4,2},{5,3},{6,0},{7,1},{8,14},{9,15},{10,... | collective-permute-start | bytes 393224 | tf_op jit(solution)/shard_map/ppermute | solution.py:34
  14.3 21.1 %collective-permute-start.6 = (bf16[4,2,2,128,128]{4,3,2,1,0:T(8,128)(2,1)S(1)}, bf16[4,2,2,128,128]{4,3,2,1,0:T(8,128)(2,1)S(1)}, u32[]{:S(2)}, u32[]{:S(2)}) collective-permute-start(bf16[4,2,2,128,128]{4,3,2,1,0:T(8,128)(2,1)S(1)} %pad_maximum_fusion.1.refs_0_), channel_id=1, source_target_pairs={{0,8},{1,9},{2,10},{3,11},{4,12},{5,13},{6,14},{7,15},{8,16},{9,17... | collective-permute-start | bytes 1572872 | tf_op jit(solution)/shard_map/ppermute | solution.py:34
  18.8 9.8 %collective-permute-start.3 = (bf16[5,2,128,128]{3,2,1,0:T(8,128)(2,1)S(1)}, bf16[5,2,128,128]{3,2,1,0:T(8,128)(2,1)S(1)}, u32[]{:S(2)}, u32[]{:S(2)}) collective-permute-start(bf16[5,2,128,128]{3,2,1,0:T(8,128)(2,1)S(1)} %get-tuple-element.59), channel_id=1, source_target_pairs={{0,2},{1,3},{2,0},{3,1},{4,6},{5,7},{6,4},{7,5},{8,10},{9,11},{10,... | collective-permute-start | bytes 983048 | tf_op jit(solution)/shard_map/ppermute | solution.py:34
  20.4 10.6 %collective-permute-start.4 = (bf16[5,2,128,128]{3,2,1,0:T(8,128)(2,1)S(1)}, bf16[5,2,128,128]{3,2,1,0:T(8,128)(2,1)S(1)}, u32[]{:S(2)}, u32[]{:S(2)}) collective-permute-start(bf16[5,2,128,128]{3,2,1,0:T(8,128)(2,1)S(1)} %get-tuple-element.60), channel_id=1, source_target_pairs={{0,4},{1,5},{2,6},{3,7},{4,0},{5,1},{6,2},{7,3},{8,12},{9,13},{10,... | collective-permute-start | bytes 983048 | tf_op jit(solution)/shard_map/ppermute | solution.py:34
  21.9 13.5 %collective-permute-start.5 = (bf16[5,2,128,128]{3,2,1,0:T(8,128)(2,1)S(1)}, bf16[5,2,128,128]{3,2,1,0:T(8,128)(2,1)S(1)}, u32[]{:S(2)}, u32[]{:S(2)}) collective-permute-start(bf16[5,2,128,128]{3,2,1,0:T(8,128)(2,1)S(1)} %get-tuple-element.61), channel_id=1, source_target_pairs={{0,6},{1,7},{2,4},{3,5},{4,2},{5,3},{6,0},{7,1},{8,14},{9,15},{10,... | collective-permute-start | bytes 983048 | tf_op jit(solution)/shard_map/ppermute | solution.py:34
  35.6 19.2 %collective-permute-start.13 = (bf16[4,3,2,128,128]{4,3,2,1,0:T(8,128)(2,1)S(1)}, bf16[4,3,2,128,128]{4,3,2,1,0:T(8,128)(2,1)S(1)}, u32[]{:S(2)}, u32[]{:S(2)}) collective-permute-start(bf16[4,3,2,128,128]{4,3,2,1,0:T(8,128)(2,1)S(1)} %pad_maximum_fusion.refs_0_), channel_id=1, source_target_pairs={{0,8},{1,9},{2,10},{3,11},{4,12},{5,13},{6,14},{7,15},{8,16},{9,17... | collective-permute-start | bytes 2359304 | tf_op jit(solution)/shard_map/ppermute | solution.py:34
  40.4 14.4 %collective-permute-start.10 = (bf16[3,2,128,128]{3,2,1,0:T(8,128)(2,1)S(1)}, bf16[3,2,128,128]{3,2,1,0:T(8,128)(2,1)S(1)}, u32[]{:S(2)}, u32[]{:S(2)}) collective-permute-start(bf16[3,2,128,128]{3,2,1,0:T(8,128)(2,1)S(1)} %get-tuple-element.70), channel_id=1, source_target_pairs={{0,2},{1,3},{2,0},{3,1},{4,6},{5,7},{6,4},{7,5},{8,10},{9,11},{10,... | collective-permute-start | bytes 589832 | tf_op jit(solution)/shard_map/ppermute | solution.py:34
  41.4 13.5 %collective-permute-start.11 = (bf16[3,2,128,128]{3,2,1,0:T(8,128)(2,1)S(1)}, bf16[3,2,128,128]{3,2,1,0:T(8,128)(2,1)S(1)}, u32[]{:S(2)}, u32[]{:S(2)}) collective-permute-start(bf16[3,2,128,128]{3,2,1,0:T(8,128)(2,1)S(1)} %get-tuple-element.71), channel_id=1, source_target_pairs={{0,4},{1,5},{2,6},{3,7},{4,0},{5,1},{6,2},{7,3},{8,12},{9,13},{10,... | collective-permute-start | bytes 589832 | tf_op jit(solution)/shard_map/ppermute | solution.py:34
  42.9 12.0 %collective-permute-start.12 = (bf16[3,2,128,128]{3,2,1,0:T(8,128)(2,1)S(1)}, bf16[3,2,128,128]{3,2,1,0:T(8,128)(2,1)S(1)}, u32[]{:S(2)}, u32[]{:S(2)}) collective-permute-start(bf16[3,2,128,128]{3,2,1,0:T(8,128)(2,1)S(1)} %get-tuple-element.72), channel_id=1, source_target_pairs={{0,6},{1,7},{2,4},{3,5},{4,2},{5,3},{6,0},{7,1},{8,14},{9,15},{10,... | collective-permute-start | bytes 589832 | tf_op jit(solution)/shard_map/ppermute | solution.py:34
  55.0 6.7 %collective-permute-start.7 = (bf16[4,3,2,128,128]{4,3,2,1,0:T(8,128)(2,1)S(1)}, bf16[4,3,2,128,128]{4,3,2,1,0:T(8,128)(2,1)S(1)}, u32[]{:S(2)}, u32[]{:S(2)}) collective-permute-start(bf16[4,3,2,128,128]{4,3,2,1,0:T(8,128)(2,1)S(1)} %pad_maximum_fusion.refs_0_), channel_id=1, source_target_pairs={{0,1},{1,0},{2,3},{3,2},{4,5},{5,4},{6,7},{7,6},{8,9},{9,8},{10,11... | collective-permute-start | bytes 2359304 | tf_op jit(solution)/shard_map/ppermute | solution.py:34
  55.5 7.3 %collective-permute-start.14 = (bf16[4,3,2,128,128]{4,3,2,1,0:T(8,128)(2,1)S(1)}, bf16[4,3,2,128,128]{4,3,2,1,0:T(8,128)(2,1)S(1)}, u32[]{:S(2)}, u32[]{:S(2)}) collective-permute-start(bf16[4,3,2,128,128]{4,3,2,1,0:T(8,128)(2,1)S(1)} %collective-permute-done.13.refs_2_), channel_id=1, source_target_pairs={{0,1},{1,0},{2,3},{3,2},{4,5},{5,4},{6,7},{7,6},{8,9},{9,8},{10,11... | collective-permute-start | bytes 2359304 | tf_op jit(solution)/shard_map/ppermute | solution.py:34
  57.8 21.0 %collective-permute-start.16 = (bf16[4,2,2,128,128]{4,3,2,1,0:T(8,128)(2,1)S(1)}, bf16[4,2,2,128,128]{4,3,2,1,0:T(8,128)(2,1)S(1)}, u32[]{:S(2)}, u32[]{:S(2)}) collective-permute-start(bf16[4,2,2,128,128]{4,3,2,1,0:T(8,128)(2,1)S(1)} %add_convert_fusion.1), channel_id=1, source_target_pairs={{8,0},{9,1},{10,2},{11,3},{12,4},{13,5},{14,6},{15,7},{16,8},{17,9... | collective-permute-start | bytes 1572872 | tf_op jit(solution)/shard_map/ppermute | solution.py:34
  59.2 19.5 %collective-permute-start.17 = (bf16[2,2,128,128]{3,2,1,0:T(8,128)(2,1)S(1)}, bf16[2,2,128,128]{3,2,1,0:T(8,128)(2,1)S(1)}, u32[]{:S(2)}, u32[]{:S(2)}) collective-permute-start(bf16[2,2,128,128]{3,2,1,0:T(8,128)(2,1)S(1)} %get-tuple-element.86), channel_id=1, source_target_pairs={{0,2},{1,3},{2,0},{3,1},{4,6},{5,7},{6,4},{7,5},{8,10},{9,11},{10,... | collective-permute-start | bytes 393224 | tf_op jit(solution)/shard_map/ppermute | solution.py:34
  60.2 18.6 %collective-permute-start.18 = (bf16[2,2,128,128]{3,2,1,0:T(8,128)(2,1)S(1)}, bf16[2,2,128,128]{3,2,1,0:T(8,128)(2,1)S(1)}, u32[]{:S(2)}, u32[]{:S(2)}) collective-permute-start(bf16[2,2,128,128]{3,2,1,0:T(8,128)(2,1)S(1)} %get-tuple-element.87), channel_id=1, source_target_pairs={{0,4},{1,5},{2,6},{3,7},{4,0},{5,1},{6,2},{7,3},{8,12},{9,13},{10,... | collective-permute-start | bytes 393224 | tf_op jit(solution)/shard_map/ppermute | solution.py:34
  61.7 17.1 %collective-permute-start.19 = (bf16[2,2,128,128]{3,2,1,0:T(8,128)(2,1)S(1)}, bf16[2,2,128,128]{3,2,1,0:T(8,128)(2,1)S(1)}, u32[]{:S(2)}, u32[]{:S(2)}) collective-permute-start(bf16[2,2,128,128]{3,2,1,0:T(8,128)(2,1)S(1)} %get-tuple-element.88), channel_id=1, source_target_pairs={{0,6},{1,7},{2,4},{3,5},{4,2},{5,3},{6,0},{7,1},{8,14},{9,15},{10,... | collective-permute-start | bytes 393224 | tf_op jit(solution)/shard_map/ppermute | solution.py:34
  82.5 22.4 %collective-permute-start.24 = (bf16[4,3,2,128,128]{4,3,2,1,0:T(8,128)(2,1)S(1)}, bf16[4,3,2,128,128]{4,3,2,1,0:T(8,128)(2,1)S(1)}, u32[]{:S(2)}, u32[]{:S(2)}) collective-permute-start(bf16[4,3,2,128,128]{4,3,2,1,0:T(8,128)(2,1)S(1)} %add_convert_fusion), channel_id=1, source_target_pairs={{8,0},{9,1},{10,2},{11,3},{12,4},{13,5},{14,6},{15,7},{16,8},{17,9... | collective-permute-start | bytes 2359304 | tf_op jit(solution)/shard_map/ppermute | solution.py:34
  84.1 23.5 %collective-permute-start.20 = (bf16[5,2,128,128]{3,2,1,0:T(8,128)(2,1)S(1)}, bf16[5,2,128,128]{3,2,1,0:T(8,128)(2,1)S(1)}, u32[]{:S(2)}, u32[]{:S(2)}) collective-permute-start(bf16[5,2,128,128]{3,2,1,0:T(8,128)(2,1)S(1)} %pad_maximum_fusion.3), channel_id=1, source_target_pairs={{0,2},{1,3},{2,0},{3,1},{4,6},{5,7},{6,4},{7,5},{8,10},{9,11},{10,... | collective-permute-start | bytes 983048 | tf_op jit(solution)/shard_map/ppermute | solution.py:34
  85.0 23.8 %collective-permute-start.21 = (bf16[5,2,128,128]{3,2,1,0:T(8,128)(2,1)S(1)}, bf16[5,2,128,128]{3,2,1,0:T(8,128)(2,1)S(1)}, u32[]{:S(2)}, u32[]{:S(2)}) collective-permute-start(bf16[5,2,128,128]{3,2,1,0:T(8,128)(2,1)S(1)} %pad_maximum_fusion.4), channel_id=1, source_target_pairs={{0,4},{1,5},{2,6},{3,7},{4,0},{5,1},{6,2},{7,3},{8,12},{9,13},{10,... | collective-permute-start | bytes 983048 | tf_op jit(solution)/shard_map/ppermute | solution.py:34
  86.6 22.2 %collective-permute-start.22 = (bf16[5,2,128,128]{3,2,1,0:T(8,128)(2,1)S(1)}, bf16[5,2,128,128]{3,2,1,0:T(8,128)(2,1)S(1)}, u32[]{:S(2)}, u32[]{:S(2)}) collective-permute-start(bf16[5,2,128,128]{3,2,1,0:T(8,128)(2,1)S(1)} %pad_maximum_fusion.5), channel_id=1, source_target_pairs={{0,6},{1,7},{2,4},{3,5},{4,2},{5,3},{6,0},{7,1},{8,14},{9,15},{10,... | collective-permute-start | bytes 983048 | tf_op jit(solution)/shard_map/ppermute | solution.py:34
  105.2 8.8 %collective-permute-start.27 = (bf16[3,2,128,128]{3,2,1,0:T(8,128)(2,1)S(1)}, bf16[3,2,128,128]{3,2,1,0:T(8,128)(2,1)S(1)}, u32[]{:S(2)}, u32[]{:S(2)}) collective-permute-start(bf16[3,2,128,128]{3,2,1,0:T(8,128)(2,1)S(1)} %get-tuple-element.106), channel_id=1, source_target_pairs={{0,6},{1,7},{2,4},{3,5},{4,2},{5,3},{6,0},{7,1},{8,14},{9,15},{10,... | collective-permute-start | bytes 589832 | tf_op jit(solution)/shard_map/ppermute | solution.py:34
  107.1 9.2 %collective-permute-start.26 = (bf16[3,2,128,128]{3,2,1,0:T(8,128)(2,1)S(1)}, bf16[3,2,128,128]{3,2,1,0:T(8,128)(2,1)S(1)}, u32[]{:S(2)}, u32[]{:S(2)}) collective-permute-start(bf16[3,2,128,128]{3,2,1,0:T(8,128)(2,1)S(1)} %get-tuple-element.107), channel_id=1, source_target_pairs={{0,4},{1,5},{2,6},{3,7},{4,0},{5,1},{6,2},{7,3},{8,12},{9,13},{10,... | collective-permute-start | bytes 589832 | tf_op jit(solution)/shard_map/ppermute | solution.py:34
  107.6 9.2 %collective-permute-start.25 = (bf16[3,2,128,128]{3,2,1,0:T(8,128)(2,1)S(1)}, bf16[3,2,128,128]{3,2,1,0:T(8,128)(2,1)S(1)}, u32[]{:S(2)}, u32[]{:S(2)}) collective-permute-start(bf16[3,2,128,128]{3,2,1,0:T(8,128)(2,1)S(1)} %get-tuple-element.108), channel_id=1, source_target_pairs={{0,2},{1,3},{2,0},{3,1},{4,6},{5,7},{6,4},{7,5},{8,10},{9,11},{10,... | collective-permute-start | bytes 589832 | tf_op jit(solution)/shard_map/ppermute | solution.py:34
  (10 other events, 68.7 us)

commit v3 on v2

--- a/solution.py
+++ b/solution.py
@@ -29,8 +29,7 @@
     for t in range(frames):
         for h in range(heads):
             t2, h2 = to(t, h)
-            if 0 <= t2 < frames:
-                route.append((t * heads + h, t2 * heads + h2))
+            route.append((t * heads + h, t2 % frames * heads + h2))
     return lax.ppermute(block, AXES, route)
 
 
@@ -120,64 +119,105 @@
     qg_refs = refs[4:8]
     aq_refs = refs[8:12]
     own_f, halo_f, sent_b = refs[12:15]
-    kv, ksel, vsel, acc = refs[15:]
+    kv, qg, aq, scaled, ksel, vsel, probs, dscores = refs[15:]
     group, x = me[0] // GROUP, me[0] % GROUP
     y, core = me[1] // CORES, me[1] % CORES
+    bf, f32 = jnp.bfloat16, jnp.float32
     scale = 1.0 / math.sqrt(HD)
     c2 = scale * math.log2(math.e)
+    span = SEL * HD
     for part in range(4):
         for s in range(SLOTS):
-            kv[part * SLOTS + s] = kv_refs[part][s]
-    acc[...] = jnp.zeros_like(acc)
+            place = (2 - part // 2 * 2) + (x ^ (s // 2))
+            kv[place * QT + part % 2 * 2 + s % 2] = kv_refs[part][s]
+    for s in range(SLOTS):
+        qg[(x ^ (s // 2)) * 2 + s % 2] = qg_refs[s][...]
+
+    def bias_of(frame, lag):
+        return jnp.where((lag <= frame) & (lag < win[frame]), 0.0, NEG)
+
+    biases = {}
+    cols = {}
+    for a in range(GROUP):
+        for d in range(2):
+            j = a * 2 + d
+            tile = (y ^ d) * CORES + core
+            biases[j] = [bias_of(group * GROUP + a, lag) for lag in range(W)]
+            for lag in range(W):
+                base = (GROUP + a - lag) * QT
+                left = QT * (QT - 1) // 2
+                for i in range(SEL):
+                    t = tp[lag, tile, i]
+                    left = left - t
+                    col = ((t % CORES) ^ core) * 2 + ((t // CORES) ^ y)
+                    cols[j, lag, i] = col
+                    at = (lag * SEL + i) * HD
+                    ksel[j, at : at + HD] = kv[base + col, 0]
+                    vsel[j, at : at + HD] = kv[base + col, 1]
+                cols[j, lag, SEL] = ((left % CORES) ^ core) * 2 + ((left // CORES) ^ y)
+
+    def score(j):
+        s = dot(qg[j, 0], ksel[j], ((1,), (1,)))
+        return jnp.concatenate(
+            [s[:, lag * span : (lag + 1) * span] + biases[j][lag] for lag in range(W)], 1
+        )
+
+    def soft(s):
+        top = jnp.max(s, -1, keepdims=True)
+        e = jnp.exp2((s - top) * c2)
+        return e, 1.0 / jnp.sum(e, -1, keepdims=True)
+
+    def spread(ref, j, block):
+        a, d = j // 2, j % 2
+        for lag in range(W):
+            place = GROUP + a - lag
+            row = d * HD + (a * 2 * HD if 0 < place < 3 else 0)
+            for i in range(SEL):
+                at = (lag * SEL + i) * HD
+                ref[place * QT + cols[j, lag, i], row : row + HD] = block[:, at : at + HD]
+            ref[place * QT + cols[j, lag, SEL], row : row + HD] = jnp.zeros((HD, HD), bf)
+
+    def rest_of(j, e, inv, dprob):
+        gf = qg[j, 1].astype(f32)
+        e_b = e.astype(bf)
+        out = dot(e_b, vsel[j], ((1,), (0,))) * inv
+        delta = jnp.sum(gf * out, -1, keepdims=True)
+        spread(probs, j, e_b)
+        ds = (e * (dprob - delta)).astype(bf)
+        spread(dscores, j, ds)
+        aq[j, 0] = out.astype(bf)
+        aq[j, 1] = (dot(ds, ksel[j], ((1,), (0,))) * (inv * scale)).astype(bf)
+        scaled[0, j * HD : (j + 1) * HD] = (qg[j, 0].astype(f32) * inv).astype(bf)
+        scaled[1, j * HD : (j + 1) * HD] = (gf * inv).astype(bf)
+
+    def grads(place):
+        low, rows = {0: (0, 2 * HD), 1: (0, 4 * HD), 2: (0, 4 * HD), 3: (2 * HD, 2 * HD)}[place]
+        to = ((place % 2) ^ x) * 2
+        for n, ref in enumerate((dscores, probs)):
+            right = jnp.concatenate([ref[place * QT + c, :rows] for c in range(QT)], 1)
+            got = dot(scaled[n, low : low + rows], right, ((0,), (0,)))
+            for c in range(QT):
+                block = got[:, c * HD : (c + 1) * HD].T
+                block = block * scale if n == 0 else block
+                if c < 2:
+                    (own_f if place >= GROUP else halo_f)[to + c, n] = block
+                else:
+                    first = 0 if place >= GROUP else SLOTS
+                    sent_b[first + to + c - 2, n] = block.astype(bf)
+
+    s = score(0)
     for j in range(SLOTS):
-        q = qg_refs[j][0]
-        g = qg_refs[j][1]
-        xq = x ^ (j // 2)
-        tile = (y ^ (j % 2)) * CORES + core
-        frame = group * GROUP + xq
-        limit = win[frame]
-        slots = []
-        biases = []
-        for lag in range(W):
-            rest = xq - lag
-            plane = jnp.where(rest < 0, 1, 0)
-            dx = (rest & 1) ^ x
-            live = (lag <= frame) & (lag < limit)
-            biases.append(jnp.where(live, 0.0, NEG))
-            for i in range(SEL):
-                t = tp[lag, tile, i]
-                dc = (t % CORES) ^ core
-                dy = (t // CORES) ^ y
-                slot = plane * 8 + dc * 4 + dx * 2 + dy
-                at = (lag * SEL + i) * HD
-                ksel[j, at : at + HD] = kv[slot, 0]
-                vsel[j, at : at + HD] = kv[slot, 1]
-                slots.append(slot)
-        span = SEL * HD
-        k_all, v_all = ksel[j], vsel[j]
-        s = dot(q, k_all, ((1,), (1,))) * c2
-        s = jnp.concatenate(
-            [s[:, lag * span : (lag + 1) * span] + biases[lag] for lag in range(W)], 1
-        )
-        top = jnp.max(s, -1, keepdims=True)
-        e = jnp.exp2(s - top)
-        prob = e * (1.0 / jnp.sum(e, -1, keepdims=True))
-        prob_b = prob.astype(jnp.bfloat16)
-        out = dot(prob_b, v_all, ((1,), (0,)))
-        delta = jnp.sum(g.astype(jnp.float32) * out, -1, keepdims=True)
-        dprob = dot(g, v_all, ((1,), (1,)))
-        ds = (prob * (dprob - delta)).astype(jnp.bfloat16)
-        aq_refs[j][0] = out.astype(jnp.bfloat16)
-        aq_refs[j][1] = (dot(ds, k_all, ((1,), (0,))) * scale).astype(jnp.bfloat16)
-        dk = dot(q, ds, ((0,), (0,)))
-        dv = dot(g, prob_b, ((0,), (0,)))
-        for i, slot in enumerate(slots):
-            acc[slot, 0] += dk[:, i * HD : (i + 1) * HD]
-            acc[slot, 1] += dv[:, i * HD : (i + 1) * HD]
-    for part, (ref, to) in enumerate(((own_f, 0), (sent_b, 0), (halo_f, 0), (sent_b, SLOTS))):
-        for s in range(SLOTS):
-            ref[to + s, 0] = (acc[part * SLOTS + s, 0].T * scale).astype(ref.dtype)
-            ref[to + s, 1] = acc[part * SLOTS + s, 1].T.astype(ref.dtype)
+        dprob = dot(qg[j, 1], vsel[j], ((1,), (1,)))
+        e, inv = soft(s)
+        if j + 1 < SLOTS:
+            s = score(j + 1)
+        rest_of(j, e, inv, dprob)
+        if j == 1:
+            grads(0)
+    for place in range(1, 4):
+        grads(place)
+    for s in range(SLOTS):
+        aq_refs[s][...] = aq[(x ^ (s // 2)) * 2 + s % 2]
 
 
 def attend(me, tp, win, own, other, halo, halo_other, qg, qg_at):
@@ -201,10 +241,14 @@
         in_specs=[smem] * 3 + [kv_spec] * 4 + [qg_spec] * 4,
         out_specs=[aq_spec] * 4 + [kv_spec] * 2 + [both_spec],
         scratch_shapes=[
-            pltpu.VMEM((4 * SLOTS, 2, rows, HD), bf),
+            pltpu.VMEM((2 * GROUP * QT, 2, rows, HD), bf),
+            pltpu.VMEM((SLOTS, 2, rows, HD), bf),
+            pltpu.VMEM((SLOTS, 2, rows, HD), bf),
+            pltpu.VMEM((2, SLOTS * rows, HD), bf),
             pltpu.VMEM((SLOTS, count, HD), bf),
             pltpu.VMEM((SLOTS, count, HD), bf),
-            pltpu.VMEM((4 * SLOTS, 2, HD, rows), f32),
+            pltpu.VMEM((2 * GROUP * QT, SLOTS * rows, HD), bf),
+            pltpu.VMEM((2 * GROUP * QT, SLOTS * rows, HD), bf),
         ],
         compiler_params=params(),
         cost_estimate=pl.CostEstimate(flops=1, bytes_accessed=1, transcendentals=0),

time: 119 us -> 109 us (0.916)
  Pallas kernels: 32.6 us -> 26.3 us
  starting transfers between devices: 33.7 us -> 29.3 us
    pallas_call x2, Pallas kernels: 26.7 us -> 20.5 us  [attend(): pl.pallas_call(attend_kernel, grid=(nh,), out_shape=[jax.ShapeDtypeStruct...]
    ppermute x28, starting transfers between devices: 33.7 us -> 29.3 us  [moved(): return lax.ppermute(block, AXES, route)]
  transfers between devices with their start and end apart: 28 -> 28, of which waited for: 12 -> 14; matrix products, arithmetic and copies ran while one was open for 1% -> 1% of each run, Pallas kernels for 25% -> 22%
where the time goes in v3:
time: 109 us
  waiting for transfers between devices  48.6 us (45%)
  starting transfers between devices  29.3 us (27%)
  Pallas kernels  26.3 us (24%)
  local copies, waits for them, and re-layouts  2.33 us (2%)
  other arithmetic  1.3 us (1%)
    ppermute x28, waiting for transfers between devices, moved(): return lax.ppermute(block, AXES, route)  48.6 us
    ppermute x28, starting transfers between devices, moved(): return lax.ppermute(block, AXES, route)  29.3 us
    pallas_call x2, Pallas kernels, attend(): pl.pallas_call(attend_kernel, grid=(nh,), out_shape=[jax.ShapeDtypeStruct...  20.5 us
    pallas_call x2, Pallas kernels, unpack(): pl.pallas_call(lambda *refs: unpack_kernel(places, per_chip, *refs), out_...  3.67 us
    unnamed x12, local copies, waits for them, and re-layouts  2.28 us
  transfers between devices with their start and end apart: 28, of which 14 were waited for; matrix products, arithmetic and copies ran while one was open for 1% of the time, Pallas kernels for 22%

profile of v3, /device:TPU:0, one launch (start us, length us, event | category | flops | bytes accessed | tf_op | source)
XLA Modules:
  0.0 108.7 jit_solution(8429078006402654600)
XLA Ops:
  3.6 3.0 %collective-permute-start = (bf16[2,2,128,128]{3,2,1,0:T(8,128)(2,1)S(1)}, bf16[2,2,128,128]{3,2,1,0:T(8,128)(2,1)S(1)}, u32[]{:S(2)}, u32[]{:S(2)}) collective-permute-start(bf16[2,2,128,128]{3,2,1,0:T(8,128)(2,1)S(1)} %get-tuple-element.55), channel_id=1, source_target_pairs={{0,2},{1,3},{2,0},{3,1},{4,6},{5,7},{6,4},{7,5},{8,10},{9,11},{10,... | collective-permute-start | bytes 393224 | tf_op jit(solution)/shard_map/ppermute | solution.py:33
  8.2 2.0 %collective-permute-done.refs_5_ = bf16[2,2,128,128]{3,2,1,0:T(8,128)(2,1)S(1)} collective-permute-done((bf16[2,2,128,128]{3,2,1,0:T(8,128)(2,1)S(1)}, bf16[2,2,128,128]{3,2,1,0:T(8,128)(2,1)S(1)}, u32[]{:S(2)}, u32[]{:S(2)}) %collective-permute-start) | collective-permute-done | bytes 131104 | tf_op jit(solution)/shard_map/ppermute | solution.py:33
  10.2 2.9 %collective-permute-done.1.refs_6_ = bf16[2,2,128,128]{3,2,1,0:T(8,128)(2,1)S(1)} collective-permute-done((bf16[2,2,128,128]{3,2,1,0:T(8,128)(2,1)S(1)}, bf16[2,2,128,128]{3,2,1,0:T(8,128)(2,1)S(1)}, u32[]{:S(2)}, u32[]{:S(2)}) %collective-permute-start.1) | collective-permute-done | bytes 131104 | tf_op jit(solution)/shard_map/ppermute | solution.py:33
  14.3 1.8 %collective-permute-start.6 = (bf16[4,2,2,128,128]{4,3,2,1,0:T(8,128)(2,1)S(1)}, bf16[4,2,2,128,128]{4,3,2,1,0:T(8,128)(2,1)S(1)}, u32[]{:S(2)}, u32[]{:S(2)}) collective-permute-start(bf16[4,2,2,128,128]{4,3,2,1,0:T(8,128)(2,1)S(1)} %pad_maximum_fusion.1.refs_0_), channel_id=1, source_target_pairs={{0,8},{1,9},{2,10},{3,11},{4,12},{5,13},{6,14},{7,15},{8,16},{9,17... | collective-permute-start | bytes 1572872 | tf_op jit(solution)/shard_map/ppermute | solution.py:33
  16.9 1.6 %collective-permute-start.3 = (bf16[5,2,128,128]{3,2,1,0:T(8,128)(2,1)S(1)}, bf16[5,2,128,128]{3,2,1,0:T(8,128)(2,1)S(1)}, u32[]{:S(2)}, u32[]{:S(2)}) collective-permute-start(bf16[5,2,128,128]{3,2,1,0:T(8,128)(2,1)S(1)} %get-tuple-element.59), channel_id=1, source_target_pairs={{0,2},{1,3},{2,0},{3,1},{4,6},{5,7},{6,4},{7,5},{8,10},{9,11},{10,... | collective-permute-start | bytes 983048 | tf_op jit(solution)/shard_map/ppermute | solution.py:33
  20.5 6.3 %collective-permute-done.3.refs_5_.refs_3_ = bf16[5,2,128,128]{3,2,1,0:T(8,128)(2,1)S(1)} collective-permute-done((bf16[5,2,128,128]{3,2,1,0:T(8,128)(2,1)S(1)}, bf16[5,2,128,128]{3,2,1,0:T(8,128)(2,1)S(1)}, u32[]{:S(2)}, u32[]{:S(2)}) %collective-permute-start.3) | collective-permute-done | bytes 327712 | tf_op jit(solution)/shard_map/ppermute | solution.py:33
  26.7 2.4 %collective-permute-done.4.refs_6_.refs_4_ = bf16[5,2,128,128]{3,2,1,0:T(8,128)(2,1)S(1)} collective-permute-done((bf16[5,2,128,128]{3,2,1,0:T(8,128)(2,1)S(1)}, bf16[5,2,128,128]{3,2,1,0:T(8,128)(2,1)S(1)}, u32[]{:S(2)}, u32[]{:S(2)}) %collective-permute-start.4) | collective-permute-done | bytes 327712 | tf_op jit(solution)/shard_map/ppermute | solution.py:33
  29.1 4.4 %collective-permute-done.5.refs_7_.refs_5_ = bf16[5,2,128,128]{3,2,1,0:T(8,128)(2,1)S(1)} collective-permute-done((bf16[5,2,128,128]{3,2,1,0:T(8,128)(2,1)S(1)}, bf16[5,2,128,128]{3,2,1,0:T(8,128)(2,1)S(1)}, u32[]{:S(2)}, u32[]{:S(2)}) %collective-permute-start.5) | collective-permute-done | bytes 327712 | tf_op jit(solution)/shard_map/ppermute | solution.py:33
  33.7 1.6 %collective-permute-start.13 = (bf16[4,3,2,128,128]{4,3,2,1,0:T(8,128)(2,1)S(1)}, bf16[4,3,2,128,128]{4,3,2,1,0:T(8,128)(2,1)S(1)}, u32[]{:S(2)}, u32[]{:S(2)}) collective-permute-start(bf16[4,3,2,128,128]{4,3,2,1,0:T(8,128)(2,1)S(1)} %pad_maximum_fusion.refs_0_), channel_id=1, source_target_pairs={{0,8},{1,9},{2,10},{3,11},{4,12},{5,13},{6,14},{7,15},{8,16},{9,17... | collective-permute-start | bytes 2359304 | tf_op jit(solution)/shard_map/ppermute | solution.py:33
  37.5 1.5 %collective-permute-start.11 = (bf16[3,2,128,128]{3,2,1,0:T(8,128)(2,1)S(1)}, bf16[3,2,128,128]{3,2,1,0:T(8,128)(2,1)S(1)}, u32[]{:S(2)}, u32[]{:S(2)}) collective-permute-start(bf16[3,2,128,128]{3,2,1,0:T(8,128)(2,1)S(1)} %get-tuple-element.71), channel_id=1, source_target_pairs={{0,4},{1,5},{2,6},{3,7},{4,0},{5,1},{6,2},{7,3},{8,12},{9,13},{10,... | collective-permute-start | bytes 589832 | tf_op jit(solution)/shard_map/ppermute | solution.py:33
  40.1 8.3 %shard_map.95 = (bf16[2,2,128,128]{3,2,1,0:T(8,128)(2,1)S(1)}, bf16[2,2,128,128]{3,2,1,0:T(8,128)(2,1)S(1)}, bf16[2,2,128,128]{3,2,1,0:T(8,128)(2,1)S(1)}, bf16[...) custom-call(s32[2]{0:T(128)S(1)} %pad_add_fusion.refs_0_.me, ...), custom_call_target="tpu_custom_call" | custom-call | flops 1 | bytes 1 | tf_op jit(solution)/shard_map/pallas_call | solution.py:232
  48.9 3.7 %collective-permute-done.13.refs_2_ = bf16[4,3,2,128,128]{4,3,2,1,0:T(8,128)(2,1)S(1)} collective-permute-done((bf16[4,3,2,128,128]{4,3,2,1,0:T(8,128)(2,1)S(1)}, bf16[4,3,2,128,128]{4,3,2,1,0:T(8,128)(2,1)S(1)}, u32[]{:S(2)}, u32[]{:S(2)}) %collective-permute-start.13) | collective-permute-done | bytes 786464 | tf_op jit(solution)/shard_map/ppermute | solution.py:33
  53.1 2.1 %collective-permute-done.15 = bf16[8,2,2,128,128]{4,3,2,1,0:T(8,128)(2,1)S(1)} collective-permute-done((bf16[8,2,2,128,128]{4,3,2,1,0:T(8,128)(2,1)S(1)}, bf16[8,2,2,128,128]{4,3,2,1,0:T(8,128)(2,1)S(1)}, u32[]{:S(2)}, u32[]{:S(2)}) %collective-permute-start.15) | collective-permute-done | bytes 1048608 | tf_op jit(solution)/shard_map/ppermute | solution.py:33
  57.7 2.0 %collective-permute-start.19 = (bf16[2,2,128,128]{3,2,1,0:T(8,128)(2,1)S(1)}, bf16[2,2,128,128]{3,2,1,0:T(8,128)(2,1)S(1)}, u32[]{:S(2)}, u32[]{:S(2)}) collective-permute-start(bf16[2,2,128,128]{3,2,1,0:T(8,128)(2,1)S(1)} %get-tuple-element.88), channel_id=1, source_target_pairs={{0,6},{1,7},{2,4},{3,5},{4,2},{5,3},{6,0},{7,1},{8,14},{9,15},{10,... | collective-permute-start | bytes 393224 | tf_op jit(solution)/shard_map/ppermute | solution.py:33
  59.7 12.1 %shard_map.97 = (bf16[3,2,128,128]{3,2,1,0:T(8,128)(2,1)S(1)}, bf16[3,2,128,128]{3,2,1,0:T(8,128)(2,1)S(1)}, bf16[3,2,128,128]{3,2,1,0:T(8,128)(2,1)S(1)}, bf16[...) custom-call(s32[2]{0:T(128)S(1)} %pad_add_fusion.refs_0_.me, ...), custom_call_target="tpu_custom_call" | custom-call | flops 1 | bytes 1 | tf_op jit(solution)/shard_map/pallas_call | solution.py:232
  72.0 3.4 %collective-permute-done.23 = bf16[8,3,2,128,128]{4,3,2,1,0:T(8,128)(2,1)S(1)} collective-permute-done((bf16[8,3,2,128,128]{4,3,2,1,0:T(8,128)(2,1)S(1)}, bf16[8,3,2,128,128]{4,3,2,1,0:T(8,128)(2,1)S(1)}, u32[]{:S(2)}, u32[]{:S(2)}) %collective-permute-start.23) | collective-permute-done | bytes 1572896 | tf_op jit(solution)/shard_map/ppermute | solution.py:33
  75.6 1.5 %collective-permute-start.24 = (bf16[4,3,2,128,128]{4,3,2,1,0:T(8,128)(2,1)S(1)}, bf16[4,3,2,128,128]{4,3,2,1,0:T(8,128)(2,1)S(1)}, u32[]{:S(2)}, u32[]{:S(2)}) collective-permute-start(bf16[4,3,2,128,128]{4,3,2,1,0:T(8,128)(2,1)S(1)} %add_convert_fusion), channel_id=1, source_target_pairs={{0,24},{1,25},{2,26},{3,27},{4,28},{5,29},{6,30},{7,31},{8,0},{9,1... | collective-permute-start | bytes 2359304 | tf_op jit(solution)/shard_map/ppermute | solution.py:33
  77.7 1.6 %collective-permute-start.21 = (bf16[5,2,128,128]{3,2,1,0:T(8,128)(2,1)S(1)}, bf16[5,2,128,128]{3,2,1,0:T(8,128)(2,1)S(1)}, u32[]{:S(2)}, u32[]{:S(2)}) collective-permute-start(bf16[5,2,128,128]{3,2,1,0:T(8,128)(2,1)S(1)} %pad_maximum_fusion.4), channel_id=1, source_target_pairs={{0,4},{1,5},{2,6},{3,7},{4,0},{5,1},{6,2},{7,3},{8,12},{9,13},{10,... | collective-permute-start | bytes 983048 | tf_op jit(solution)/shard_map/ppermute | solution.py:33
  79.4 1.8 %collective-permute-start.22 = (bf16[5,2,128,128]{3,2,1,0:T(8,128)(2,1)S(1)}, bf16[5,2,128,128]{3,2,1,0:T(8,128)(2,1)S(1)}, u32[]{:S(2)}, u32[]{:S(2)}) collective-permute-start(bf16[5,2,128,128]{3,2,1,0:T(8,128)(2,1)S(1)} %pad_maximum_fusion.5), channel_id=1, source_target_pairs={{0,6},{1,7},{2,4},{3,5},{4,2},{5,3},{6,0},{7,1},{8,14},{9,15},{10,... | collective-permute-start | bytes 983048 | tf_op jit(solution)/shard_map/ppermute | solution.py:33
  81.2 14.1 %collective-permute-done.24 = bf16[4,3,2,128,128]{4,3,2,1,0:T(8,128)(2,1)S(1)} collective-permute-done((bf16[4,3,2,128,128]{4,3,2,1,0:T(8,128)(2,1)S(1)}, bf16[4,3,2,128,128]{4,3,2,1,0:T(8,128)(2,1)S(1)}, u32[]{:S(2)}, u32[]{:S(2)}) %collective-permute-start.24) | collective-permute-done | bytes 786464 | tf_op jit(solution)/shard_map/ppermute | solution.py:33
  97.2 2.0 %collective-permute-start.25 = (bf16[3,2,128,128]{3,2,1,0:T(8,128)(2,1)S(1)}, bf16[3,2,128,128]{3,2,1,0:T(8,128)(2,1)S(1)}, u32[]{:S(2)}, u32[]{:S(2)}) collective-permute-start(bf16[3,2,128,128]{3,2,1,0:T(8,128)(2,1)S(1)} %get-tuple-element.108), channel_id=1, source_target_pairs={{0,2},{1,3},{2,0},{3,1},{4,6},{5,7},{6,4},{7,5},{8,10},{9,11},{10,... | collective-permute-start | bytes 589832 | tf_op jit(solution)/shard_map/ppermute | solution.py:33
  99.2 1.8 %shard_map.98 = (bf16[128,2560]{1,0:T(8,128)(2,1)}, bf16[128,2560]{1,0:T(8,128)(2,1)}) custom-call(s32[2]{0:T(128)S(1)} %pad_add_fusion.refs_0_.me, bf16[2,2,128,128]{3,2,1,0:T(8,128)(2,1)S(1)} %get-tuple-element.89.refs_1_, bf16[2,2,128,128]{3,2,1,0:T(8,128)(2,1)S(1)} %collective-permute-done.17.refs_2_, ...), custom_call_target="tpu_custom_call" | custom-call | tf_op jit(solution)/shard_map/pallas_call | solution.py:104
  101.0 3.4 %collective-permute-done.27.refs_8_ = bf16[3,2,128,128]{3,2,1,0:T(8,128)(2,1)S(1)} collective-permute-done((bf16[3,2,128,128]{3,2,1,0:T(8,128)(2,1)S(1)}, bf16[3,2,128,128]{3,2,1,0:T(8,128)(2,1)S(1)}, u32[]{:S(2)}, u32[]{:S(2)}) %collective-permute-start.27) | collective-permute-done | bytes 196640 | tf_op jit(solution)/shard_map/ppermute | solution.py:33
  106.9 1.8 %shard_map.99 = (bf16[128,2560]{1,0:T(8,128)(2,1)}, bf16[128,2560]{1,0:T(8,128)(2,1)}) custom-call(s32[2]{0:T(128)S(1)} %pad_add_fusion.refs_0_.me, bf16[5,2,128,128]{3,2,1,0:T(8,128)(2,1)S(1)} %pad_maximum_fusion.2.refs_5_.refs_1_, bf16[5,2,128,128]{3,2,1,0:T(8,128)(2,1)S(1)} %collective-permute-done.20.refs_6_.refs_2_, ...), custom_call_target="tpu_custom_call" | custom-call | tf_op jit(solution)/shard_map/pallas_call | solution.py:104
  (64 shorter events, 20.7 us)
Async XLA Ops:
  3.6 6.5 %collective-permute-start = (bf16[2,2,128,128]{3,2,1,0:T(8,128)(2,1)S(1)}, bf16[2,2,128,128]{3,2,1,0:T(8,128)(2,1)S(1)}, u32[]{:S(2)}, u32[]{:S(2)}) collective-permute-start(bf16[2,2,128,128]{3,2,1,0:T(8,128)(2,1)S(1)} %get-tuple-element.55), channel_id=1, source_target_pairs={{0,2},{1,3},{2,0},{3,1},{4,6},{5,7},{6,4},{7,5},{8,10},{9,11},{10,... | collective-permute-start | bytes 393224 | tf_op jit(solution)/shard_map/ppermute | solution.py:33
  6.7 6.4 %collective-permute-start.1 = (bf16[2,2,128,128]{3,2,1,0:T(8,128)(2,1)S(1)}, bf16[2,2,128,128]{3,2,1,0:T(8,128)(2,1)S(1)}, u32[]{:S(2)}, u32[]{:S(2)}) collective-permute-start(bf16[2,2,128,128]{3,2,1,0:T(8,128)(2,1)S(1)} %get-tuple-element.56), channel_id=1, source_target_pairs={{0,4},{1,5},{2,6},{3,7},{4,0},{5,1},{6,2},{7,3},{8,12},{9,13},{10,... | collective-permute-start | bytes 393224 | tf_op jit(solution)/shard_map/ppermute | solution.py:33
  8.2 6.1 %collective-permute-start.2 = (bf16[2,2,128,128]{3,2,1,0:T(8,128)(2,1)S(1)}, bf16[2,2,128,128]{3,2,1,0:T(8,128)(2,1)S(1)}, u32[]{:S(2)}, u32[]{:S(2)}) collective-permute-start(bf16[2,2,128,128]{3,2,1,0:T(8,128)(2,1)S(1)} %get-tuple-element.57), channel_id=1, source_target_pairs={{0,6},{1,7},{2,4},{3,5},{4,2},{5,3},{6,0},{7,1},{8,14},{9,15},{10,... | collective-permute-start | bytes 393224 | tf_op jit(solution)/shard_map/ppermute | solution.py:33
  14.3 19.2 %collective-permute-start.6 = (bf16[4,2,2,128,128]{4,3,2,1,0:T(8,128)(2,1)S(1)}, bf16[4,2,2,128,128]{4,3,2,1,0:T(8,128)(2,1)S(1)}, u32[]{:S(2)}, u32[]{:S(2)}) collective-permute-start(bf16[4,2,2,128,128]{4,3,2,1,0:T(8,128)(2,1)S(1)} %pad_maximum_fusion.1.refs_0_), channel_id=1, source_target_pairs={{0,8},{1,9},{2,10},{3,11},{4,12},{5,13},{6,14},{7,15},{8,16},{9,17... | collective-permute-start | bytes 1572872 | tf_op jit(solution)/shard_map/ppermute | solution.py:33
  16.9 9.8 %collective-permute-start.3 = (bf16[5,2,128,128]{3,2,1,0:T(8,128)(2,1)S(1)}, bf16[5,2,128,128]{3,2,1,0:T(8,128)(2,1)S(1)}, u32[]{:S(2)}, u32[]{:S(2)}) collective-permute-start(bf16[5,2,128,128]{3,2,1,0:T(8,128)(2,1)S(1)} %get-tuple-element.59), channel_id=1, source_target_pairs={{0,2},{1,3},{2,0},{3,1},{4,6},{5,7},{6,4},{7,5},{8,10},{9,11},{10,... | collective-permute-start | bytes 983048 | tf_op jit(solution)/shard_map/ppermute | solution.py:33
  18.5 10.6 %collective-permute-start.4 = (bf16[5,2,128,128]{3,2,1,0:T(8,128)(2,1)S(1)}, bf16[5,2,128,128]{3,2,1,0:T(8,128)(2,1)S(1)}, u32[]{:S(2)}, u32[]{:S(2)}) collective-permute-start(bf16[5,2,128,128]{3,2,1,0:T(8,128)(2,1)S(1)} %get-tuple-element.60), channel_id=1, source_target_pairs={{0,4},{1,5},{2,6},{3,7},{4,0},{5,1},{6,2},{7,3},{8,12},{9,13},{10,... | collective-permute-start | bytes 983048 | tf_op jit(solution)/shard_map/ppermute | solution.py:33
  20.0 13.5 %collective-permute-start.5 = (bf16[5,2,128,128]{3,2,1,0:T(8,128)(2,1)S(1)}, bf16[5,2,128,128]{3,2,1,0:T(8,128)(2,1)S(1)}, u32[]{:S(2)}, u32[]{:S(2)}) collective-permute-start(bf16[5,2,128,128]{3,2,1,0:T(8,128)(2,1)S(1)} %get-tuple-element.61), channel_id=1, source_target_pairs={{0,6},{1,7},{2,4},{3,5},{4,2},{5,3},{6,0},{7,1},{8,14},{9,15},{10,... | collective-permute-start | bytes 983048 | tf_op jit(solution)/shard_map/ppermute | solution.py:33
  33.7 18.8 %collective-permute-start.13 = (bf16[4,3,2,128,128]{4,3,2,1,0:T(8,128)(2,1)S(1)}, bf16[4,3,2,128,128]{4,3,2,1,0:T(8,128)(2,1)S(1)}, u32[]{:S(2)}, u32[]{:S(2)}) collective-permute-start(bf16[4,3,2,128,128]{4,3,2,1,0:T(8,128)(2,1)S(1)} %pad_maximum_fusion.refs_0_), channel_id=1, source_target_pairs={{0,8},{1,9},{2,10},{3,11},{4,12},{5,13},{6,14},{7,15},{8,16},{9,17... | collective-permute-start | bytes 2359304 | tf_op jit(solution)/shard_map/ppermute | solution.py:33
  36.6 11.9 %collective-permute-start.10 = (bf16[3,2,128,128]{3,2,1,0:T(8,128)(2,1)S(1)}, bf16[3,2,128,128]{3,2,1,0:T(8,128)(2,1)S(1)}, u32[]{:S(2)}, u32[]{:S(2)}) collective-permute-start(bf16[3,2,128,128]{3,2,1,0:T(8,128)(2,1)S(1)} %get-tuple-element.70), channel_id=1, source_target_pairs={{0,2},{1,3},{2,0},{3,1},{4,6},{5,7},{6,4},{7,5},{8,10},{9,11},{10,... | collective-permute-start | bytes 589832 | tf_op jit(solution)/shard_map/ppermute | solution.py:33
  37.5 11.0 %collective-permute-start.11 = (bf16[3,2,128,128]{3,2,1,0:T(8,128)(2,1)S(1)}, bf16[3,2,128,128]{3,2,1,0:T(8,128)(2,1)S(1)}, u32[]{:S(2)}, u32[]{:S(2)}) collective-permute-start(bf16[3,2,128,128]{3,2,1,0:T(8,128)(2,1)S(1)} %get-tuple-element.71), channel_id=1, source_target_pairs={{0,4},{1,5},{2,6},{3,7},{4,0},{5,1},{6,2},{7,3},{8,12},{9,13},{10,... | collective-permute-start | bytes 589832 | tf_op jit(solution)/shard_map/ppermute | solution.py:33
  39.0 9.9 %collective-permute-start.12 = (bf16[3,2,128,128]{3,2,1,0:T(8,128)(2,1)S(1)}, bf16[3,2,128,128]{3,2,1,0:T(8,128)(2,1)S(1)}, u32[]{:S(2)}, u32[]{:S(2)}) collective-permute-start(bf16[3,2,128,128]{3,2,1,0:T(8,128)(2,1)S(1)} %get-tuple-element.72), channel_id=1, source_target_pairs={{0,6},{1,7},{2,4},{3,5},{4,2},{5,3},{6,0},{7,1},{8,14},{9,15},{10,... | collective-permute-start | bytes 589832 | tf_op jit(solution)/shard_map/ppermute | solution.py:33
  52.5 5.2 %collective-permute-start.7 = (bf16[4,3,2,128,128]{4,3,2,1,0:T(8,128)(2,1)S(1)}, bf16[4,3,2,128,128]{4,3,2,1,0:T(8,128)(2,1)S(1)}, u32[]{:S(2)}, u32[]{:S(2)}) collective-permute-start(bf16[4,3,2,128,128]{4,3,2,1,0:T(8,128)(2,1)S(1)} %pad_maximum_fusion.refs_0_), channel_id=1, source_target_pairs={{0,1},{1,0},{2,3},{3,2},{4,5},{5,4},{6,7},{7,6},{8,9},{9,8},{10,11... | collective-permute-start | bytes 2359304 | tf_op jit(solution)/shard_map/ppermute | solution.py:33
  53.1 6.6 %collective-permute-start.14 = (bf16[4,3,2,128,128]{4,3,2,1,0:T(8,128)(2,1)S(1)}, bf16[4,3,2,128,128]{4,3,2,1,0:T(8,128)(2,1)S(1)}, u32[]{:S(2)}, u32[]{:S(2)}) collective-permute-start(bf16[4,3,2,128,128]{4,3,2,1,0:T(8,128)(2,1)S(1)} %collective-permute-done.13.refs_2_), channel_id=1, source_target_pairs={{0,1},{1,0},{2,3},{3,2},{4,5},{5,4},{6,7},{7,6},{8,9},{9,8},{10,11... | collective-permute-start | bytes 2359304 | tf_op jit(solution)/shard_map/ppermute | solution.py:33
  55.4 16.5 %collective-permute-start.16 = (bf16[4,2,2,128,128]{4,3,2,1,0:T(8,128)(2,1)S(1)}, bf16[4,2,2,128,128]{4,3,2,1,0:T(8,128)(2,1)S(1)}, u32[]{:S(2)}, u32[]{:S(2)}) collective-permute-start(bf16[4,2,2,128,128]{4,3,2,1,0:T(8,128)(2,1)S(1)} %add_convert_fusion.1), channel_id=1, source_target_pairs={{0,24},{1,25},{2,26},{3,27},{4,28},{5,29},{6,30},{7,31},{8,0},{9,1... | collective-permute-start | bytes 1572872 | tf_op jit(solution)/shard_map/ppermute | solution.py:33
  56.2 15.7 %collective-permute-start.17 = (bf16[2,2,128,128]{3,2,1,0:T(8,128)(2,1)S(1)}, bf16[2,2,128,128]{3,2,1,0:T(8,128)(2,1)S(1)}, u32[]{:S(2)}, u32[]{:S(2)}) collective-permute-start(bf16[2,2,128,128]{3,2,1,0:T(8,128)(2,1)S(1)} %get-tuple-element.86), channel_id=1, source_target_pairs={{0,2},{1,3},{2,0},{3,1},{4,6},{5,7},{6,4},{7,5},{8,10},{9,11},{10,... | collective-permute-start | bytes 393224 | tf_op jit(solution)/shard_map/ppermute | solution.py:33
  56.2 15.6 %collective-permute-start.18 = (bf16[2,2,128,128]{3,2,1,0:T(8,128)(2,1)S(1)}, bf16[2,2,128,128]{3,2,1,0:T(8,128)(2,1)S(1)}, u32[]{:S(2)}, u32[]{:S(2)}) collective-permute-start(bf16[2,2,128,128]{3,2,1,0:T(8,128)(2,1)S(1)} %get-tuple-element.87), channel_id=1, source_target_pairs={{0,4},{1,5},{2,6},{3,7},{4,0},{5,1},{6,2},{7,3},{8,12},{9,13},{10,... | collective-permute-start | bytes 393224 | tf_op jit(solution)/shard_map/ppermute | solution.py:33
  57.7 14.1 %collective-permute-start.19 = (bf16[2,2,128,128]{3,2,1,0:T(8,128)(2,1)S(1)}, bf16[2,2,128,128]{3,2,1,0:T(8,128)(2,1)S(1)}, u32[]{:S(2)}, u32[]{:S(2)}) collective-permute-start(bf16[2,2,128,128]{3,2,1,0:T(8,128)(2,1)S(1)} %get-tuple-element.88), channel_id=1, source_target_pairs={{0,6},{1,7},{2,4},{3,5},{4,2},{5,3},{6,0},{7,1},{8,14},{9,15},{10,... | collective-permute-start | bytes 393224 | tf_op jit(solution)/shard_map/ppermute | solution.py:33
  75.6 19.6 %collective-permute-start.24 = (bf16[4,3,2,128,128]{4,3,2,1,0:T(8,128)(2,1)S(1)}, bf16[4,3,2,128,128]{4,3,2,1,0:T(8,128)(2,1)S(1)}, u32[]{:S(2)}, u32[]{:S(2)}) collective-permute-start(bf16[4,3,2,128,128]{4,3,2,1,0:T(8,128)(2,1)S(1)} %add_convert_fusion), channel_id=1, source_target_pairs={{0,24},{1,25},{2,26},{3,27},{4,28},{5,29},{6,30},{7,31},{8,0},{9,1... | collective-permute-start | bytes 2359304 | tf_op jit(solution)/shard_map/ppermute | solution.py:33
  77.4 19.8 %collective-permute-start.20 = (bf16[5,2,128,128]{3,2,1,0:T(8,128)(2,1)S(1)}, bf16[5,2,128,128]{3,2,1,0:T(8,128)(2,1)S(1)}, u32[]{:S(2)}, u32[]{:S(2)}) collective-permute-start(bf16[5,2,128,128]{3,2,1,0:T(8,128)(2,1)S(1)} %pad_maximum_fusion.3), channel_id=1, source_target_pairs={{0,2},{1,3},{2,0},{3,1},{4,6},{5,7},{6,4},{7,5},{8,10},{9,11},{10,... | collective-permute-start | bytes 983048 | tf_op jit(solution)/shard_map/ppermute | solution.py:33
  77.7 21.5 %collective-permute-start.21 = (bf16[5,2,128,128]{3,2,1,0:T(8,128)(2,1)S(1)}, bf16[5,2,128,128]{3,2,1,0:T(8,128)(2,1)S(1)}, u32[]{:S(2)}, u32[]{:S(2)}) collective-permute-start(bf16[5,2,128,128]{3,2,1,0:T(8,128)(2,1)S(1)} %pad_maximum_fusion.4), channel_id=1, source_target_pairs={{0,4},{1,5},{2,6},{3,7},{4,0},{5,1},{6,2},{7,3},{8,12},{9,13},{10,... | collective-permute-start | bytes 983048 | tf_op jit(solution)/shard_map/ppermute | solution.py:33
  79.4 19.8 %collective-permute-start.22 = (bf16[5,2,128,128]{3,2,1,0:T(8,128)(2,1)S(1)}, bf16[5,2,128,128]{3,2,1,0:T(8,128)(2,1)S(1)}, u32[]{:S(2)}, u32[]{:S(2)}) collective-permute-start(bf16[5,2,128,128]{3,2,1,0:T(8,128)(2,1)S(1)} %pad_maximum_fusion.5), channel_id=1, source_target_pairs={{0,6},{1,7},{2,4},{3,5},{4,2},{5,3},{6,0},{7,1},{8,14},{9,15},{10,... | collective-permute-start | bytes 983048 | tf_op jit(solution)/shard_map/ppermute | solution.py:33
  95.6 8.8 %collective-permute-start.27 = (bf16[3,2,128,128]{3,2,1,0:T(8,128)(2,1)S(1)}, bf16[3,2,128,128]{3,2,1,0:T(8,128)(2,1)S(1)}, u32[]{:S(2)}, u32[]{:S(2)}) collective-permute-start(bf16[3,2,128,128]{3,2,1,0:T(8,128)(2,1)S(1)} %get-tuple-element.106), channel_id=1, source_target_pairs={{0,6},{1,7},{2,4},{3,5},{4,2},{5,3},{6,0},{7,1},{8,14},{9,15},{10,... | collective-permute-start | bytes 589832 | tf_op jit(solution)/shard_map/ppermute | solution.py:33
  96.7 8.8 %collective-permute-start.26 = (bf16[3,2,128,128]{3,2,1,0:T(8,128)(2,1)S(1)}, bf16[3,2,128,128]{3,2,1,0:T(8,128)(2,1)S(1)}, u32[]{:S(2)}, u32[]{:S(2)}) collective-permute-start(bf16[3,2,128,128]{3,2,1,0:T(8,128)(2,1)S(1)} %get-tuple-element.107), channel_id=1, source_target_pairs={{0,4},{1,5},{2,6},{3,7},{4,0},{5,1},{6,2},{7,3},{8,12},{9,13},{10,... | collective-permute-start | bytes 589832 | tf_op jit(solution)/shard_map/ppermute | solution.py:33
  97.2 9.7 %collective-permute-start.25 = (bf16[3,2,128,128]{3,2,1,0:T(8,128)(2,1)S(1)}, bf16[3,2,128,128]{3,2,1,0:T(8,128)(2,1)S(1)}, u32[]{:S(2)}, u32[]{:S(2)}) collective-permute-start(bf16[3,2,128,128]{3,2,1,0:T(8,128)(2,1)S(1)} %get-tuple-element.108), channel_id=1, source_target_pairs={{0,2},{1,3},{2,0},{3,1},{4,6},{5,7},{6,4},{7,5},{8,10},{9,11},{10,... | collective-permute-start | bytes 589832 | tf_op jit(solution)/shard_map/ppermute | solution.py:33
  (10 other events, 60.9 us)

commit v4 on v3

--- a/solution.py
+++ b/solution.py
@@ -220,9 +220,10 @@
         aq_refs[s][...] = aq[(x ^ (s // 2)) * 2 + s % 2]
 
 
-def attend(me, tp, win, own, other, halo, halo_other, qg, qg_at):
-    nh, rows = own.shape[1], own.shape[3]
+def attend(me, tp, win, own, other, halo, halo_other, qg, qg_at, kv_at, nh):
+    rows = own.shape[3]
     smem = pl.BlockSpec(memory_space=pltpu.SMEM)
+    in_spec = pl.BlockSpec((SLOTS, None, 2, rows, HD), lambda h: (0, h + kv_at, 0, 0, 0))
     kv_spec = pl.BlockSpec((SLOTS, None, 2, rows, HD), lambda h: (0, h, 0, 0, 0))
     both_spec = pl.BlockSpec((2 * SLOTS, None, 2, rows, HD), lambda h: (0, h, 0, 0, 0))
     qg_spec = pl.BlockSpec((None, 2, rows, HD), lambda h: (h + qg_at, 0, 0, 0))
@@ -238,7 +239,7 @@
             jax.ShapeDtypeStruct((SLOTS, nh, 2, rows, HD), f32),
             jax.ShapeDtypeStruct((2 * SLOTS, nh, 2, rows, HD), bf),
         ],
-        in_specs=[smem] * 3 + [kv_spec] * 4 + [qg_spec] * 4,
+        in_specs=[smem] * 3 + [in_spec] * 4 + [qg_spec] * 4,
         out_specs=[aq_spec] * 4 + [kv_spec] * 2 + [both_spec],
         scratch_shapes=[
             pltpu.VMEM((2 * GROUP * QT, 2, rows, HD), bf),
@@ -263,8 +264,9 @@
 def shards(query, keys, values, grad_out, tile_pattern, window):
     width = query.shape[1]
     per_chip = width // HD // (GROUP * (lax.axis_size("head") // CORES))
-    na = min(FIRST, per_chip - 1)
+    na = min(FIRST, per_chip - 2)
     nb = per_chip - na
+    nc = max(1, nb - na)
     me = where_am_i()
     f32, bf = jnp.float32, jnp.bfloat16
     heads = range(per_chip)
@@ -302,7 +304,7 @@
     )
     halo_other_a = to_core(halo_a)
     aq_a, (own_fa, halo_fa, sent_a) = attend(
-        me, tile_pattern, window, own_a, other_a, halo_a, halo_other_a, mixed, 0
+        me, tile_pattern, window, own_a, other_a, halo_a, halo_other_a, mixed, 0, 0, na
     )
     sent_a, qg_b, halo_b = lax.optimization_barrier((sent_a, qg_b, halo_b))
     mine_a, back_a, later_a = backward(halo_fa, sent_a)
@@ -310,12 +312,20 @@
     halo_other_b = to_core(halo_b)
     qg_b, back_a = lax.optimization_barrier((qg_b, back_a))
     aq_b, (own_fb, halo_fb, sent_b) = attend(
-        me, tile_pattern, window, own_b, other_b, halo_b, halo_other_b, qg_b, 0
+        me, tile_pattern, window, own_b, other_b, halo_b, halo_other_b, qg_b, 0, 0, nb - nc
     )
     sent_b, later_a, got_aq_a = lax.optimization_barrier((sent_b, later_a, got_aq_a))
-    mine_b, _, later_b = backward(halo_fb, sent_b)
+    mine_b, back_b, later_b = backward(halo_fb, sent_b)
+    qg_b, sent_b = lax.optimization_barrier((qg_b, sent_b))
+    aq_c, (own_fc, halo_fc, sent_c) = attend(
+        me, tile_pattern, window, own_b, other_b, halo_b, halo_other_b, qg_b, nb - nc, nb - nc, nc
+    )
+    sent_c, mine_b = lax.optimization_barrier((sent_c, mine_b))
+    mine_c, _, later_c = backward(halo_fc, sent_c)
     total_a = summed(own_fa, mine_a, later_a)
-    got_mixed = exchange([jnp.concatenate([aq_b[s], total_a[s]]) for s in range(SLOTS)])
+    got_mixed = exchange(
+        [jnp.concatenate([aq_b[s], aq_c[s], total_a[s]]) for s in range(SLOTS)]
+    )
     attended, grad_query = unpack(
         me,
         [got_aq_a, got_mixed],
@@ -324,10 +334,13 @@
         width,
     )
     got_b = exchange(summed(own_fb, mine_b, later_b))
+    got_c = exchange(summed(own_fc, mine_c, later_c))
     grad_keys, grad_values = unpack(
         me,
-        [got_mixed, got_b],
-        [(0, nb + n) for n in range(na)] + [(1, n) for n in range(nb)],
+        [got_mixed, got_b, got_c],
+        [(0, nb + n) for n in range(na)]
+        + [(1, n) for n in range(nb - nc)]
+        + [(2, n) for n in range(nc)],
         per_chip,
         width,
     )

time: 109 us -> 105 us (0.963)
  waiting for transfers between devices: 48.6 us -> 41.2 us
  starting transfers between devices: 29.3 us -> 32.8 us
    ppermute x28 -> x33, waiting for transfers between devices: 48.6 us -> 41.2 us  [moved(): return lax.ppermute(block, AXES, route)]
    ppermute x28 -> x33, starting transfers between devices: 29.3 us -> 32.8 us  [moved(): return lax.ppermute(block, AXES, route)]
    pallas_call x2 -> x3, Pallas kernels: 20.5 us -> 20.8 us  [attend(): pl.pallas_call(attend_kernel, grid=(nh,), out_shape=[jax.ShapeDtypeStruct...]
  transfers between devices with their start and end apart: 28 -> 33, of which waited for: 14 -> 17; matrix products, arithmetic and copies ran while one was open for 1% -> 1% of each run, Pallas kernels for 22% -> 23%
where the time goes in v4:
time: 105 us
  waiting for transfers between devices  41.2 us (39%)
  starting transfers between devices  32.8 us (31%)
  Pallas kernels  26.6 us (25%)
  local copies, waits for them, and re-layouts  2.26 us (2%)
  other arithmetic  1.2 us (1%)
    ppermute x33, waiting for transfers between devices, moved(): return lax.ppermute(block, AXES, route)  41.2 us
    ppermute x33, starting transfers between devices, moved(): return lax.ppermute(block, AXES, route)  32.8 us
    pallas_call x3, Pallas kernels, attend(): pl.pallas_call(attend_kernel, grid=(nh,), out_shape=[jax.ShapeDtypeStruct...  20.8 us
    pallas_call x2, Pallas kernels, unpack(): pl.pallas_call(lambda *refs: unpack_kernel(places, per_chip, *refs), out_...  3.67 us
    unnamed x12, local copies, waits for them, and re-layouts  2.19 us
    pallas_call x3, Pallas kernels, pack(): pl.pallas_call(lambda *refs: pack_kernel(plan, per_chip, used, *refs), ou...  2.15 us
  transfers between devices with their start and end apart: 33, of which 17 were waited for; matrix products, arithmetic and copies ran while one was open for 1% of the time, Pallas kernels for 23%

profile of v4, /device:TPU:0, one launch (start us, length us, event | category | flops | bytes accessed | tf_op | source)
XLA Modules:
  0.0 104.9 jit_solution(4772739886108887343)
XLA Ops:
  3.6 3.0 %collective-permute-start = (bf16[2,2,128,128]{3,2,1,0:T(8,128)(2,1)S(1)}, bf16[2,2,128,128]{3,2,1,0:T(8,128)(2,1)S(1)}, u32[]{:S(2)}, u32[]{:S(2)}) collective-permute-start(bf16[2,2,128,128]{3,2,1,0:T(8,128)(2,1)S(1)} %get-tuple-element.68), channel_id=1, source_target_pairs={{0,2},{1,3},{2,0},{3,1},{4,6},{5,7},{6,4},{7,5},{8,10},{9,11},{10,... | collective-permute-start | bytes 393224 | tf_op jit(solution)/shard_map/ppermute | solution.py:33
  8.1 2.0 %collective-permute-done.refs_5_ = bf16[2,2,128,128]{3,2,1,0:T(8,128)(2,1)S(1)} collective-permute-done((bf16[2,2,128,128]{3,2,1,0:T(8,128)(2,1)S(1)}, bf16[2,2,128,128]{3,2,1,0:T(8,128)(2,1)S(1)}, u32[]{:S(2)}, u32[]{:S(2)}) %collective-permute-start) | collective-permute-done | bytes 131104 | tf_op jit(solution)/shard_map/ppermute | solution.py:33
  10.1 2.9 %collective-permute-done.1.refs_6_ = bf16[2,2,128,128]{3,2,1,0:T(8,128)(2,1)S(1)} collective-permute-done((bf16[2,2,128,128]{3,2,1,0:T(8,128)(2,1)S(1)}, bf16[2,2,128,128]{3,2,1,0:T(8,128)(2,1)S(1)}, u32[]{:S(2)}, u32[]{:S(2)}) %collective-permute-start.1) | collective-permute-done | bytes 131104 | tf_op jit(solution)/shard_map/ppermute | solution.py:33
  14.2 1.8 %collective-permute-start.6 = (bf16[4,2,2,128,128]{4,3,2,1,0:T(8,128)(2,1)S(1)}, bf16[4,2,2,128,128]{4,3,2,1,0:T(8,128)(2,1)S(1)}, u32[]{:S(2)}, u32[]{:S(2)}) collective-permute-start(bf16[4,2,2,128,128]{4,3,2,1,0:T(8,128)(2,1)S(1)} %pad_maximum_fusion.1.refs_0_), channel_id=1, source_target_pairs={{0,8},{1,9},{2,10},{3,11},{4,12},{5,13},{6,14},{7,15},{8,16},{9,17... | collective-permute-start | bytes 1572872 | tf_op jit(solution)/shard_map/ppermute | solution.py:33
  16.8 1.6 %collective-permute-start.3 = (bf16[5,2,128,128]{3,2,1,0:T(8,128)(2,1)S(1)}, bf16[5,2,128,128]{3,2,1,0:T(8,128)(2,1)S(1)}, u32[]{:S(2)}, u32[]{:S(2)}) collective-permute-start(bf16[5,2,128,128]{3,2,1,0:T(8,128)(2,1)S(1)} %get-tuple-element.72), channel_id=1, source_target_pairs={{0,2},{1,3},{2,0},{3,1},{4,6},{5,7},{6,4},{7,5},{8,10},{9,11},{10,... | collective-permute-start | bytes 983048 | tf_op jit(solution)/shard_map/ppermute | solution.py:33
  20.4 6.3 %collective-permute-done.3.refs_5_.refs_3_ = bf16[5,2,128,128]{3,2,1,0:T(8,128)(2,1)S(1)} collective-permute-done((bf16[5,2,128,128]{3,2,1,0:T(8,128)(2,1)S(1)}, bf16[5,2,128,128]{3,2,1,0:T(8,128)(2,1)S(1)}, u32[]{:S(2)}, u32[]{:S(2)}) %collective-permute-start.3) | collective-permute-done | bytes 327712 | tf_op jit(solution)/shard_map/ppermute | solution.py:33
  26.6 2.4 %collective-permute-done.4.refs_6_.refs_4_ = bf16[5,2,128,128]{3,2,1,0:T(8,128)(2,1)S(1)} collective-permute-done((bf16[5,2,128,128]{3,2,1,0:T(8,128)(2,1)S(1)}, bf16[5,2,128,128]{3,2,1,0:T(8,128)(2,1)S(1)}, u32[]{:S(2)}, u32[]{:S(2)}) %collective-permute-start.4) | collective-permute-done | bytes 327712 | tf_op jit(solution)/shard_map/ppermute | solution.py:33
  29.0 4.4 %collective-permute-done.5.refs_7_.refs_5_ = bf16[5,2,128,128]{3,2,1,0:T(8,128)(2,1)S(1)} collective-permute-done((bf16[5,2,128,128]{3,2,1,0:T(8,128)(2,1)S(1)}, bf16[5,2,128,128]{3,2,1,0:T(8,128)(2,1)S(1)}, u32[]{:S(2)}, u32[]{:S(2)}) %collective-permute-start.5) | collective-permute-done | bytes 327712 | tf_op jit(solution)/shard_map/ppermute | solution.py:33
  33.6 1.6 %collective-permute-start.13 = (bf16[4,3,2,128,128]{4,3,2,1,0:T(8,128)(2,1)S(1)}, bf16[4,3,2,128,128]{4,3,2,1,0:T(8,128)(2,1)S(1)}, u32[]{:S(2)}, u32[]{:S(2)}) collective-permute-start(bf16[4,3,2,128,128]{4,3,2,1,0:T(8,128)(2,1)S(1)} %pad_maximum_fusion.refs_0_), channel_id=1, source_target_pairs={{0,8},{1,9},{2,10},{3,11},{4,12},{5,13},{6,14},{7,15},{8,16},{9,17... | collective-permute-start | bytes 2359304 | tf_op jit(solution)/shard_map/ppermute | solution.py:33
  37.4 1.5 %collective-permute-start.11 = (bf16[3,2,128,128]{3,2,1,0:T(8,128)(2,1)S(1)}, bf16[3,2,128,128]{3,2,1,0:T(8,128)(2,1)S(1)}, u32[]{:S(2)}, u32[]{:S(2)}) collective-permute-start(bf16[3,2,128,128]{3,2,1,0:T(8,128)(2,1)S(1)} %get-tuple-element.84), channel_id=1, source_target_pairs={{0,4},{1,5},{2,6},{3,7},{4,0},{5,1},{6,2},{7,3},{8,12},{9,13},{10,... | collective-permute-start | bytes 589832 | tf_op jit(solution)/shard_map/ppermute | solution.py:33
  40.0 8.3 %shard_map.95 = (bf16[2,2,128,128]{3,2,1,0:T(8,128)(2,1)S(1)}, bf16[2,2,128,128]{3,2,1,0:T(8,128)(2,1)S(1)}, bf16[2,2,128,128]{3,2,1,0:T(8,128)(2,1)S(1)}, bf16[...) custom-call(s32[2]{0:T(128)S(1)} %pad_add_fusion.refs_0_.me, ...), custom_call_target="tpu_custom_call" | custom-call | flops 1 | bytes 1 | tf_op jit(solution)/shard_map/pallas_call | solution.py:233
  48.7 3.7 %collective-permute-done.13.refs_2_ = bf16[4,3,2,128,128]{4,3,2,1,0:T(8,128)(2,1)S(1)} collective-permute-done((bf16[4,3,2,128,128]{4,3,2,1,0:T(8,128)(2,1)S(1)}, bf16[4,3,2,128,128]{4,3,2,1,0:T(8,128)(2,1)S(1)}, u32[]{:S(2)}, u32[]{:S(2)}) %collective-permute-start.13) | collective-permute-done | bytes 786464 | tf_op jit(solution)/shard_map/ppermute | solution.py:33
  52.9 2.1 %collective-permute-done.15 = bf16[8,2,2,128,128]{4,3,2,1,0:T(8,128)(2,1)S(1)} collective-permute-done((bf16[8,2,2,128,128]{4,3,2,1,0:T(8,128)(2,1)S(1)}, bf16[8,2,2,128,128]{4,3,2,1,0:T(8,128)(2,1)S(1)}, u32[]{:S(2)}, u32[]{:S(2)}) %collective-permute-start.15) | collective-permute-done | bytes 1048608 | tf_op jit(solution)/shard_map/ppermute | solution.py:33
  56.3 1.5 %collective-permute-start.18 = (bf16[2,2,128,128]{3,2,1,0:T(8,128)(2,1)S(1)}, bf16[2,2,128,128]{3,2,1,0:T(8,128)(2,1)S(1)}, u32[]{:S(2)}, u32[]{:S(2)}) collective-permute-start(bf16[2,2,128,128]{3,2,1,0:T(8,128)(2,1)S(1)} %get-tuple-element.100), channel_id=1, source_target_pairs={{0,4},{1,5},{2,6},{3,7},{4,0},{5,1},{6,2},{7,3},{8,12},{9,13},{10,... | collective-permute-start | bytes 393224 | tf_op jit(solution)/shard_map/ppermute | solution.py:33
  57.8 2.0 %collective-permute-start.19 = (bf16[2,2,128,128]{3,2,1,0:T(8,128)(2,1)S(1)}, bf16[2,2,128,128]{3,2,1,0:T(8,128)(2,1)S(1)}, u32[]{:S(2)}, u32[]{:S(2)}) collective-permute-start(bf16[2,2,128,128]{3,2,1,0:T(8,128)(2,1)S(1)} %get-tuple-element.101), channel_id=1, source_target_pairs={{0,6},{1,7},{2,4},{3,5},{4,2},{5,3},{6,0},{7,1},{8,14},{9,15},{10,... | collective-permute-start | bytes 393224 | tf_op jit(solution)/shard_map/ppermute | solution.py:33
  59.7 8.3 %shard_map.97 = (bf16[2,2,128,128]{3,2,1,0:T(8,128)(2,1)S(1)}, bf16[2,2,128,128]{3,2,1,0:T(8,128)(2,1)S(1)}, bf16[2,2,128,128]{3,2,1,0:T(8,128)(2,1)S(1)}, bf16[...) custom-call(s32[2]{0:T(128)S(1)} %pad_add_fusion.refs_0_.me, ...), custom_call_target="tpu_custom_call" | custom-call | flops 1 | bytes 1 | tf_op jit(solution)/shard_map/pallas_call | solution.py:233
  69.4 4.3 %shard_map.98 = (bf16[1,2,128,128]{3,2,1,0:T(8,128)(2,1)S(1)}, bf16[1,2,128,128]{3,2,1,0:T(8,128)(2,1)S(1)}, bf16[1,2,128,128]{3,2,1,0:T(8,128)(2,1)S(1)}, bf16[...) custom-call(s32[2]{0:T(128)S(1)} %pad_add_fusion.refs_0_.me, ...), custom_call_target="tpu_custom_call" | custom-call | flops 1 | bytes 1 | tf_op jit(solution)/shard_map/pallas_call | solution.py:233
  74.6 2.6 %collective-permute-start.24 = (bf16[4,2,2,128,128]{4,3,2,1,0:T(8,128)(2,1)S(1)}, bf16[4,2,2,128,128]{4,3,2,1,0:T(8,128)(2,1)S(1)}, u32[]{:S(2)}, u32[]{:S(2)}) collective-permute-start(bf16[4,2,2,128,128]{4,3,2,1,0:T(8,128)(2,1)S(1)} %add_convert_fusion), channel_id=1, source_target_pairs={{0,24},{1,25},{2,26},{3,27},{4,28},{5,29},{6,30},{7,31},{8,0},{9,1... | collective-permute-start | bytes 1572872 | tf_op jit(solution)/shard_map/ppermute | solution.py:33
  79.1 2.0 %collective-permute-start.20 = (bf16[5,2,128,128]{3,2,1,0:T(8,128)(2,1)S(1)}, bf16[5,2,128,128]{3,2,1,0:T(8,128)(2,1)S(1)}, u32[]{:S(2)}, u32[]{:S(2)}) collective-permute-start(bf16[5,2,128,128]{3,2,1,0:T(8,128)(2,1)S(1)} %pad_maximum_fusion.3), channel_id=1, source_target_pairs={{0,2},{1,3},{2,0},{3,1},{4,6},{5,7},{6,4},{7,5},{8,10},{9,11},{10,... | collective-permute-start | bytes 983048 | tf_op jit(solution)/shard_map/ppermute | solution.py:33
  81.2 8.3 %collective-permute-done.24 = bf16[4,2,2,128,128]{4,3,2,1,0:T(8,128)(2,1)S(1)} collective-permute-done((bf16[4,2,2,128,128]{4,3,2,1,0:T(8,128)(2,1)S(1)}, bf16[4,2,2,128,128]{4,3,2,1,0:T(8,128)(2,1)S(1)}, u32[]{:S(2)}, u32[]{:S(2)}) %collective-permute-start.24) | collective-permute-done | bytes 524320 | tf_op jit(solution)/shard_map/ppermute | solution.py:33
  91.4 2.9 %collective-permute-done.29 = bf16[4,1,2,128,128]{4,3,2,1,0:T(8,128)(2,1)S(1)} collective-permute-done((bf16[4,1,2,128,128]{4,3,2,1,0:T(8,128)(2,1)S(1)}, bf16[4,1,2,128,128]{4,3,2,1,0:T(8,128)(2,1)S(1)}, u32[]{:S(2)}, u32[]{:S(2)}) %collective-permute-start.29) | collective-permute-done | bytes 262176 | tf_op jit(solution)/shard_map/ppermute | solution.py:33
  96.0 2.0 %collective-permute-start.31 = (bf16[1,2,128,128]{3,2,1,0:T(8,128)(2,1)S(1)}, bf16[1,2,128,128]{3,2,1,0:T(8,128)(2,1)S(1)}, u32[]{:S(2)}, u32[]{:S(2)}) collective-permute-start(bf16[1,2,128,128]{3,2,1,0:T(8,128)(2,1)S(1)} %get-tuple-element.141), channel_id=1, source_target_pairs={{0,4},{1,5},{2,6},{3,7},{4,0},{5,1},{6,2},{7,3},{8,12},{9,13},{10,... | collective-permute-start | bytes 196616 | tf_op jit(solution)/shard_map/ppermute | solution.py:33
  98.8 1.8 %shard_map.99 = (bf16[128,2560]{1,0:T(8,128)(2,1)}, bf16[128,2560]{1,0:T(8,128)(2,1)}) custom-call(s32[2]{0:T(128)S(1)} %pad_add_fusion.refs_0_.me, bf16[2,2,128,128]{3,2,1,0:T(8,128)(2,1)S(1)} %get-tuple-element.102.refs_1_, bf16[2,2,128,128]{3,2,1,0:T(8,128)(2,1)S(1)} %collective-permute-done.17.refs_2_, ...), custom_call_target="tpu_custom_call" | custom-call | tf_op jit(solution)/shard_map/pallas_call | solution.py:104
  103.1 1.8 %shard_map.100 = (bf16[128,2560]{1,0:T(8,128)(2,1)}, bf16[128,2560]{1,0:T(8,128)(2,1)}) custom-call(s32[2]{0:T(128)S(1)} %pad_add_fusion.refs_0_.me, bf16[5,2,128,128]{3,2,1,0:T(8,128)(2,1)S(1)} %pad_maximum_fusion.2.refs_5_.refs_1_, bf16[5,2,128,128]{3,2,1,0:T(8,128)(2,1)S(1)} %collective-permute-done.20.refs_6_.refs_2_, ...), custom_call_target="tpu_custom_call" | custom-call | tf_op jit(solution)/shard_map/pallas_call | solution.py:104
  (77 shorter events, 25.1 us)
Async XLA Ops:
  3.6 6.5 %collective-permute-start = (bf16[2,2,128,128]{3,2,1,0:T(8,128)(2,1)S(1)}, bf16[2,2,128,128]{3,2,1,0:T(8,128)(2,1)S(1)}, u32[]{:S(2)}, u32[]{:S(2)}) collective-permute-start(bf16[2,2,128,128]{3,2,1,0:T(8,128)(2,1)S(1)} %get-tuple-element.68), channel_id=1, source_target_pairs={{0,2},{1,3},{2,0},{3,1},{4,6},{5,7},{6,4},{7,5},{8,10},{9,11},{10,... | collective-permute-start | bytes 393224 | tf_op jit(solution)/shard_map/ppermute | solution.py:33
  14.2 19.2 %collective-permute-start.6 = (bf16[4,2,2,128,128]{4,3,2,1,0:T(8,128)(2,1)S(1)}, bf16[4,2,2,128,128]{4,3,2,1,0:T(8,128)(2,1)S(1)}, u32[]{:S(2)}, u32[]{:S(2)}) collective-permute-start(bf16[4,2,2,128,128]{4,3,2,1,0:T(8,128)(2,1)S(1)} %pad_maximum_fusion.1.refs_0_), channel_id=1, source_target_pairs={{0,8},{1,9},{2,10},{3,11},{4,12},{5,13},{6,14},{7,15},{8,16},{9,17... | collective-permute-start | bytes 1572872 | tf_op jit(solution)/shard_map/ppermute | solution.py:33
  16.8 9.8 %collective-permute-start.3 = (bf16[5,2,128,128]{3,2,1,0:T(8,128)(2,1)S(1)}, bf16[5,2,128,128]{3,2,1,0:T(8,128)(2,1)S(1)}, u32[]{:S(2)}, u32[]{:S(2)}) collective-permute-start(bf16[5,2,128,128]{3,2,1,0:T(8,128)(2,1)S(1)} %get-tuple-element.72), channel_id=1, source_target_pairs={{0,2},{1,3},{2,0},{3,1},{4,6},{5,7},{6,4},{7,5},{8,10},{9,11},{10,... | collective-permute-start | bytes 983048 | tf_op jit(solution)/shard_map/ppermute | solution.py:33
  18.4 10.6 %collective-permute-start.4 = (bf16[5,2,128,128]{3,2,1,0:T(8,128)(2,1)S(1)}, bf16[5,2,128,128]{3,2,1,0:T(8,128)(2,1)S(1)}, u32[]{:S(2)}, u32[]{:S(2)}) collective-permute-start(bf16[5,2,128,128]{3,2,1,0:T(8,128)(2,1)S(1)} %get-tuple-element.73), channel_id=1, source_target_pairs={{0,4},{1,5},{2,6},{3,7},{4,0},{5,1},{6,2},{7,3},{8,12},{9,13},{10,... | collective-permute-start | bytes 983048 | tf_op jit(solution)/shard_map/ppermute | solution.py:33
  19.9 13.5 %collective-permute-start.5 = (bf16[5,2,128,128]{3,2,1,0:T(8,128)(2,1)S(1)}, bf16[5,2,128,128]{3,2,1,0:T(8,128)(2,1)S(1)}, u32[]{:S(2)}, u32[]{:S(2)}) collective-permute-start(bf16[5,2,128,128]{3,2,1,0:T(8,128)(2,1)S(1)} %get-tuple-element.74), channel_id=1, source_target_pairs={{0,6},{1,7},{2,4},{3,5},{4,2},{5,3},{6,0},{7,1},{8,14},{9,15},{10,... | collective-permute-start | bytes 983048 | tf_op jit(solution)/shard_map/ppermute | solution.py:33
  33.6 18.8 %collective-permute-start.13 = (bf16[4,3,2,128,128]{4,3,2,1,0:T(8,128)(2,1)S(1)}, bf16[4,3,2,128,128]{4,3,2,1,0:T(8,128)(2,1)S(1)}, u32[]{:S(2)}, u32[]{:S(2)}) collective-permute-start(bf16[4,3,2,128,128]{4,3,2,1,0:T(8,128)(2,1)S(1)} %pad_maximum_fusion.refs_0_), channel_id=1, source_target_pairs={{0,8},{1,9},{2,10},{3,11},{4,12},{5,13},{6,14},{7,15},{8,16},{9,17... | collective-permute-start | bytes 2359304 | tf_op jit(solution)/shard_map/ppermute | solution.py:33
  36.5 11.9 %collective-permute-start.10 = (bf16[3,2,128,128]{3,2,1,0:T(8,128)(2,1)S(1)}, bf16[3,2,128,128]{3,2,1,0:T(8,128)(2,1)S(1)}, u32[]{:S(2)}, u32[]{:S(2)}) collective-permute-start(bf16[3,2,128,128]{3,2,1,0:T(8,128)(2,1)S(1)} %get-tuple-element.83), channel_id=1, source_target_pairs={{0,2},{1,3},{2,0},{3,1},{4,6},{5,7},{6,4},{7,5},{8,10},{9,11},{10,... | collective-permute-start | bytes 589832 | tf_op jit(solution)/shard_map/ppermute | solution.py:33
  37.4 11.0 %collective-permute-start.11 = (bf16[3,2,128,128]{3,2,1,0:T(8,128)(2,1)S(1)}, bf16[3,2,128,128]{3,2,1,0:T(8,128)(2,1)S(1)}, u32[]{:S(2)}, u32[]{:S(2)}) collective-permute-start(bf16[3,2,128,128]{3,2,1,0:T(8,128)(2,1)S(1)} %get-tuple-element.84), channel_id=1, source_target_pairs={{0,4},{1,5},{2,6},{3,7},{4,0},{5,1},{6,2},{7,3},{8,12},{9,13},{10,... | collective-permute-start | bytes 589832 | tf_op jit(solution)/shard_map/ppermute | solution.py:33
  38.9 9.9 %collective-permute-start.12 = (bf16[3,2,128,128]{3,2,1,0:T(8,128)(2,1)S(1)}, bf16[3,2,128,128]{3,2,1,0:T(8,128)(2,1)S(1)}, u32[]{:S(2)}, u32[]{:S(2)}) collective-permute-start(bf16[3,2,128,128]{3,2,1,0:T(8,128)(2,1)S(1)} %get-tuple-element.85), channel_id=1, source_target_pairs={{0,6},{1,7},{2,4},{3,5},{4,2},{5,3},{6,0},{7,1},{8,14},{9,15},{10,... | collective-permute-start | bytes 589832 | tf_op jit(solution)/shard_map/ppermute | solution.py:33
  52.9 6.8 %collective-permute-start.14 = (bf16[4,3,2,128,128]{4,3,2,1,0:T(8,128)(2,1)S(1)}, bf16[4,3,2,128,128]{4,3,2,1,0:T(8,128)(2,1)S(1)}, u32[]{:S(2)}, u32[]{:S(2)}) collective-permute-start(bf16[4,3,2,128,128]{4,3,2,1,0:T(8,128)(2,1)S(1)} %collective-permute-done.13.refs_2_), channel_id=1, source_target_pairs={{0,1},{1,0},{2,3},{3,2},{4,5},{5,4},{6,7},{7,6},{8,9},{9,8},{10,11... | collective-permute-start | bytes 2359304 | tf_op jit(solution)/shard_map/ppermute | solution.py:33
  55.2 14.2 %collective-permute-start.16 = (bf16[4,2,2,128,128]{4,3,2,1,0:T(8,128)(2,1)S(1)}, bf16[4,2,2,128,128]{4,3,2,1,0:T(8,128)(2,1)S(1)}, u32[]{:S(2)}, u32[]{:S(2)}) collective-permute-start(bf16[4,2,2,128,128]{4,3,2,1,0:T(8,128)(2,1)S(1)} %add_convert_fusion.1), channel_id=1, source_target_pairs={{0,24},{1,25},{2,26},{3,27},{4,28},{5,29},{6,30},{7,31},{8,0},{9,1... | collective-permute-start | bytes 1572872 | tf_op jit(solution)/shard_map/ppermute | solution.py:33
  56.2 11.8 %collective-permute-start.17 = (bf16[2,2,128,128]{3,2,1,0:T(8,128)(2,1)S(1)}, bf16[2,2,128,128]{3,2,1,0:T(8,128)(2,1)S(1)}, u32[]{:S(2)}, u32[]{:S(2)}) collective-permute-start(bf16[2,2,128,128]{3,2,1,0:T(8,128)(2,1)S(1)} %get-tuple-element.99), channel_id=1, source_target_pairs={{0,2},{1,3},{2,0},{3,1},{4,6},{5,7},{6,4},{7,5},{8,10},{9,11},{10,... | collective-permute-start | bytes 393224 | tf_op jit(solution)/shard_map/ppermute | solution.py:33
  56.3 11.7 %collective-permute-start.18 = (bf16[2,2,128,128]{3,2,1,0:T(8,128)(2,1)S(1)}, bf16[2,2,128,128]{3,2,1,0:T(8,128)(2,1)S(1)}, u32[]{:S(2)}, u32[]{:S(2)}) collective-permute-start(bf16[2,2,128,128]{3,2,1,0:T(8,128)(2,1)S(1)} %get-tuple-element.100), channel_id=1, source_target_pairs={{0,4},{1,5},{2,6},{3,7},{4,0},{5,1},{6,2},{7,3},{8,12},{9,13},{10,... | collective-permute-start | bytes 393224 | tf_op jit(solution)/shard_map/ppermute | solution.py:33
  57.8 10.3 %collective-permute-start.19 = (bf16[2,2,128,128]{3,2,1,0:T(8,128)(2,1)S(1)}, bf16[2,2,128,128]{3,2,1,0:T(8,128)(2,1)S(1)}, u32[]{:S(2)}, u32[]{:S(2)}) collective-permute-start(bf16[2,2,128,128]{3,2,1,0:T(8,128)(2,1)S(1)} %get-tuple-element.101), channel_id=1, source_target_pairs={{0,6},{1,7},{2,4},{3,5},{4,2},{5,3},{6,0},{7,1},{8,14},{9,15},{10,... | collective-permute-start | bytes 393224 | tf_op jit(solution)/shard_map/ppermute | solution.py:33
  74.6 14.9 %collective-permute-start.24 = (bf16[4,2,2,128,128]{4,3,2,1,0:T(8,128)(2,1)S(1)}, bf16[4,2,2,128,128]{4,3,2,1,0:T(8,128)(2,1)S(1)}, u32[]{:S(2)}, u32[]{:S(2)}) collective-permute-start(bf16[4,2,2,128,128]{4,3,2,1,0:T(8,128)(2,1)S(1)} %add_convert_fusion), channel_id=1, source_target_pairs={{0,24},{1,25},{2,26},{3,27},{4,28},{5,29},{6,30},{7,31},{8,0},{9,1... | collective-permute-start | bytes 1572872 | tf_op jit(solution)/shard_map/ppermute | solution.py:33
  77.3 13.6 %collective-permute-start.22 = (bf16[5,2,128,128]{3,2,1,0:T(8,128)(2,1)S(1)}, bf16[5,2,128,128]{3,2,1,0:T(8,128)(2,1)S(1)}, u32[]{:S(2)}, u32[]{:S(2)}) collective-permute-start(bf16[5,2,128,128]{3,2,1,0:T(8,128)(2,1)S(1)} %pad_maximum_fusion.5), channel_id=1, source_target_pairs={{0,6},{1,7},{2,4},{3,5},{4,2},{5,3},{6,0},{7,1},{8,14},{9,15},{10,... | collective-permute-start | bytes 983048 | tf_op jit(solution)/shard_map/ppermute | solution.py:33
  78.4 16.1 %collective-permute-start.21 = (bf16[5,2,128,128]{3,2,1,0:T(8,128)(2,1)S(1)}, bf16[5,2,128,128]{3,2,1,0:T(8,128)(2,1)S(1)}, u32[]{:S(2)}, u32[]{:S(2)}) collective-permute-start(bf16[5,2,128,128]{3,2,1,0:T(8,128)(2,1)S(1)} %pad_maximum_fusion.4), channel_id=1, source_target_pairs={{0,4},{1,5},{2,6},{3,7},{4,0},{5,1},{6,2},{7,3},{8,12},{9,13},{10,... | collective-permute-start | bytes 983048 | tf_op jit(solution)/shard_map/ppermute | solution.py:33
  79.0 15.2 %collective-permute-start.29 = (bf16[4,1,2,128,128]{4,3,2,1,0:T(8,128)(2,1)S(1)}, bf16[4,1,2,128,128]{4,3,2,1,0:T(8,128)(2,1)S(1)}, u32[]{:S(2)}, u32[]{:S(2)}) collective-permute-start(bf16[4,1,2,128,128]{4,3,2,1,0:T(8,128)(2,1)S(1)} %add_convert_fusion.2), channel_id=1, source_target_pairs={{0,24},{1,25},{2,26},{3,27},{4,28},{5,29},{6,30},{7,31},{8,0},{9,1... | collective-permute-start | bytes 786440 | tf_op jit(solution)/shard_map/ppermute | solution.py:33
  79.1 16.8 %collective-permute-start.20 = (bf16[5,2,128,128]{3,2,1,0:T(8,128)(2,1)S(1)}, bf16[5,2,128,128]{3,2,1,0:T(8,128)(2,1)S(1)}, u32[]{:S(2)}, u32[]{:S(2)}) collective-permute-start(bf16[5,2,128,128]{3,2,1,0:T(8,128)(2,1)S(1)} %pad_maximum_fusion.3), channel_id=1, source_target_pairs={{0,2},{1,3},{2,0},{3,1},{4,6},{5,7},{6,4},{7,5},{8,10},{9,11},{10,... | collective-permute-start | bytes 983048 | tf_op jit(solution)/shard_map/ppermute | solution.py:33
  89.7 9.0 %collective-permute-start.27 = (bf16[2,2,128,128]{3,2,1,0:T(8,128)(2,1)S(1)}, bf16[2,2,128,128]{3,2,1,0:T(8,128)(2,1)S(1)}, u32[]{:S(2)}, u32[]{:S(2)}) collective-permute-start(bf16[2,2,128,128]{3,2,1,0:T(8,128)(2,1)S(1)} %get-tuple-element.132), channel_id=1, source_target_pairs={{0,6},{1,7},{2,4},{3,5},{4,2},{5,3},{6,0},{7,1},{8,14},{9,15},{10,... | collective-permute-start | bytes 393224 | tf_op jit(solution)/shard_map/ppermute | solution.py:33
  90.8 9.8 %collective-permute-start.26 = (bf16[2,2,128,128]{3,2,1,0:T(8,128)(2,1)S(1)}, bf16[2,2,128,128]{3,2,1,0:T(8,128)(2,1)S(1)}, u32[]{:S(2)}, u32[]{:S(2)}) collective-permute-start(bf16[2,2,128,128]{3,2,1,0:T(8,128)(2,1)S(1)} %get-tuple-element.133), channel_id=1, source_target_pairs={{0,4},{1,5},{2,6},{3,7},{4,0},{5,1},{6,2},{7,3},{8,12},{9,13},{10,... | collective-permute-start | bytes 393224 | tf_op jit(solution)/shard_map/ppermute | solution.py:33
  94.2 7.6 %collective-permute-start.25 = (bf16[2,2,128,128]{3,2,1,0:T(8,128)(2,1)S(1)}, bf16[2,2,128,128]{3,2,1,0:T(8,128)(2,1)S(1)}, u32[]{:S(2)}, u32[]{:S(2)}) collective-permute-start(bf16[2,2,128,128]{3,2,1,0:T(8,128)(2,1)S(1)} %get-tuple-element.134), channel_id=1, source_target_pairs={{0,2},{1,3},{2,0},{3,1},{4,6},{5,7},{6,4},{7,5},{8,10},{9,11},{10,... | collective-permute-start | bytes 393224 | tf_op jit(solution)/shard_map/ppermute | solution.py:33
  94.5 7.9 %collective-permute-start.32 = (bf16[1,2,128,128]{3,2,1,0:T(8,128)(2,1)S(1)}, bf16[1,2,128,128]{3,2,1,0:T(8,128)(2,1)S(1)}, u32[]{:S(2)}, u32[]{:S(2)}) collective-permute-start(bf16[1,2,128,128]{3,2,1,0:T(8,128)(2,1)S(1)} %get-tuple-element.140), channel_id=1, source_target_pairs={{0,6},{1,7},{2,4},{3,5},{4,2},{5,3},{6,0},{7,1},{8,14},{9,15},{10,... | collective-permute-start | bytes 196616 | tf_op jit(solution)/shard_map/ppermute | solution.py:33
  96.0 6.4 %collective-permute-start.31 = (bf16[1,2,128,128]{3,2,1,0:T(8,128)(2,1)S(1)}, bf16[1,2,128,128]{3,2,1,0:T(8,128)(2,1)S(1)}, u32[]{:S(2)}, u32[]{:S(2)}) collective-permute-start(bf16[1,2,128,128]{3,2,1,0:T(8,128)(2,1)S(1)} %get-tuple-element.141), channel_id=1, source_target_pairs={{0,4},{1,5},{2,6},{3,7},{4,0},{5,1},{6,2},{7,3},{8,12},{9,13},{10,... | collective-permute-start | bytes 196616 | tf_op jit(solution)/shard_map/ppermute | solution.py:33
  (15 other events, 77.5 us)

commit v5 on v4

--- a/solution.py
+++ b/solution.py
@@ -206,12 +206,14 @@
                     sent_b[first + to + c - 2, n] = block.astype(bf)
 
     s = score(0)
+    dprob = dot(qg[0, 1], vsel[0], ((1,), (1,)))
     for j in range(SLOTS):
-        dprob = dot(qg[j, 1], vsel[j], ((1,), (1,)))
         e, inv = soft(s)
+        this = dprob
         if j + 1 < SLOTS:
             s = score(j + 1)
-        rest_of(j, e, inv, dprob)
+            dprob = dot(qg[j + 1, 1], vsel[j + 1], ((1,), (1,)))
+        rest_of(j, e, inv, this)
         if j == 1:
             grads(0)
     for place in range(1, 4):

time: 105 us -> 105 us (level)
  no operation moved by 1% of the time
where the time goes in v5:
time: 105 us
  waiting for transfers between devices  41.5 us (40%)
  starting transfers between devices  32.8 us (31%)
  Pallas kernels  26.2 us (25%)
  local copies, waits for them, and re-layouts  2.26 us (2%)
  other arithmetic  1.2 us (1%)
    ppermute x33, waiting for transfers between devices, moved(): return lax.ppermute(block, AXES, route)  41.5 us
    ppermute x33, starting transfers between devices, moved(): return lax.ppermute(block, AXES, route)  32.8 us
    pallas_call x3, Pallas kernels, attend(): pl.pallas_call(attend_kernel, grid=(nh,), out_shape=[jax.ShapeDtypeStruct...  20.4 us
    pallas_call x2, Pallas kernels, unpack(): pl.pallas_call(lambda *refs: unpack_kernel(places, per_chip, *refs), out_...  3.67 us
    unnamed x12, local copies, waits for them, and re-layouts  2.19 us
    pallas_call x3, Pallas kernels, pack(): pl.pallas_call(lambda *refs: pack_kernel(plan, per_chip, used, *refs), ou...  2.15 us
  transfers between devices with their start and end apart: 33, of which 17 were waited for; matrix products, arithmetic and copies ran while one was open for 1% of the time, Pallas kernels for 23%

profile of v5, /device:TPU:0, one launch (start us, length us, event | category | flops | bytes accessed | tf_op | source)
XLA Modules:
  0.0 104.8 jit_solution(9153757128077535123)
XLA Ops:
  3.6 3.0 %collective-permute-start = (bf16[2,2,128,128]{3,2,1,0:T(8,128)(2,1)S(1)}, bf16[2,2,128,128]{3,2,1,0:T(8,128)(2,1)S(1)}, u32[]{:S(2)}, u32[]{:S(2)}) collective-permute-start(bf16[2,2,128,128]{3,2,1,0:T(8,128)(2,1)S(1)} %get-tuple-element.68), channel_id=1, source_target_pairs={{0,2},{1,3},{2,0},{3,1},{4,6},{5,7},{6,4},{7,5},{8,10},{9,11},{10,... | collective-permute-start | bytes 393224 | tf_op jit(solution)/shard_map/ppermute | solution.py:33
  8.1 2.0 %collective-permute-done.refs_5_ = bf16[2,2,128,128]{3,2,1,0:T(8,128)(2,1)S(1)} collective-permute-done((bf16[2,2,128,128]{3,2,1,0:T(8,128)(2,1)S(1)}, bf16[2,2,128,128]{3,2,1,0:T(8,128)(2,1)S(1)}, u32[]{:S(2)}, u32[]{:S(2)}) %collective-permute-start) | collective-permute-done | bytes 131104 | tf_op jit(solution)/shard_map/ppermute | solution.py:33
  10.1 2.9 %collective-permute-done.1.refs_6_ = bf16[2,2,128,128]{3,2,1,0:T(8,128)(2,1)S(1)} collective-permute-done((bf16[2,2,128,128]{3,2,1,0:T(8,128)(2,1)S(1)}, bf16[2,2,128,128]{3,2,1,0:T(8,128)(2,1)S(1)}, u32[]{:S(2)}, u32[]{:S(2)}) %collective-permute-start.1) | collective-permute-done | bytes 131104 | tf_op jit(solution)/shard_map/ppermute | solution.py:33
  14.2 1.8 %collective-permute-start.6 = (bf16[4,2,2,128,128]{4,3,2,1,0:T(8,128)(2,1)S(1)}, bf16[4,2,2,128,128]{4,3,2,1,0:T(8,128)(2,1)S(1)}, u32[]{:S(2)}, u32[]{:S(2)}) collective-permute-start(bf16[4,2,2,128,128]{4,3,2,1,0:T(8,128)(2,1)S(1)} %pad_maximum_fusion.1.refs_0_), channel_id=1, source_target_pairs={{0,8},{1,9},{2,10},{3,11},{4,12},{5,13},{6,14},{7,15},{8,16},{9,17... | collective-permute-start | bytes 1572872 | tf_op jit(solution)/shard_map/ppermute | solution.py:33
  16.8 1.6 %collective-permute-start.3 = (bf16[5,2,128,128]{3,2,1,0:T(8,128)(2,1)S(1)}, bf16[5,2,128,128]{3,2,1,0:T(8,128)(2,1)S(1)}, u32[]{:S(2)}, u32[]{:S(2)}) collective-permute-start(bf16[5,2,128,128]{3,2,1,0:T(8,128)(2,1)S(1)} %get-tuple-element.72), channel_id=1, source_target_pairs={{0,2},{1,3},{2,0},{3,1},{4,6},{5,7},{6,4},{7,5},{8,10},{9,11},{10,... | collective-permute-start | bytes 983048 | tf_op jit(solution)/shard_map/ppermute | solution.py:33
  20.4 6.3 %collective-permute-done.3.refs_5_.refs_3_ = bf16[5,2,128,128]{3,2,1,0:T(8,128)(2,1)S(1)} collective-permute-done((bf16[5,2,128,128]{3,2,1,0:T(8,128)(2,1)S(1)}, bf16[5,2,128,128]{3,2,1,0:T(8,128)(2,1)S(1)}, u32[]{:S(2)}, u32[]{:S(2)}) %collective-permute-start.3) | collective-permute-done | bytes 327712 | tf_op jit(solution)/shard_map/ppermute | solution.py:33
  26.6 2.4 %collective-permute-done.4.refs_6_.refs_4_ = bf16[5,2,128,128]{3,2,1,0:T(8,128)(2,1)S(1)} collective-permute-done((bf16[5,2,128,128]{3,2,1,0:T(8,128)(2,1)S(1)}, bf16[5,2,128,128]{3,2,1,0:T(8,128)(2,1)S(1)}, u32[]{:S(2)}, u32[]{:S(2)}) %collective-permute-start.4) | collective-permute-done | bytes 327712 | tf_op jit(solution)/shard_map/ppermute | solution.py:33
  29.0 4.4 %collective-permute-done.5.refs_7_.refs_5_ = bf16[5,2,128,128]{3,2,1,0:T(8,128)(2,1)S(1)} collective-permute-done((bf16[5,2,128,128]{3,2,1,0:T(8,128)(2,1)S(1)}, bf16[5,2,128,128]{3,2,1,0:T(8,128)(2,1)S(1)}, u32[]{:S(2)}, u32[]{:S(2)}) %collective-permute-start.5) | collective-permute-done | bytes 327712 | tf_op jit(solution)/shard_map/ppermute | solution.py:33
  33.6 1.6 %collective-permute-start.13 = (bf16[4,3,2,128,128]{4,3,2,1,0:T(8,128)(2,1)S(1)}, bf16[4,3,2,128,128]{4,3,2,1,0:T(8,128)(2,1)S(1)}, u32[]{:S(2)}, u32[]{:S(2)}) collective-permute-start(bf16[4,3,2,128,128]{4,3,2,1,0:T(8,128)(2,1)S(1)} %pad_maximum_fusion.refs_0_), channel_id=1, source_target_pairs={{0,8},{1,9},{2,10},{3,11},{4,12},{5,13},{6,14},{7,15},{8,16},{9,17... | collective-permute-start | bytes 2359304 | tf_op jit(solution)/shard_map/ppermute | solution.py:33
  37.4 1.5 %collective-permute-start.11 = (bf16[3,2,128,128]{3,2,1,0:T(8,128)(2,1)S(1)}, bf16[3,2,128,128]{3,2,1,0:T(8,128)(2,1)S(1)}, u32[]{:S(2)}, u32[]{:S(2)}) collective-permute-start(bf16[3,2,128,128]{3,2,1,0:T(8,128)(2,1)S(1)} %get-tuple-element.84), channel_id=1, source_target_pairs={{0,4},{1,5},{2,6},{3,7},{4,0},{5,1},{6,2},{7,3},{8,12},{9,13},{10,... | collective-permute-start | bytes 589832 | tf_op jit(solution)/shard_map/ppermute | solution.py:33
  40.0 8.1 %shard_map.95 = (bf16[2,2,128,128]{3,2,1,0:T(8,128)(2,1)S(1)}, bf16[2,2,128,128]{3,2,1,0:T(8,128)(2,1)S(1)}, bf16[2,2,128,128]{3,2,1,0:T(8,128)(2,1)S(1)}, bf16[...) custom-call(s32[2]{0:T(128)S(1)} %pad_add_fusion.refs_0_.me, ...), custom_call_target="tpu_custom_call" | custom-call | flops 1 | bytes 1 | tf_op jit(solution)/shard_map/pallas_call | solution.py:235
  48.7 3.7 %collective-permute-done.13.refs_2_ = bf16[4,3,2,128,128]{4,3,2,1,0:T(8,128)(2,1)S(1)} collective-permute-done((bf16[4,3,2,128,128]{4,3,2,1,0:T(8,128)(2,1)S(1)}, bf16[4,3,2,128,128]{4,3,2,1,0:T(8,128)(2,1)S(1)}, u32[]{:S(2)}, u32[]{:S(2)}) %collective-permute-start.13) | collective-permute-done | bytes 786464 | tf_op jit(solution)/shard_map/ppermute | solution.py:33
  52.9 2.1 %collective-permute-done.15 = bf16[8,2,2,128,128]{4,3,2,1,0:T(8,128)(2,1)S(1)} collective-permute-done((bf16[8,2,2,128,128]{4,3,2,1,0:T(8,128)(2,1)S(1)}, bf16[8,2,2,128,128]{4,3,2,1,0:T(8,128)(2,1)S(1)}, u32[]{:S(2)}, u32[]{:S(2)}) %collective-permute-start.15) | collective-permute-done | bytes 1048608 | tf_op jit(solution)/shard_map/ppermute | solution.py:33
  57.8 2.0 %collective-permute-start.19 = (bf16[2,2,128,128]{3,2,1,0:T(8,128)(2,1)S(1)}, bf16[2,2,128,128]{3,2,1,0:T(8,128)(2,1)S(1)}, u32[]{:S(2)}, u32[]{:S(2)}) collective-permute-start(bf16[2,2,128,128]{3,2,1,0:T(8,128)(2,1)S(1)} %get-tuple-element.101), channel_id=1, source_target_pairs={{0,6},{1,7},{2,4},{3,5},{4,2},{5,3},{6,0},{7,1},{8,14},{9,15},{10,... | collective-permute-start | bytes 393224 | tf_op jit(solution)/shard_map/ppermute | solution.py:33
  59.7 8.1 %shard_map.97 = (bf16[2,2,128,128]{3,2,1,0:T(8,128)(2,1)S(1)}, bf16[2,2,128,128]{3,2,1,0:T(8,128)(2,1)S(1)}, bf16[2,2,128,128]{3,2,1,0:T(8,128)(2,1)S(1)}, bf16[...) custom-call(s32[2]{0:T(128)S(1)} %pad_add_fusion.refs_0_.me, ...), custom_call_target="tpu_custom_call" | custom-call | flops 1 | bytes 1 | tf_op jit(solution)/shard_map/pallas_call | solution.py:235
  67.9 1.5 %collective-permute-done.16 = bf16[4,2,2,128,128]{4,3,2,1,0:T(8,128)(2,1)S(1)} collective-permute-done((bf16[4,2,2,128,128]{4,3,2,1,0:T(8,128)(2,1)S(1)}, bf16[4,2,2,128,128]{4,3,2,1,0:T(8,128)(2,1)S(1)}, u32[]{:S(2)}, u32[]{:S(2)}) %collective-permute-start.16) | collective-permute-done | bytes 524320 | tf_op jit(solution)/shard_map/ppermute | solution.py:33
  69.4 4.1 %shard_map.98 = (bf16[1,2,128,128]{3,2,1,0:T(8,128)(2,1)S(1)}, bf16[1,2,128,128]{3,2,1,0:T(8,128)(2,1)S(1)}, bf16[1,2,128,128]{3,2,1,0:T(8,128)(2,1)S(1)}, bf16[...) custom-call(s32[2]{0:T(128)S(1)} %pad_add_fusion.refs_0_.me, ...), custom_call_target="tpu_custom_call" | custom-call | flops 1 | bytes 1 | tf_op jit(solution)/shard_map/pallas_call | solution.py:235
  74.5 2.6 %collective-permute-start.24 = (bf16[4,2,2,128,128]{4,3,2,1,0:T(8,128)(2,1)S(1)}, bf16[4,2,2,128,128]{4,3,2,1,0:T(8,128)(2,1)S(1)}, u32[]{:S(2)}, u32[]{:S(2)}) collective-permute-start(bf16[4,2,2,128,128]{4,3,2,1,0:T(8,128)(2,1)S(1)} %add_convert_fusion), channel_id=1, source_target_pairs={{0,24},{1,25},{2,26},{3,27},{4,28},{5,29},{6,30},{7,31},{8,0},{9,1... | collective-permute-start | bytes 1572872 | tf_op jit(solution)/shard_map/ppermute | solution.py:33
  79.0 2.0 %collective-permute-start.20 = (bf16[5,2,128,128]{3,2,1,0:T(8,128)(2,1)S(1)}, bf16[5,2,128,128]{3,2,1,0:T(8,128)(2,1)S(1)}, u32[]{:S(2)}, u32[]{:S(2)}) collective-permute-start(bf16[5,2,128,128]{3,2,1,0:T(8,128)(2,1)S(1)} %pad_maximum_fusion.3), channel_id=1, source_target_pairs={{0,2},{1,3},{2,0},{3,1},{4,6},{5,7},{6,4},{7,5},{8,10},{9,11},{10,... | collective-permute-start | bytes 983048 | tf_op jit(solution)/shard_map/ppermute | solution.py:33
  81.1 8.3 %collective-permute-done.24 = bf16[4,2,2,128,128]{4,3,2,1,0:T(8,128)(2,1)S(1)} collective-permute-done((bf16[4,2,2,128,128]{4,3,2,1,0:T(8,128)(2,1)S(1)}, bf16[4,2,2,128,128]{4,3,2,1,0:T(8,128)(2,1)S(1)}, u32[]{:S(2)}, u32[]{:S(2)}) %collective-permute-start.24) | collective-permute-done | bytes 524320 | tf_op jit(solution)/shard_map/ppermute | solution.py:33
  91.2 2.9 %collective-permute-done.29 = bf16[4,1,2,128,128]{4,3,2,1,0:T(8,128)(2,1)S(1)} collective-permute-done((bf16[4,1,2,128,128]{4,3,2,1,0:T(8,128)(2,1)S(1)}, bf16[4,1,2,128,128]{4,3,2,1,0:T(8,128)(2,1)S(1)}, u32[]{:S(2)}, u32[]{:S(2)}) %collective-permute-start.29) | collective-permute-done | bytes 262176 | tf_op jit(solution)/shard_map/ppermute | solution.py:33
  95.8 2.0 %collective-permute-start.31 = (bf16[1,2,128,128]{3,2,1,0:T(8,128)(2,1)S(1)}, bf16[1,2,128,128]{3,2,1,0:T(8,128)(2,1)S(1)}, u32[]{:S(2)}, u32[]{:S(2)}) collective-permute-start(bf16[1,2,128,128]{3,2,1,0:T(8,128)(2,1)S(1)} %get-tuple-element.141), channel_id=1, source_target_pairs={{0,4},{1,5},{2,6},{3,7},{4,0},{5,1},{6,2},{7,3},{8,12},{9,13},{10,... | collective-permute-start | bytes 196616 | tf_op jit(solution)/shard_map/ppermute | solution.py:33
  98.7 1.8 %shard_map.99 = (bf16[128,2560]{1,0:T(8,128)(2,1)}, bf16[128,2560]{1,0:T(8,128)(2,1)}) custom-call(s32[2]{0:T(128)S(1)} %pad_add_fusion.refs_0_.me, bf16[2,2,128,128]{3,2,1,0:T(8,128)(2,1)S(1)} %get-tuple-element.102.refs_1_, bf16[2,2,128,128]{3,2,1,0:T(8,128)(2,1)S(1)} %collective-permute-done.17.refs_2_, ...), custom_call_target="tpu_custom_call" | custom-call | tf_op jit(solution)/shard_map/pallas_call | solution.py:104
  103.0 1.8 %shard_map.100 = (bf16[128,2560]{1,0:T(8,128)(2,1)}, bf16[128,2560]{1,0:T(8,128)(2,1)}) custom-call(s32[2]{0:T(128)S(1)} %pad_add_fusion.refs_0_.me, bf16[5,2,128,128]{3,2,1,0:T(8,128)(2,1)S(1)} %pad_maximum_fusion.2.refs_5_.refs_1_, bf16[5,2,128,128]{3,2,1,0:T(8,128)(2,1)S(1)} %collective-permute-done.20.refs_6_.refs_2_, ...), custom_call_target="tpu_custom_call" | custom-call | tf_op jit(solution)/shard_map/pallas_call | solution.py:104
  (77 shorter events, 25.3 us)
Async XLA Ops:
  3.6 6.5 %collective-permute-start = (bf16[2,2,128,128]{3,2,1,0:T(8,128)(2,1)S(1)}, bf16[2,2,128,128]{3,2,1,0:T(8,128)(2,1)S(1)}, u32[]{:S(2)}, u32[]{:S(2)}) collective-permute-start(bf16[2,2,128,128]{3,2,1,0:T(8,128)(2,1)S(1)} %get-tuple-element.68), channel_id=1, source_target_pairs={{0,2},{1,3},{2,0},{3,1},{4,6},{5,7},{6,4},{7,5},{8,10},{9,11},{10,... | collective-permute-start | bytes 393224 | tf_op jit(solution)/shard_map/ppermute | solution.py:33
  14.2 19.2 %collective-permute-start.6 = (bf16[4,2,2,128,128]{4,3,2,1,0:T(8,128)(2,1)S(1)}, bf16[4,2,2,128,128]{4,3,2,1,0:T(8,128)(2,1)S(1)}, u32[]{:S(2)}, u32[]{:S(2)}) collective-permute-start(bf16[4,2,2,128,128]{4,3,2,1,0:T(8,128)(2,1)S(1)} %pad_maximum_fusion.1.refs_0_), channel_id=1, source_target_pairs={{0,8},{1,9},{2,10},{3,11},{4,12},{5,13},{6,14},{7,15},{8,16},{9,17... | collective-permute-start | bytes 1572872 | tf_op jit(solution)/shard_map/ppermute | solution.py:33
  16.8 9.8 %collective-permute-start.3 = (bf16[5,2,128,128]{3,2,1,0:T(8,128)(2,1)S(1)}, bf16[5,2,128,128]{3,2,1,0:T(8,128)(2,1)S(1)}, u32[]{:S(2)}, u32[]{:S(2)}) collective-permute-start(bf16[5,2,128,128]{3,2,1,0:T(8,128)(2,1)S(1)} %get-tuple-element.72), channel_id=1, source_target_pairs={{0,2},{1,3},{2,0},{3,1},{4,6},{5,7},{6,4},{7,5},{8,10},{9,11},{10,... | collective-permute-start | bytes 983048 | tf_op jit(solution)/shard_map/ppermute | solution.py:33
  18.4 10.6 %collective-permute-start.4 = (bf16[5,2,128,128]{3,2,1,0:T(8,128)(2,1)S(1)}, bf16[5,2,128,128]{3,2,1,0:T(8,128)(2,1)S(1)}, u32[]{:S(2)}, u32[]{:S(2)}) collective-permute-start(bf16[5,2,128,128]{3,2,1,0:T(8,128)(2,1)S(1)} %get-tuple-element.73), channel_id=1, source_target_pairs={{0,4},{1,5},{2,6},{3,7},{4,0},{5,1},{6,2},{7,3},{8,12},{9,13},{10,... | collective-permute-start | bytes 983048 | tf_op jit(solution)/shard_map/ppermute | solution.py:33
  19.9 13.5 %collective-permute-start.5 = (bf16[5,2,128,128]{3,2,1,0:T(8,128)(2,1)S(1)}, bf16[5,2,128,128]{3,2,1,0:T(8,128)(2,1)S(1)}, u32[]{:S(2)}, u32[]{:S(2)}) collective-permute-start(bf16[5,2,128,128]{3,2,1,0:T(8,128)(2,1)S(1)} %get-tuple-element.74), channel_id=1, source_target_pairs={{0,6},{1,7},{2,4},{3,5},{4,2},{5,3},{6,0},{7,1},{8,14},{9,15},{10,... | collective-permute-start | bytes 983048 | tf_op jit(solution)/shard_map/ppermute | solution.py:33
  33.6 18.8 %collective-permute-start.13 = (bf16[4,3,2,128,128]{4,3,2,1,0:T(8,128)(2,1)S(1)}, bf16[4,3,2,128,128]{4,3,2,1,0:T(8,128)(2,1)S(1)}, u32[]{:S(2)}, u32[]{:S(2)}) collective-permute-start(bf16[4,3,2,128,128]{4,3,2,1,0:T(8,128)(2,1)S(1)} %pad_maximum_fusion.refs_0_), channel_id=1, source_target_pairs={{0,8},{1,9},{2,10},{3,11},{4,12},{5,13},{6,14},{7,15},{8,16},{9,17... | collective-permute-start | bytes 2359304 | tf_op jit(solution)/shard_map/ppermute | solution.py:33
  36.5 11.7 %collective-permute-start.10 = (bf16[3,2,128,128]{3,2,1,0:T(8,128)(2,1)S(1)}, bf16[3,2,128,128]{3,2,1,0:T(8,128)(2,1)S(1)}, u32[]{:S(2)}, u32[]{:S(2)}) collective-permute-start(bf16[3,2,128,128]{3,2,1,0:T(8,128)(2,1)S(1)} %get-tuple-element.83), channel_id=1, source_target_pairs={{0,2},{1,3},{2,0},{3,1},{4,6},{5,7},{6,4},{7,5},{8,10},{9,11},{10,... | collective-permute-start | bytes 589832 | tf_op jit(solution)/shard_map/ppermute | solution.py:33
  37.4 10.8 %collective-permute-start.11 = (bf16[3,2,128,128]{3,2,1,0:T(8,128)(2,1)S(1)}, bf16[3,2,128,128]{3,2,1,0:T(8,128)(2,1)S(1)}, u32[]{:S(2)}, u32[]{:S(2)}) collective-permute-start(bf16[3,2,128,128]{3,2,1,0:T(8,128)(2,1)S(1)} %get-tuple-element.84), channel_id=1, source_target_pairs={{0,4},{1,5},{2,6},{3,7},{4,0},{5,1},{6,2},{7,3},{8,12},{9,13},{10,... | collective-permute-start | bytes 589832 | tf_op jit(solution)/shard_map/ppermute | solution.py:33
  38.9 9.9 %collective-permute-start.12 = (bf16[3,2,128,128]{3,2,1,0:T(8,128)(2,1)S(1)}, bf16[3,2,128,128]{3,2,1,0:T(8,128)(2,1)S(1)}, u32[]{:S(2)}, u32[]{:S(2)}) collective-permute-start(bf16[3,2,128,128]{3,2,1,0:T(8,128)(2,1)S(1)} %get-tuple-element.85), channel_id=1, source_target_pairs={{0,6},{1,7},{2,4},{3,5},{4,2},{5,3},{6,0},{7,1},{8,14},{9,15},{10,... | collective-permute-start | bytes 589832 | tf_op jit(solution)/shard_map/ppermute | solution.py:33
  52.9 6.8 %collective-permute-start.14 = (bf16[4,3,2,128,128]{4,3,2,1,0:T(8,128)(2,1)S(1)}, bf16[4,3,2,128,128]{4,3,2,1,0:T(8,128)(2,1)S(1)}, u32[]{:S(2)}, u32[]{:S(2)}) collective-permute-start(bf16[4,3,2,128,128]{4,3,2,1,0:T(8,128)(2,1)S(1)} %collective-permute-done.13.refs_2_), channel_id=1, source_target_pairs={{0,1},{1,0},{2,3},{3,2},{4,5},{5,4},{6,7},{7,6},{8,9},{9,8},{10,11... | collective-permute-start | bytes 2359304 | tf_op jit(solution)/shard_map/ppermute | solution.py:33
  55.2 14.2 %collective-permute-start.16 = (bf16[4,2,2,128,128]{4,3,2,1,0:T(8,128)(2,1)S(1)}, bf16[4,2,2,128,128]{4,3,2,1,0:T(8,128)(2,1)S(1)}, u32[]{:S(2)}, u32[]{:S(2)}) collective-permute-start(bf16[4,2,2,128,128]{4,3,2,1,0:T(8,128)(2,1)S(1)} %add_convert_fusion.1), channel_id=1, source_target_pairs={{0,24},{1,25},{2,26},{3,27},{4,28},{5,29},{6,30},{7,31},{8,0},{9,1... | collective-permute-start | bytes 1572872 | tf_op jit(solution)/shard_map/ppermute | solution.py:33
  56.2 11.6 %collective-permute-start.17 = (bf16[2,2,128,128]{3,2,1,0:T(8,128)(2,1)S(1)}, bf16[2,2,128,128]{3,2,1,0:T(8,128)(2,1)S(1)}, u32[]{:S(2)}, u32[]{:S(2)}) collective-permute-start(bf16[2,2,128,128]{3,2,1,0:T(8,128)(2,1)S(1)} %get-tuple-element.99), channel_id=1, source_target_pairs={{0,2},{1,3},{2,0},{3,1},{4,6},{5,7},{6,4},{7,5},{8,10},{9,11},{10,... | collective-permute-start | bytes 393224 | tf_op jit(solution)/shard_map/ppermute | solution.py:33
  56.3 11.6 %collective-permute-start.18 = (bf16[2,2,128,128]{3,2,1,0:T(8,128)(2,1)S(1)}, bf16[2,2,128,128]{3,2,1,0:T(8,128)(2,1)S(1)}, u32[]{:S(2)}, u32[]{:S(2)}) collective-permute-start(bf16[2,2,128,128]{3,2,1,0:T(8,128)(2,1)S(1)} %get-tuple-element.100), channel_id=1, source_target_pairs={{0,4},{1,5},{2,6},{3,7},{4,0},{5,1},{6,2},{7,3},{8,12},{9,13},{10,... | collective-permute-start | bytes 393224 | tf_op jit(solution)/shard_map/ppermute | solution.py:33
  57.8 10.1 %collective-permute-start.19 = (bf16[2,2,128,128]{3,2,1,0:T(8,128)(2,1)S(1)}, bf16[2,2,128,128]{3,2,1,0:T(8,128)(2,1)S(1)}, u32[]{:S(2)}, u32[]{:S(2)}) collective-permute-start(bf16[2,2,128,128]{3,2,1,0:T(8,128)(2,1)S(1)} %get-tuple-element.101), channel_id=1, source_target_pairs={{0,6},{1,7},{2,4},{3,5},{4,2},{5,3},{6,0},{7,1},{8,14},{9,15},{10,... | collective-permute-start | bytes 393224 | tf_op jit(solution)/shard_map/ppermute | solution.py:33
  74.5 14.9 %collective-permute-start.24 = (bf16[4,2,2,128,128]{4,3,2,1,0:T(8,128)(2,1)S(1)}, bf16[4,2,2,128,128]{4,3,2,1,0:T(8,128)(2,1)S(1)}, u32[]{:S(2)}, u32[]{:S(2)}) collective-permute-start(bf16[4,2,2,128,128]{4,3,2,1,0:T(8,128)(2,1)S(1)} %add_convert_fusion), channel_id=1, source_target_pairs={{0,24},{1,25},{2,26},{3,27},{4,28},{5,29},{6,30},{7,31},{8,0},{9,1... | collective-permute-start | bytes 1572872 | tf_op jit(solution)/shard_map/ppermute | solution.py:33
  77.1 13.6 %collective-permute-start.22 = (bf16[5,2,128,128]{3,2,1,0:T(8,128)(2,1)S(1)}, bf16[5,2,128,128]{3,2,1,0:T(8,128)(2,1)S(1)}, u32[]{:S(2)}, u32[]{:S(2)}) collective-permute-start(bf16[5,2,128,128]{3,2,1,0:T(8,128)(2,1)S(1)} %pad_maximum_fusion.5), channel_id=1, source_target_pairs={{0,6},{1,7},{2,4},{3,5},{4,2},{5,3},{6,0},{7,1},{8,14},{9,15},{10,... | collective-permute-start | bytes 983048 | tf_op jit(solution)/shard_map/ppermute | solution.py:33
  78.2 16.1 %collective-permute-start.21 = (bf16[5,2,128,128]{3,2,1,0:T(8,128)(2,1)S(1)}, bf16[5,2,128,128]{3,2,1,0:T(8,128)(2,1)S(1)}, u32[]{:S(2)}, u32[]{:S(2)}) collective-permute-start(bf16[5,2,128,128]{3,2,1,0:T(8,128)(2,1)S(1)} %pad_maximum_fusion.4), channel_id=1, source_target_pairs={{0,4},{1,5},{2,6},{3,7},{4,0},{5,1},{6,2},{7,3},{8,12},{9,13},{10,... | collective-permute-start | bytes 983048 | tf_op jit(solution)/shard_map/ppermute | solution.py:33
  78.9 15.2 %collective-permute-start.29 = (bf16[4,1,2,128,128]{4,3,2,1,0:T(8,128)(2,1)S(1)}, bf16[4,1,2,128,128]{4,3,2,1,0:T(8,128)(2,1)S(1)}, u32[]{:S(2)}, u32[]{:S(2)}) collective-permute-start(bf16[4,1,2,128,128]{4,3,2,1,0:T(8,128)(2,1)S(1)} %add_convert_fusion.2), channel_id=1, source_target_pairs={{0,24},{1,25},{2,26},{3,27},{4,28},{5,29},{6,30},{7,31},{8,0},{9,1... | collective-permute-start | bytes 786440 | tf_op jit(solution)/shard_map/ppermute | solution.py:33
  79.0 16.8 %collective-permute-start.20 = (bf16[5,2,128,128]{3,2,1,0:T(8,128)(2,1)S(1)}, bf16[5,2,128,128]{3,2,1,0:T(8,128)(2,1)S(1)}, u32[]{:S(2)}, u32[]{:S(2)}) collective-permute-start(bf16[5,2,128,128]{3,2,1,0:T(8,128)(2,1)S(1)} %pad_maximum_fusion.3), channel_id=1, source_target_pairs={{0,2},{1,3},{2,0},{3,1},{4,6},{5,7},{6,4},{7,5},{8,10},{9,11},{10,... | collective-permute-start | bytes 983048 | tf_op jit(solution)/shard_map/ppermute | solution.py:33
  89.6 9.0 %collective-permute-start.27 = (bf16[2,2,128,128]{3,2,1,0:T(8,128)(2,1)S(1)}, bf16[2,2,128,128]{3,2,1,0:T(8,128)(2,1)S(1)}, u32[]{:S(2)}, u32[]{:S(2)}) collective-permute-start(bf16[2,2,128,128]{3,2,1,0:T(8,128)(2,1)S(1)} %get-tuple-element.132), channel_id=1, source_target_pairs={{0,6},{1,7},{2,4},{3,5},{4,2},{5,3},{6,0},{7,1},{8,14},{9,15},{10,... | collective-permute-start | bytes 393224 | tf_op jit(solution)/shard_map/ppermute | solution.py:33
  90.7 9.8 %collective-permute-start.26 = (bf16[2,2,128,128]{3,2,1,0:T(8,128)(2,1)S(1)}, bf16[2,2,128,128]{3,2,1,0:T(8,128)(2,1)S(1)}, u32[]{:S(2)}, u32[]{:S(2)}) collective-permute-start(bf16[2,2,128,128]{3,2,1,0:T(8,128)(2,1)S(1)} %get-tuple-element.133), channel_id=1, source_target_pairs={{0,4},{1,5},{2,6},{3,7},{4,0},{5,1},{6,2},{7,3},{8,12},{9,13},{10,... | collective-permute-start | bytes 393224 | tf_op jit(solution)/shard_map/ppermute | solution.py:33
  94.1 7.6 %collective-permute-start.25 = (bf16[2,2,128,128]{3,2,1,0:T(8,128)(2,1)S(1)}, bf16[2,2,128,128]{3,2,1,0:T(8,128)(2,1)S(1)}, u32[]{:S(2)}, u32[]{:S(2)}) collective-permute-start(bf16[2,2,128,128]{3,2,1,0:T(8,128)(2,1)S(1)} %get-tuple-element.134), channel_id=1, source_target_pairs={{0,2},{1,3},{2,0},{3,1},{4,6},{5,7},{6,4},{7,5},{8,10},{9,11},{10,... | collective-permute-start | bytes 393224 | tf_op jit(solution)/shard_map/ppermute | solution.py:33
  94.4 7.9 %collective-permute-start.32 = (bf16[1,2,128,128]{3,2,1,0:T(8,128)(2,1)S(1)}, bf16[1,2,128,128]{3,2,1,0:T(8,128)(2,1)S(1)}, u32[]{:S(2)}, u32[]{:S(2)}) collective-permute-start(bf16[1,2,128,128]{3,2,1,0:T(8,128)(2,1)S(1)} %get-tuple-element.140), channel_id=1, source_target_pairs={{0,6},{1,7},{2,4},{3,5},{4,2},{5,3},{6,0},{7,1},{8,14},{9,15},{10,... | collective-permute-start | bytes 196616 | tf_op jit(solution)/shard_map/ppermute | solution.py:33
  95.8 6.4 %collective-permute-start.31 = (bf16[1,2,128,128]{3,2,1,0:T(8,128)(2,1)S(1)}, bf16[1,2,128,128]{3,2,1,0:T(8,128)(2,1)S(1)}, u32[]{:S(2)}, u32[]{:S(2)}) collective-permute-start(bf16[1,2,128,128]{3,2,1,0:T(8,128)(2,1)S(1)} %get-tuple-element.141), channel_id=1, source_target_pairs={{0,4},{1,5},{2,6},{3,7},{4,0},{5,1},{6,2},{7,3},{8,12},{9,13},{10,... | collective-permute-start | bytes 196616 | tf_op jit(solution)/shard_map/ppermute | solution.py:33
  (15 other events, 77.3 us)

commit v6 on v5

--- a/solution.py
+++ b/solution.py
@@ -164,7 +164,7 @@
 
     def soft(s):
         top = jnp.max(s, -1, keepdims=True)
-        e = jnp.exp2((s - top) * c2)
+        e = jnp.exp2(s * c2 - top * c2)
         return e, 1.0 / jnp.sum(e, -1, keepdims=True)
 
     def spread(ref, j, block):

time: 105 us -> 105 us (level)
  transfers between devices with their start and end apart: 33 -> 33, of which waited for: 17 -> 17; matrix products, arithmetic and copies ran while one was open for 1% -> 1% of each run, Pallas kernels for 23% -> 22%
where the time goes in v6:
time: 105 us
  waiting for transfers between devices  41.8 us (40%)
  starting transfers between devices  32.8 us (31%)
  Pallas kernels  26 us (25%)
  local copies, waits for them, and re-layouts  2.26 us (2%)
  other arithmetic  1.2 us (1%)
    ppermute x33, waiting for transfers between devices, moved(): return lax.ppermute(block, AXES, route)  41.8 us
    ppermute x33, starting transfers between devices, moved(): return lax.ppermute(block, AXES, route)  32.8 us
    pallas_call x3, Pallas kernels, attend(): pl.pallas_call(attend_kernel, grid=(nh,), out_shape=[jax.ShapeDtypeStruct...  20.2 us
    pallas_call x2, Pallas kernels, unpack(): pl.pallas_call(lambda *refs: unpack_kernel(places, per_chip, *refs), out_...  3.67 us
    unnamed x12, local copies, waits for them, and re-layouts  2.19 us
    pallas_call x3, Pallas kernels, pack(): pl.pallas_call(lambda *refs: pack_kernel(plan, per_chip, used, *refs), ou...  2.15 us
  transfers between devices with their start and end apart: 33, of which 17 were waited for; matrix products, arithmetic and copies ran while one was open for 1% of the time, Pallas kernels for 22%

profile of v6, /device:TPU:0, one launch (start us, length us, event | category | flops | bytes accessed | tf_op | source)
XLA Modules:
  0.0 104.8 jit_solution(14430379080419269071)
XLA Ops:
  3.6 3.0 %collective-permute-start = (bf16[2,2,128,128]{3,2,1,0:T(8,128)(2,1)S(1)}, bf16[2,2,128,128]{3,2,1,0:T(8,128)(2,1)S(1)}, u32[]{:S(2)}, u32[]{:S(2)}) collective-permute-start(bf16[2,2,128,128]{3,2,1,0:T(8,128)(2,1)S(1)} %get-tuple-element.68), channel_id=1, source_target_pairs={{0,2},{1,3},{2,0},{3,1},{4,6},{5,7},{6,4},{7,5},{8,10},{9,11},{10,... | collective-permute-start | bytes 393224 | tf_op jit(solution)/shard_map/ppermute | solution.py:33
  8.1 2.0 %collective-permute-done.refs_5_ = bf16[2,2,128,128]{3,2,1,0:T(8,128)(2,1)S(1)} collective-permute-done((bf16[2,2,128,128]{3,2,1,0:T(8,128)(2,1)S(1)}, bf16[2,2,128,128]{3,2,1,0:T(8,128)(2,1)S(1)}, u32[]{:S(2)}, u32[]{:S(2)}) %collective-permute-start) | collective-permute-done | bytes 131104 | tf_op jit(solution)/shard_map/ppermute | solution.py:33
  10.1 2.9 %collective-permute-done.1.refs_6_ = bf16[2,2,128,128]{3,2,1,0:T(8,128)(2,1)S(1)} collective-permute-done((bf16[2,2,128,128]{3,2,1,0:T(8,128)(2,1)S(1)}, bf16[2,2,128,128]{3,2,1,0:T(8,128)(2,1)S(1)}, u32[]{:S(2)}, u32[]{:S(2)}) %collective-permute-start.1) | collective-permute-done | bytes 131104 | tf_op jit(solution)/shard_map/ppermute | solution.py:33
  14.2 1.8 %collective-permute-start.6 = (bf16[4,2,2,128,128]{4,3,2,1,0:T(8,128)(2,1)S(1)}, bf16[4,2,2,128,128]{4,3,2,1,0:T(8,128)(2,1)S(1)}, u32[]{:S(2)}, u32[]{:S(2)}) collective-permute-start(bf16[4,2,2,128,128]{4,3,2,1,0:T(8,128)(2,1)S(1)} %pad_maximum_fusion.1.refs_0_), channel_id=1, source_target_pairs={{0,8},{1,9},{2,10},{3,11},{4,12},{5,13},{6,14},{7,15},{8,16},{9,17... | collective-permute-start | bytes 1572872 | tf_op jit(solution)/shard_map/ppermute | solution.py:33
  16.8 1.6 %collective-permute-start.3 = (bf16[5,2,128,128]{3,2,1,0:T(8,128)(2,1)S(1)}, bf16[5,2,128,128]{3,2,1,0:T(8,128)(2,1)S(1)}, u32[]{:S(2)}, u32[]{:S(2)}) collective-permute-start(bf16[5,2,128,128]{3,2,1,0:T(8,128)(2,1)S(1)} %get-tuple-element.72), channel_id=1, source_target_pairs={{0,2},{1,3},{2,0},{3,1},{4,6},{5,7},{6,4},{7,5},{8,10},{9,11},{10,... | collective-permute-start | bytes 983048 | tf_op jit(solution)/shard_map/ppermute | solution.py:33
  20.4 6.3 %collective-permute-done.3.refs_5_.refs_3_ = bf16[5,2,128,128]{3,2,1,0:T(8,128)(2,1)S(1)} collective-permute-done((bf16[5,2,128,128]{3,2,1,0:T(8,128)(2,1)S(1)}, bf16[5,2,128,128]{3,2,1,0:T(8,128)(2,1)S(1)}, u32[]{:S(2)}, u32[]{:S(2)}) %collective-permute-start.3) | collective-permute-done | bytes 327712 | tf_op jit(solution)/shard_map/ppermute | solution.py:33
  26.6 2.4 %collective-permute-done.4.refs_6_.refs_4_ = bf16[5,2,128,128]{3,2,1,0:T(8,128)(2,1)S(1)} collective-permute-done((bf16[5,2,128,128]{3,2,1,0:T(8,128)(2,1)S(1)}, bf16[5,2,128,128]{3,2,1,0:T(8,128)(2,1)S(1)}, u32[]{:S(2)}, u32[]{:S(2)}) %collective-permute-start.4) | collective-permute-done | bytes 327712 | tf_op jit(solution)/shard_map/ppermute | solution.py:33
  29.0 4.4 %collective-permute-done.5.refs_7_.refs_5_ = bf16[5,2,128,128]{3,2,1,0:T(8,128)(2,1)S(1)} collective-permute-done((bf16[5,2,128,128]{3,2,1,0:T(8,128)(2,1)S(1)}, bf16[5,2,128,128]{3,2,1,0:T(8,128)(2,1)S(1)}, u32[]{:S(2)}, u32[]{:S(2)}) %collective-permute-start.5) | collective-permute-done | bytes 327712 | tf_op jit(solution)/shard_map/ppermute | solution.py:33
  33.6 1.6 %collective-permute-start.13 = (bf16[4,3,2,128,128]{4,3,2,1,0:T(8,128)(2,1)S(1)}, bf16[4,3,2,128,128]{4,3,2,1,0:T(8,128)(2,1)S(1)}, u32[]{:S(2)}, u32[]{:S(2)}) collective-permute-start(bf16[4,3,2,128,128]{4,3,2,1,0:T(8,128)(2,1)S(1)} %pad_maximum_fusion.refs_0_), channel_id=1, source_target_pairs={{0,8},{1,9},{2,10},{3,11},{4,12},{5,13},{6,14},{7,15},{8,16},{9,17... | collective-permute-start | bytes 2359304 | tf_op jit(solution)/shard_map/ppermute | solution.py:33
  37.4 1.5 %collective-permute-start.11 = (bf16[3,2,128,128]{3,2,1,0:T(8,128)(2,1)S(1)}, bf16[3,2,128,128]{3,2,1,0:T(8,128)(2,1)S(1)}, u32[]{:S(2)}, u32[]{:S(2)}) collective-permute-start(bf16[3,2,128,128]{3,2,1,0:T(8,128)(2,1)S(1)} %get-tuple-element.84), channel_id=1, source_target_pairs={{0,4},{1,5},{2,6},{3,7},{4,0},{5,1},{6,2},{7,3},{8,12},{9,13},{10,... | collective-permute-start | bytes 589832 | tf_op jit(solution)/shard_map/ppermute | solution.py:33
  40.0 8.0 %shard_map.95 = (bf16[2,2,128,128]{3,2,1,0:T(8,128)(2,1)S(1)}, bf16[2,2,128,128]{3,2,1,0:T(8,128)(2,1)S(1)}, bf16[2,2,128,128]{3,2,1,0:T(8,128)(2,1)S(1)}, bf16[...) custom-call(s32[2]{0:T(128)S(1)} %pad_add_fusion.refs_0_.me, ...), custom_call_target="tpu_custom_call" | custom-call | flops 1 | bytes 1 | tf_op jit(solution)/shard_map/pallas_call | solution.py:235
  48.7 3.7 %collective-permute-done.13.refs_2_ = bf16[4,3,2,128,128]{4,3,2,1,0:T(8,128)(2,1)S(1)} collective-permute-done((bf16[4,3,2,128,128]{4,3,2,1,0:T(8,128)(2,1)S(1)}, bf16[4,3,2,128,128]{4,3,2,1,0:T(8,128)(2,1)S(1)}, u32[]{:S(2)}, u32[]{:S(2)}) %collective-permute-start.13) | collective-permute-done | bytes 786464 | tf_op jit(solution)/shard_map/ppermute | solution.py:33
  52.9 2.1 %collective-permute-done.15 = bf16[8,2,2,128,128]{4,3,2,1,0:T(8,128)(2,1)S(1)} collective-permute-done((bf16[8,2,2,128,128]{4,3,2,1,0:T(8,128)(2,1)S(1)}, bf16[8,2,2,128,128]{4,3,2,1,0:T(8,128)(2,1)S(1)}, u32[]{:S(2)}, u32[]{:S(2)}) %collective-permute-start.15) | collective-permute-done | bytes 1048608 | tf_op jit(solution)/shard_map/ppermute | solution.py:33
  57.8 2.0 %collective-permute-start.19 = (bf16[2,2,128,128]{3,2,1,0:T(8,128)(2,1)S(1)}, bf16[2,2,128,128]{3,2,1,0:T(8,128)(2,1)S(1)}, u32[]{:S(2)}, u32[]{:S(2)}) collective-permute-start(bf16[2,2,128,128]{3,2,1,0:T(8,128)(2,1)S(1)} %get-tuple-element.101), channel_id=1, source_target_pairs={{0,6},{1,7},{2,4},{3,5},{4,2},{5,3},{6,0},{7,1},{8,14},{9,15},{10,... | collective-permute-start | bytes 393224 | tf_op jit(solution)/shard_map/ppermute | solution.py:33
  59.7 8.0 %shard_map.97 = (bf16[2,2,128,128]{3,2,1,0:T(8,128)(2,1)S(1)}, bf16[2,2,128,128]{3,2,1,0:T(8,128)(2,1)S(1)}, bf16[2,2,128,128]{3,2,1,0:T(8,128)(2,1)S(1)}, bf16[...) custom-call(s32[2]{0:T(128)S(1)} %pad_add_fusion.refs_0_.me, ...), custom_call_target="tpu_custom_call" | custom-call | flops 1 | bytes 1 | tf_op jit(solution)/shard_map/pallas_call | solution.py:235
  67.8 1.7 %collective-permute-done.16 = bf16[4,2,2,128,128]{4,3,2,1,0:T(8,128)(2,1)S(1)} collective-permute-done((bf16[4,2,2,128,128]{4,3,2,1,0:T(8,128)(2,1)S(1)}, bf16[4,2,2,128,128]{4,3,2,1,0:T(8,128)(2,1)S(1)}, u32[]{:S(2)}, u32[]{:S(2)}) %collective-permute-start.16) | collective-permute-done | bytes 524320 | tf_op jit(solution)/shard_map/ppermute | solution.py:33
  69.4 4.2 %shard_map.98 = (bf16[1,2,128,128]{3,2,1,0:T(8,128)(2,1)S(1)}, bf16[1,2,128,128]{3,2,1,0:T(8,128)(2,1)S(1)}, bf16[1,2,128,128]{3,2,1,0:T(8,128)(2,1)S(1)}, bf16[...) custom-call(s32[2]{0:T(128)S(1)} %pad_add_fusion.refs_0_.me, ...), custom_call_target="tpu_custom_call" | custom-call | flops 1 | bytes 1 | tf_op jit(solution)/shard_map/pallas_call | solution.py:235
  74.5 2.6 %collective-permute-start.24 = (bf16[4,2,2,128,128]{4,3,2,1,0:T(8,128)(2,1)S(1)}, bf16[4,2,2,128,128]{4,3,2,1,0:T(8,128)(2,1)S(1)}, u32[]{:S(2)}, u32[]{:S(2)}) collective-permute-start(bf16[4,2,2,128,128]{4,3,2,1,0:T(8,128)(2,1)S(1)} %add_convert_fusion), channel_id=1, source_target_pairs={{0,24},{1,25},{2,26},{3,27},{4,28},{5,29},{6,30},{7,31},{8,0},{9,1... | collective-permute-start | bytes 1572872 | tf_op jit(solution)/shard_map/ppermute | solution.py:33
  79.1 2.1 %collective-permute-start.20 = (bf16[5,2,128,128]{3,2,1,0:T(8,128)(2,1)S(1)}, bf16[5,2,128,128]{3,2,1,0:T(8,128)(2,1)S(1)}, u32[]{:S(2)}, u32[]{:S(2)}) collective-permute-start(bf16[5,2,128,128]{3,2,1,0:T(8,128)(2,1)S(1)} %pad_maximum_fusion.3), channel_id=1, source_target_pairs={{0,2},{1,3},{2,0},{3,1},{4,6},{5,7},{6,4},{7,5},{8,10},{9,11},{10,... | collective-permute-start | bytes 983048 | tf_op jit(solution)/shard_map/ppermute | solution.py:33
  81.1 8.3 %collective-permute-done.24 = bf16[4,2,2,128,128]{4,3,2,1,0:T(8,128)(2,1)S(1)} collective-permute-done((bf16[4,2,2,128,128]{4,3,2,1,0:T(8,128)(2,1)S(1)}, bf16[4,2,2,128,128]{4,3,2,1,0:T(8,128)(2,1)S(1)}, u32[]{:S(2)}, u32[]{:S(2)}) %collective-permute-start.24) | collective-permute-done | bytes 524320 | tf_op jit(solution)/shard_map/ppermute | solution.py:33
  91.3 2.9 %collective-permute-done.29 = bf16[4,1,2,128,128]{4,3,2,1,0:T(8,128)(2,1)S(1)} collective-permute-done((bf16[4,1,2,128,128]{4,3,2,1,0:T(8,128)(2,1)S(1)}, bf16[4,1,2,128,128]{4,3,2,1,0:T(8,128)(2,1)S(1)}, u32[]{:S(2)}, u32[]{:S(2)}) %collective-permute-start.29) | collective-permute-done | bytes 262176 | tf_op jit(solution)/shard_map/ppermute | solution.py:33
  95.9 2.0 %collective-permute-start.31 = (bf16[1,2,128,128]{3,2,1,0:T(8,128)(2,1)S(1)}, bf16[1,2,128,128]{3,2,1,0:T(8,128)(2,1)S(1)}, u32[]{:S(2)}, u32[]{:S(2)}) collective-permute-start(bf16[1,2,128,128]{3,2,1,0:T(8,128)(2,1)S(1)} %get-tuple-element.141), channel_id=1, source_target_pairs={{0,4},{1,5},{2,6},{3,7},{4,0},{5,1},{6,2},{7,3},{8,12},{9,13},{10,... | collective-permute-start | bytes 196616 | tf_op jit(solution)/shard_map/ppermute | solution.py:33
  98.7 1.8 %shard_map.99 = (bf16[128,2560]{1,0:T(8,128)(2,1)}, bf16[128,2560]{1,0:T(8,128)(2,1)}) custom-call(s32[2]{0:T(128)S(1)} %pad_add_fusion.refs_0_.me, bf16[2,2,128,128]{3,2,1,0:T(8,128)(2,1)S(1)} %get-tuple-element.102.refs_1_, bf16[2,2,128,128]{3,2,1,0:T(8,128)(2,1)S(1)} %collective-permute-done.17.refs_2_, ...), custom_call_target="tpu_custom_call" | custom-call | tf_op jit(solution)/shard_map/pallas_call | solution.py:104
  103.0 1.8 %shard_map.100 = (bf16[128,2560]{1,0:T(8,128)(2,1)}, bf16[128,2560]{1,0:T(8,128)(2,1)}) custom-call(s32[2]{0:T(128)S(1)} %pad_add_fusion.refs_0_.me, bf16[5,2,128,128]{3,2,1,0:T(8,128)(2,1)S(1)} %pad_maximum_fusion.2.refs_5_.refs_1_, bf16[5,2,128,128]{3,2,1,0:T(8,128)(2,1)S(1)} %collective-permute-done.20.refs_6_.refs_2_, ...), custom_call_target="tpu_custom_call" | custom-call | tf_op jit(solution)/shard_map/pallas_call | solution.py:104
  (77 shorter events, 25.4 us)
Async XLA Ops:
  3.6 6.5 %collective-permute-start = (bf16[2,2,128,128]{3,2,1,0:T(8,128)(2,1)S(1)}, bf16[2,2,128,128]{3,2,1,0:T(8,128)(2,1)S(1)}, u32[]{:S(2)}, u32[]{:S(2)}) collective-permute-start(bf16[2,2,128,128]{3,2,1,0:T(8,128)(2,1)S(1)} %get-tuple-element.68), channel_id=1, source_target_pairs={{0,2},{1,3},{2,0},{3,1},{4,6},{5,7},{6,4},{7,5},{8,10},{9,11},{10,... | collective-permute-start | bytes 393224 | tf_op jit(solution)/shard_map/ppermute | solution.py:33
  14.2 19.2 %collective-permute-start.6 = (bf16[4,2,2,128,128]{4,3,2,1,0:T(8,128)(2,1)S(1)}, bf16[4,2,2,128,128]{4,3,2,1,0:T(8,128)(2,1)S(1)}, u32[]{:S(2)}, u32[]{:S(2)}) collective-permute-start(bf16[4,2,2,128,128]{4,3,2,1,0:T(8,128)(2,1)S(1)} %pad_maximum_fusion.1.refs_0_), channel_id=1, source_target_pairs={{0,8},{1,9},{2,10},{3,11},{4,12},{5,13},{6,14},{7,15},{8,16},{9,17... | collective-permute-start | bytes 1572872 | tf_op jit(solution)/shard_map/ppermute | solution.py:33
  16.8 9.8 %collective-permute-start.3 = (bf16[5,2,128,128]{3,2,1,0:T(8,128)(2,1)S(1)}, bf16[5,2,128,128]{3,2,1,0:T(8,128)(2,1)S(1)}, u32[]{:S(2)}, u32[]{:S(2)}) collective-permute-start(bf16[5,2,128,128]{3,2,1,0:T(8,128)(2,1)S(1)} %get-tuple-element.72), channel_id=1, source_target_pairs={{0,2},{1,3},{2,0},{3,1},{4,6},{5,7},{6,4},{7,5},{8,10},{9,11},{10,... | collective-permute-start | bytes 983048 | tf_op jit(solution)/shard_map/ppermute | solution.py:33
  18.4 10.6 %collective-permute-start.4 = (bf16[5,2,128,128]{3,2,1,0:T(8,128)(2,1)S(1)}, bf16[5,2,128,128]{3,2,1,0:T(8,128)(2,1)S(1)}, u32[]{:S(2)}, u32[]{:S(2)}) collective-permute-start(bf16[5,2,128,128]{3,2,1,0:T(8,128)(2,1)S(1)} %get-tuple-element.73), channel_id=1, source_target_pairs={{0,4},{1,5},{2,6},{3,7},{4,0},{5,1},{6,2},{7,3},{8,12},{9,13},{10,... | collective-permute-start | bytes 983048 | tf_op jit(solution)/shard_map/ppermute | solution.py:33
  19.9 13.5 %collective-permute-start.5 = (bf16[5,2,128,128]{3,2,1,0:T(8,128)(2,1)S(1)}, bf16[5,2,128,128]{3,2,1,0:T(8,128)(2,1)S(1)}, u32[]{:S(2)}, u32[]{:S(2)}) collective-permute-start(bf16[5,2,128,128]{3,2,1,0:T(8,128)(2,1)S(1)} %get-tuple-element.74), channel_id=1, source_target_pairs={{0,6},{1,7},{2,4},{3,5},{4,2},{5,3},{6,0},{7,1},{8,14},{9,15},{10,... | collective-permute-start | bytes 983048 | tf_op jit(solution)/shard_map/ppermute | solution.py:33
  33.6 18.8 %collective-permute-start.13 = (bf16[4,3,2,128,128]{4,3,2,1,0:T(8,128)(2,1)S(1)}, bf16[4,3,2,128,128]{4,3,2,1,0:T(8,128)(2,1)S(1)}, u32[]{:S(2)}, u32[]{:S(2)}) collective-permute-start(bf16[4,3,2,128,128]{4,3,2,1,0:T(8,128)(2,1)S(1)} %pad_maximum_fusion.refs_0_), channel_id=1, source_target_pairs={{0,8},{1,9},{2,10},{3,11},{4,12},{5,13},{6,14},{7,15},{8,16},{9,17... | collective-permute-start | bytes 2359304 | tf_op jit(solution)/shard_map/ppermute | solution.py:33
  36.5 11.6 %collective-permute-start.10 = (bf16[3,2,128,128]{3,2,1,0:T(8,128)(2,1)S(1)}, bf16[3,2,128,128]{3,2,1,0:T(8,128)(2,1)S(1)}, u32[]{:S(2)}, u32[]{:S(2)}) collective-permute-start(bf16[3,2,128,128]{3,2,1,0:T(8,128)(2,1)S(1)} %get-tuple-element.83), channel_id=1, source_target_pairs={{0,2},{1,3},{2,0},{3,1},{4,6},{5,7},{6,4},{7,5},{8,10},{9,11},{10,... | collective-permute-start | bytes 589832 | tf_op jit(solution)/shard_map/ppermute | solution.py:33
  37.4 10.7 %collective-permute-start.11 = (bf16[3,2,128,128]{3,2,1,0:T(8,128)(2,1)S(1)}, bf16[3,2,128,128]{3,2,1,0:T(8,128)(2,1)S(1)}, u32[]{:S(2)}, u32[]{:S(2)}) collective-permute-start(bf16[3,2,128,128]{3,2,1,0:T(8,128)(2,1)S(1)} %get-tuple-element.84), channel_id=1, source_target_pairs={{0,4},{1,5},{2,6},{3,7},{4,0},{5,1},{6,2},{7,3},{8,12},{9,13},{10,... | collective-permute-start | bytes 589832 | tf_op jit(solution)/shard_map/ppermute | solution.py:33
  38.9 9.9 %collective-permute-start.12 = (bf16[3,2,128,128]{3,2,1,0:T(8,128)(2,1)S(1)}, bf16[3,2,128,128]{3,2,1,0:T(8,128)(2,1)S(1)}, u32[]{:S(2)}, u32[]{:S(2)}) collective-permute-start(bf16[3,2,128,128]{3,2,1,0:T(8,128)(2,1)S(1)} %get-tuple-element.85), channel_id=1, source_target_pairs={{0,6},{1,7},{2,4},{3,5},{4,2},{5,3},{6,0},{7,1},{8,14},{9,15},{10,... | collective-permute-start | bytes 589832 | tf_op jit(solution)/shard_map/ppermute | solution.py:33
  52.9 6.8 %collective-permute-start.14 = (bf16[4,3,2,128,128]{4,3,2,1,0:T(8,128)(2,1)S(1)}, bf16[4,3,2,128,128]{4,3,2,1,0:T(8,128)(2,1)S(1)}, u32[]{:S(2)}, u32[]{:S(2)}) collective-permute-start(bf16[4,3,2,128,128]{4,3,2,1,0:T(8,128)(2,1)S(1)} %collective-permute-done.13.refs_2_), channel_id=1, source_target_pairs={{0,1},{1,0},{2,3},{3,2},{4,5},{5,4},{6,7},{7,6},{8,9},{9,8},{10,11... | collective-permute-start | bytes 2359304 | tf_op jit(solution)/shard_map/ppermute | solution.py:33
  55.2 14.2 %collective-permute-start.16 = (bf16[4,2,2,128,128]{4,3,2,1,0:T(8,128)(2,1)S(1)}, bf16[4,2,2,128,128]{4,3,2,1,0:T(8,128)(2,1)S(1)}, u32[]{:S(2)}, u32[]{:S(2)}) collective-permute-start(bf16[4,2,2,128,128]{4,3,2,1,0:T(8,128)(2,1)S(1)} %add_convert_fusion.1), channel_id=1, source_target_pairs={{0,24},{1,25},{2,26},{3,27},{4,28},{5,29},{6,30},{7,31},{8,0},{9,1... | collective-permute-start | bytes 1572872 | tf_op jit(solution)/shard_map/ppermute | solution.py:33
  56.2 11.5 %collective-permute-start.17 = (bf16[2,2,128,128]{3,2,1,0:T(8,128)(2,1)S(1)}, bf16[2,2,128,128]{3,2,1,0:T(8,128)(2,1)S(1)}, u32[]{:S(2)}, u32[]{:S(2)}) collective-permute-start(bf16[2,2,128,128]{3,2,1,0:T(8,128)(2,1)S(1)} %get-tuple-element.99), channel_id=1, source_target_pairs={{0,2},{1,3},{2,0},{3,1},{4,6},{5,7},{6,4},{7,5},{8,10},{9,11},{10,... | collective-permute-start | bytes 393224 | tf_op jit(solution)/shard_map/ppermute | solution.py:33
  56.3 11.4 %collective-permute-start.18 = (bf16[2,2,128,128]{3,2,1,0:T(8,128)(2,1)S(1)}, bf16[2,2,128,128]{3,2,1,0:T(8,128)(2,1)S(1)}, u32[]{:S(2)}, u32[]{:S(2)}) collective-permute-start(bf16[2,2,128,128]{3,2,1,0:T(8,128)(2,1)S(1)} %get-tuple-element.100), channel_id=1, source_target_pairs={{0,4},{1,5},{2,6},{3,7},{4,0},{5,1},{6,2},{7,3},{8,12},{9,13},{10,... | collective-permute-start | bytes 393224 | tf_op jit(solution)/shard_map/ppermute | solution.py:33
  57.8 10.0 %collective-permute-start.19 = (bf16[2,2,128,128]{3,2,1,0:T(8,128)(2,1)S(1)}, bf16[2,2,128,128]{3,2,1,0:T(8,128)(2,1)S(1)}, u32[]{:S(2)}, u32[]{:S(2)}) collective-permute-start(bf16[2,2,128,128]{3,2,1,0:T(8,128)(2,1)S(1)} %get-tuple-element.101), channel_id=1, source_target_pairs={{0,6},{1,7},{2,4},{3,5},{4,2},{5,3},{6,0},{7,1},{8,14},{9,15},{10,... | collective-permute-start | bytes 393224 | tf_op jit(solution)/shard_map/ppermute | solution.py:33
  74.5 14.9 %collective-permute-start.24 = (bf16[4,2,2,128,128]{4,3,2,1,0:T(8,128)(2,1)S(1)}, bf16[4,2,2,128,128]{4,3,2,1,0:T(8,128)(2,1)S(1)}, u32[]{:S(2)}, u32[]{:S(2)}) collective-permute-start(bf16[4,2,2,128,128]{4,3,2,1,0:T(8,128)(2,1)S(1)} %add_convert_fusion), channel_id=1, source_target_pairs={{0,24},{1,25},{2,26},{3,27},{4,28},{5,29},{6,30},{7,31},{8,0},{9,1... | collective-permute-start | bytes 1572872 | tf_op jit(solution)/shard_map/ppermute | solution.py:33
  77.2 13.6 %collective-permute-start.22 = (bf16[5,2,128,128]{3,2,1,0:T(8,128)(2,1)S(1)}, bf16[5,2,128,128]{3,2,1,0:T(8,128)(2,1)S(1)}, u32[]{:S(2)}, u32[]{:S(2)}) collective-permute-start(bf16[5,2,128,128]{3,2,1,0:T(8,128)(2,1)S(1)} %pad_maximum_fusion.5), channel_id=1, source_target_pairs={{0,6},{1,7},{2,4},{3,5},{4,2},{5,3},{6,0},{7,1},{8,14},{9,15},{10,... | collective-permute-start | bytes 983048 | tf_op jit(solution)/shard_map/ppermute | solution.py:33
  78.3 16.1 %collective-permute-start.21 = (bf16[5,2,128,128]{3,2,1,0:T(8,128)(2,1)S(1)}, bf16[5,2,128,128]{3,2,1,0:T(8,128)(2,1)S(1)}, u32[]{:S(2)}, u32[]{:S(2)}) collective-permute-start(bf16[5,2,128,128]{3,2,1,0:T(8,128)(2,1)S(1)} %pad_maximum_fusion.4), channel_id=1, source_target_pairs={{0,4},{1,5},{2,6},{3,7},{4,0},{5,1},{6,2},{7,3},{8,12},{9,13},{10,... | collective-permute-start | bytes 983048 | tf_op jit(solution)/shard_map/ppermute | solution.py:33
  78.9 15.2 %collective-permute-start.29 = (bf16[4,1,2,128,128]{4,3,2,1,0:T(8,128)(2,1)S(1)}, bf16[4,1,2,128,128]{4,3,2,1,0:T(8,128)(2,1)S(1)}, u32[]{:S(2)}, u32[]{:S(2)}) collective-permute-start(bf16[4,1,2,128,128]{4,3,2,1,0:T(8,128)(2,1)S(1)} %add_convert_fusion.2), channel_id=1, source_target_pairs={{0,24},{1,25},{2,26},{3,27},{4,28},{5,29},{6,30},{7,31},{8,0},{9,1... | collective-permute-start | bytes 786440 | tf_op jit(solution)/shard_map/ppermute | solution.py:33
  79.1 16.8 %collective-permute-start.20 = (bf16[5,2,128,128]{3,2,1,0:T(8,128)(2,1)S(1)}, bf16[5,2,128,128]{3,2,1,0:T(8,128)(2,1)S(1)}, u32[]{:S(2)}, u32[]{:S(2)}) collective-permute-start(bf16[5,2,128,128]{3,2,1,0:T(8,128)(2,1)S(1)} %pad_maximum_fusion.3), channel_id=1, source_target_pairs={{0,2},{1,3},{2,0},{3,1},{4,6},{5,7},{6,4},{7,5},{8,10},{9,11},{10,... | collective-permute-start | bytes 983048 | tf_op jit(solution)/shard_map/ppermute | solution.py:33
  89.6 9.0 %collective-permute-start.27 = (bf16[2,2,128,128]{3,2,1,0:T(8,128)(2,1)S(1)}, bf16[2,2,128,128]{3,2,1,0:T(8,128)(2,1)S(1)}, u32[]{:S(2)}, u32[]{:S(2)}) collective-permute-start(bf16[2,2,128,128]{3,2,1,0:T(8,128)(2,1)S(1)} %get-tuple-element.132), channel_id=1, source_target_pairs={{0,6},{1,7},{2,4},{3,5},{4,2},{5,3},{6,0},{7,1},{8,14},{9,15},{10,... | collective-permute-start | bytes 393224 | tf_op jit(solution)/shard_map/ppermute | solution.py:33
  90.8 9.8 %collective-permute-start.26 = (bf16[2,2,128,128]{3,2,1,0:T(8,128)(2,1)S(1)}, bf16[2,2,128,128]{3,2,1,0:T(8,128)(2,1)S(1)}, u32[]{:S(2)}, u32[]{:S(2)}) collective-permute-start(bf16[2,2,128,128]{3,2,1,0:T(8,128)(2,1)S(1)} %get-tuple-element.133), channel_id=1, source_target_pairs={{0,4},{1,5},{2,6},{3,7},{4,0},{5,1},{6,2},{7,3},{8,12},{9,13},{10,... | collective-permute-start | bytes 393224 | tf_op jit(solution)/shard_map/ppermute | solution.py:33
  94.1 7.6 %collective-permute-start.25 = (bf16[2,2,128,128]{3,2,1,0:T(8,128)(2,1)S(1)}, bf16[2,2,128,128]{3,2,1,0:T(8,128)(2,1)S(1)}, u32[]{:S(2)}, u32[]{:S(2)}) collective-permute-start(bf16[2,2,128,128]{3,2,1,0:T(8,128)(2,1)S(1)} %get-tuple-element.134), channel_id=1, source_target_pairs={{0,2},{1,3},{2,0},{3,1},{4,6},{5,7},{6,4},{7,5},{8,10},{9,11},{10,... | collective-permute-start | bytes 393224 | tf_op jit(solution)/shard_map/ppermute | solution.py:33
  94.4 7.9 %collective-permute-start.32 = (bf16[1,2,128,128]{3,2,1,0:T(8,128)(2,1)S(1)}, bf16[1,2,128,128]{3,2,1,0:T(8,128)(2,1)S(1)}, u32[]{:S(2)}, u32[]{:S(2)}) collective-permute-start(bf16[1,2,128,128]{3,2,1,0:T(8,128)(2,1)S(1)} %get-tuple-element.140), channel_id=1, source_target_pairs={{0,6},{1,7},{2,4},{3,5},{4,2},{5,3},{6,0},{7,1},{8,14},{9,15},{10,... | collective-permute-start | bytes 196616 | tf_op jit(solution)/shard_map/ppermute | solution.py:33
  95.9 6.4 %collective-permute-start.31 = (bf16[1,2,128,128]{3,2,1,0:T(8,128)(2,1)S(1)}, bf16[1,2,128,128]{3,2,1,0:T(8,128)(2,1)S(1)}, u32[]{:S(2)}, u32[]{:S(2)}) collective-permute-start(bf16[1,2,128,128]{3,2,1,0:T(8,128)(2,1)S(1)} %get-tuple-element.141), channel_id=1, source_target_pairs={{0,4},{1,5},{2,6},{3,7},{4,0},{5,1},{6,2},{7,3},{8,12},{9,13},{10,... | collective-permute-start | bytes 196616 | tf_op jit(solution)/shard_map/ppermute | solution.py:33
  (15 other events, 77.4 us)
